TPU v7x, 128 devices: a whole 4x4x4 slice. The times are simulated.
128 devices in a mesh: outer: 2 (over z_hi), inner: 8 (over z_lo, x), tensor: 8 (over y, core).
Axes of the slice: x: 4, y: 4, z: 4 (z_hi: 2, z_lo: 2; z = z_hi * 2 + z_lo), core: 2. Of those that a mesh axis runs over, the one named last changes fastest.
Arguments:
- queries: bfloat16 [4096, 8192], P(('outer', 'inner'), 'tensor'), may hold values from -64 to 64
- keys: bfloat16 [4096, 1024], P(('outer', 'inner'), 'tensor'), may hold values from -5 to 5
- values: bfloat16 [4096, 1024], P(('outer', 'inner'), 'tensor'), may hold values from -8 to 8
- positions: int32 [4096], replicated, may hold values from 0 to 4095, as said below
- doc_lengths: int32 [8], replicated, may hold values from 1 to 1024, 4096 in all
- image_spans: int32 [2, 4], replicated, may hold values from 0 to 4096, as said below
- out_weight: bfloat16 [8192, 8192], P('tensor', ('outer', 'inner')), may hold values from -0.0625 to 0.0625
Outputs:
- layer_output: bfloat16 [4096, 8192], P(('outer', 'inner'), 'tensor')
Inputs may be any that keep to these rules, and one draw needn't show every extreme that they name: A permutation of the slots' positions that keeps each aligned run of 64 slots on 64 consecutive positions, in order. `image_spans`: spans are disjoint and ascending; each holds 1 to 3 whole image tiles of 256 tokens; the first span starts at 0 and the last ends at 4096.
All inputs are finite; a program needn't handle non-finite values.
Results may differ from a plain program's by a relative error of at most 0.019.
Values may be sent and summed in bfloat16 or wider, within the bound.
No kernel may reach another device: no remote copies, remote signals or barrier semaphores. Data moves between devices by JAX's collectives and lax.ppermute only.
A program may use at most 128 MiB of HBM per device.

v0:
```python
import math

import jax
import jax.numpy as jnp
from jax import lax
from jax.sharding import PartitionSpec as P

DH = 128


NEGATIVE = -1e30


def token_labels(places, doc_lengths, image_spans):
    doc_ends = jnp.cumsum(doc_lengths)
    document = jnp.sum((places[:, None] >= doc_ends[None, :]).astype(jnp.int32), axis=1)
    inside = (places[:, None] >= image_spans[0][None, :]) & (
        places[:, None] < image_spans[1][None, :]
    )
    numbers = jnp.arange(1, image_spans.shape[1] + 1, dtype=jnp.int32)
    image = jnp.sum(jnp.where(inside, numbers[None, :], 0), axis=1)
    return (document, image)


def visible(query_place, query_doc, query_img, key_place, key_doc, key_img):
    same_doc = query_doc[:, None] == key_doc[None, :]
    earlier = key_place[None, :] <= query_place[:, None]
    same_img = (query_img[:, None] == key_img[None, :]) & (query_img[:, None] > 0)
    return same_doc & (earlier | same_img)


def shards(queries, keys, values, positions, doc_lengths, image_spans, out_weight):
    row_count = queries.shape[0]
    kv_local = keys.shape[1] // DH
    q_local = queries.shape[1] // DH
    group = q_local // kv_local
    scale = 1.0 / math.sqrt(DH)
    first_slot = lax.axis_index(("outer", "inner")) * row_count
    own_places = lax.dynamic_slice_in_dim(positions, first_slot, row_count)
    own_doc, own_img = token_labels(own_places, doc_lengths, image_spans)
    query_grid = queries.reshape(row_count, kv_local, group, DH)

    def update(carry, key_slice, value_slice, allowed):
        running_top, running_total, accum = carry
        size = key_slice.shape[0]
        key_grid = key_slice.reshape(size, kv_local, DH)
        value_grid = value_slice.reshape(size, kv_local, DH)
        scores = (
            jnp.einsum("qgjd,kgd->gjqk", query_grid, key_grid, preferred_element_type=jnp.float32)
            * scale
        )
        masked = jnp.where(allowed[None, None], scores, NEGATIVE)
        new_top = jnp.maximum(running_top, jnp.max(masked, axis=-1))
        expo = jnp.where(allowed[None, None], jnp.exp(scores - new_top[..., None]), 0.0)
        shrink = jnp.exp(running_top - new_top)
        new_total = running_total * shrink + jnp.sum(expo, axis=-1)
        mixed = jnp.einsum(
            "gjqk,kgd->gjqd",
            expo.astype(jnp.bfloat16),
            value_grid,
            preferred_element_type=jnp.float32,
        )
        return (new_top, new_total, accum * shrink[..., None] + mixed)

    def attend(carry, key_slice, value_slice, block_start):
        size = key_slice.shape[0]
        places = lax.dynamic_slice_in_dim(positions, block_start, size)
        key_doc, key_img = token_labels(places, doc_lengths, image_spans)
        allowed = visible(own_places, own_doc, own_img, places, key_doc, key_img)
        return update(carry, key_slice, value_slice, allowed)

    start_state = (
        jnp.full((kv_local, group, row_count), NEGATIVE, jnp.float32),
        jnp.zeros((kv_local, group, row_count), jnp.float32),
        jnp.zeros((kv_local, group, row_count, DH), jnp.float32),
    )
    key_part = lax.all_gather(keys, ("outer", "inner"), axis=0, tiled=True)
    value_part = lax.all_gather(values, ("outer", "inner"), axis=0, tiled=True)
    count = key_part.shape[0]
    size = math.gcd(count, 512)

    def advance(index, state):
        offset = index * size
        key_slice = lax.dynamic_slice_in_dim(key_part, offset, size, 0)
        value_slice = lax.dynamic_slice_in_dim(value_part, offset, size, 0)
        return attend(state, key_slice, value_slice, offset)

    final = lax.fori_loop(0, count // size, advance, start_state)
    final_top, final_total, final_accum = final
    attended = (final_accum / final_total[..., None]).astype(jnp.bfloat16)
    flat = attended.transpose(2, 0, 1, 3).reshape(row_count, q_local * DH)
    partial_out = jnp.dot(
        flat,
        lax.all_gather(out_weight, ("outer", "inner"), axis=1, tiled=True),
        preferred_element_type=jnp.float32,
    )
    summed = lax.psum_scatter(
        partial_out.astype(jnp.bfloat16), "tensor", scatter_dimension=1, tiled=True
    )
    return summed


def solution(mesh):
    placed = (
        P(("outer", "inner"), "tensor"),
        P(("outer", "inner"), "tensor"),
        P(("outer", "inner"), "tensor"),
        P(),
        P(),
        P(),
        P("tensor", ("outer", "inner")),
    )
    return jax.shard_map(
        shards,
        mesh=mesh,
        in_specs=placed,
        out_specs=P(("outer", "inner"), "tensor"),
        check_vma=False,
    )
```

profile of v0, /device:TPU:6, one launch (start us, length us, event | category | flops | bytes accessed | tf_op | source)
XLA Modules:
  0.0 277.4 jit_solution(2548079180962271709)
XLA Ops:
  8.8 0.8 broadcast_in_dim.145
  9.7 1.2 copy.14
  11.2 0.8 dynamic_slice.30
  12.1 0.8 slice_bitcast_fusion.3
  12.9 41.5 %all-gather.4.cloned.1.call-done = bf16[4096,128]{1,0:T(8,128)(2,1)} async-done(((bf16[256,128]{1,0:T(8,128)(2,1)}), bf16[4096,128]{1,0:T(8,128)(2,1)}) %all-gather.4.cloned.1.call-update) | async-done | bytes 1048592 | tf_op jit(solution)/shard_map/all_gather | solution.py:77
  54.4 44.3 %all-gather.6.cloned.1.call-done = bf16[4096,128]{1,0:T(8,128)(2,1)} async-done(((bf16[256,128]{1,0:T(8,128)(2,1)}), bf16[4096,128]{1,0:T(8,128)(2,1)}) %all-gather.6.cloned.1.call-update) | async-done | bytes 1048592 | tf_op jit(solution)/shard_map/all_gather | solution.py:78
  98.7 83.3 %while.20 = (s32[]{:T(128)}, f32[1,8,256]{2,1,0:T(8,128)S(1)}, f32[1,8,256]{2,1,0:T(8,128)S(1)}, f32[1,8,256,128]{3,2,1,0:T(8,128)S(1)}, s32[256]{0:T(256)S(1)},...) while((s32[]{:T(128)}, f32[1,8,256]{2,1,0:T(8,128)S(1)}, ...), condition=%wide.region_8.9_spmd.clone, body=%wide.region_3.8_spmd.clone.sunk | while | flops 550012160 | bytes 32922524 | solution.py:88
  98.7 0.8 dynamic_slice.49
  99.4 0.8 slice_bitcast_fusion.5
  100.6 3.6 %fusion.36 = (f32[8,256]{1,0:T(8,128)S(1)}, f32[512,256,8]{1,0,2:T(8,128)}) fusion(pred[256,512]{0,1:T(8,128)(4,1)S(1)} %or_and_fusion.2, bf16[256,1,8,128]{3,0,2,1:T(8,128)(2,1)S(1)} %get-tuple-element.542, bf16[4096,128]{1,0:T(8,128)(2,1)} %get-tuple-element.541, s32[]{:T(128)S(6)} %select_n.79), kind=kOutput, calls=%fused_computation.2.clone.1 | convolution fusion | flops 271579136 | bytes 4988932 | tf_op jit(solution)/shard_map/while/body/eval_jaxpr/qgjd,kgd->gjqk/dot_general | solution.py:49
  104.3 3.8 %fusion.39 = f32[1,8,256,128]{3,2,1,0:T(8,128)S(1)} fusion(f32[512,256,8]{1,0,2:T(8,128)} %get-tuple-element.495, f32[8,256]{1,0:T(8,128)S(1)} %bitcast.98, pred[256,512]{0,1:T(8,128)(4,1)S(1)} %or_and_fusion.2, f32[1,8,256,128]{3,2,1,0:T(8,128)S(1)} %get-tuple-element.517, f32[8,256]{1,0:T(8,128)S(1)} %get-tuple-element.496, pred[]{:T(512)S(6)} %compare.3, ...), kind=kOutput, calls=%fused_computation.11.clone.1 | convolution fusion | flops 273416192 | bytes 6569989 | tf_op jit(solution)/shard_map/while/body/eval_jaxpr/gjqk,kgd->gjqd/dot_general | solution.py:57
  108.1 0.9 fusion.38
  109.0 0.8 dynamic_slice.49
  109.8 0.8 slice_bitcast_fusion.5
  111.0 3.6 %fusion.36 = (f32[8,256]{1,0:T(8,128)S(1)}, f32[512,256,8]{1,0,2:T(8,128)}) fusion(pred[256,512]{0,1:T(8,128)(4,1)S(1)} %or_and_fusion.2, bf16[256,1,8,128]{3,0,2,1:T(8,128)(2,1)S(1)} %get-tuple-element.542, bf16[4096,128]{1,0:T(8,128)(2,1)} %get-tuple-element.541, s32[]{:T(128)S(6)} %select_n.79), kind=kOutput, calls=%fused_computation.2.clone.1 | convolution fusion | flops 271579136 | bytes 4988932 | tf_op jit(solution)/shard_map/while/body/eval_jaxpr/qgjd,kgd->gjqk/dot_general | solution.py:49
  114.7 3.8 %fusion.39 = f32[1,8,256,128]{3,2,1,0:T(8,128)S(1)} fusion(f32[512,256,8]{1,0,2:T(8,128)} %get-tuple-element.495, f32[8,256]{1,0:T(8,128)S(1)} %bitcast.98, pred[256,512]{0,1:T(8,128)(4,1)S(1)} %or_and_fusion.2, f32[1,8,256,128]{3,2,1,0:T(8,128)S(1)} %get-tuple-element.517, f32[8,256]{1,0:T(8,128)S(1)} %get-tuple-element.496, pred[]{:T(512)S(6)} %compare.3, ...), kind=kOutput, calls=%fused_computation.11.clone.1 | convolution fusion | flops 273416192 | bytes 6569989 | tf_op jit(solution)/shard_map/while/body/eval_jaxpr/gjqk,kgd->gjqd/dot_general | solution.py:57
  118.5 0.9 fusion.38
  119.4 0.8 dynamic_slice.49
  120.2 0.8 slice_bitcast_fusion.5
  121.4 3.6 %fusion.36 = (f32[8,256]{1,0:T(8,128)S(1)}, f32[512,256,8]{1,0,2:T(8,128)}) fusion(pred[256,512]{0,1:T(8,128)(4,1)S(1)} %or_and_fusion.2, bf16[256,1,8,128]{3,0,2,1:T(8,128)(2,1)S(1)} %get-tuple-element.542, bf16[4096,128]{1,0:T(8,128)(2,1)} %get-tuple-element.541, s32[]{:T(128)S(6)} %select_n.79), kind=kOutput, calls=%fused_computation.2.clone.1 | convolution fusion | flops 271579136 | bytes 4988932 | tf_op jit(solution)/shard_map/while/body/eval_jaxpr/qgjd,kgd->gjqk/dot_general | solution.py:49
  125.0 3.8 %fusion.39 = f32[1,8,256,128]{3,2,1,0:T(8,128)S(1)} fusion(f32[512,256,8]{1,0,2:T(8,128)} %get-tuple-element.495, f32[8,256]{1,0:T(8,128)S(1)} %bitcast.98, pred[256,512]{0,1:T(8,128)(4,1)S(1)} %or_and_fusion.2, f32[1,8,256,128]{3,2,1,0:T(8,128)S(1)} %get-tuple-element.517, f32[8,256]{1,0:T(8,128)S(1)} %get-tuple-element.496, pred[]{:T(512)S(6)} %compare.3, ...), kind=kOutput, calls=%fused_computation.11.clone.1 | convolution fusion | flops 273416192 | bytes 6569989 | tf_op jit(solution)/shard_map/while/body/eval_jaxpr/gjqk,kgd->gjqd/dot_general | solution.py:57
  128.8 0.9 fusion.38
  129.8 0.8 dynamic_slice.49
  131.8 3.6 %fusion.36 = (f32[8,256]{1,0:T(8,128)S(1)}, f32[512,256,8]{1,0,2:T(8,128)}) fusion(pred[256,512]{0,1:T(8,128)(4,1)S(1)} %or_and_fusion.2, bf16[256,1,8,128]{3,0,2,1:T(8,128)(2,1)S(1)} %get-tuple-element.542, bf16[4096,128]{1,0:T(8,128)(2,1)} %get-tuple-element.541, s32[]{:T(128)S(6)} %select_n.79), kind=kOutput, calls=%fused_computation.2.clone.1 | convolution fusion | flops 271579136 | bytes 4988932 | tf_op jit(solution)/shard_map/while/body/eval_jaxpr/qgjd,kgd->gjqk/dot_general | solution.py:49
  135.4 3.8 %fusion.39 = f32[1,8,256,128]{3,2,1,0:T(8,128)S(1)} fusion(f32[512,256,8]{1,0,2:T(8,128)} %get-tuple-element.495, f32[8,256]{1,0:T(8,128)S(1)} %bitcast.98, pred[256,512]{0,1:T(8,128)(4,1)S(1)} %or_and_fusion.2, f32[1,8,256,128]{3,2,1,0:T(8,128)S(1)} %get-tuple-element.517, f32[8,256]{1,0:T(8,128)S(1)} %get-tuple-element.496, pred[]{:T(512)S(6)} %compare.3, ...), kind=kOutput, calls=%fused_computation.11.clone.1 | convolution fusion | flops 273416192 | bytes 6569989 | tf_op jit(solution)/shard_map/while/body/eval_jaxpr/gjqk,kgd->gjqd/dot_general | solution.py:57
  139.2 0.9 fusion.38
  140.1 0.8 dynamic_slice.49
  142.1 3.6 %fusion.36 = (f32[8,256]{1,0:T(8,128)S(1)}, f32[512,256,8]{1,0,2:T(8,128)}) fusion(pred[256,512]{0,1:T(8,128)(4,1)S(1)} %or_and_fusion.2, bf16[256,1,8,128]{3,0,2,1:T(8,128)(2,1)S(1)} %get-tuple-element.542, bf16[4096,128]{1,0:T(8,128)(2,1)} %get-tuple-element.541, s32[]{:T(128)S(6)} %select_n.79), kind=kOutput, calls=%fused_computation.2.clone.1 | convolution fusion | flops 271579136 | bytes 4988932 | tf_op jit(solution)/shard_map/while/body/eval_jaxpr/qgjd,kgd->gjqk/dot_general | solution.py:49
  145.8 4.0 %fusion.39 = f32[1,8,256,128]{3,2,1,0:T(8,128)S(1)} fusion(f32[512,256,8]{1,0,2:T(8,128)} %get-tuple-element.495, f32[8,256]{1,0:T(8,128)S(1)} %bitcast.98, pred[256,512]{0,1:T(8,128)(4,1)S(1)} %or_and_fusion.2, f32[1,8,256,128]{3,2,1,0:T(8,128)S(1)} %get-tuple-element.517, f32[8,256]{1,0:T(8,128)S(1)} %get-tuple-element.496, pred[]{:T(512)S(6)} %compare.3, ...), kind=kOutput, calls=%fused_computation.11.clone.1 | convolution fusion | flops 273416192 | bytes 6569989 | tf_op jit(solution)/shard_map/while/body/eval_jaxpr/gjqk,kgd->gjqd/dot_general | solution.py:57
  149.7 0.9 fusion.38
  150.7 0.8 dynamic_slice.49
  151.4 0.8 slice_bitcast_fusion.5
  152.7 3.6 %fusion.36 = (f32[8,256]{1,0:T(8,128)S(1)}, f32[512,256,8]{1,0,2:T(8,128)}) fusion(pred[256,512]{0,1:T(8,128)(4,1)S(1)} %or_and_fusion.2, bf16[256,1,8,128]{3,0,2,1:T(8,128)(2,1)S(1)} %get-tuple-element.542, bf16[4096,128]{1,0:T(8,128)(2,1)} %get-tuple-element.541, s32[]{:T(128)S(6)} %select_n.79), kind=kOutput, calls=%fused_computation.2.clone.1 | convolution fusion | flops 271579136 | bytes 4988932 | tf_op jit(solution)/shard_map/while/body/eval_jaxpr/qgjd,kgd->gjqk/dot_general | solution.py:49
  156.3 3.8 %fusion.39 = f32[1,8,256,128]{3,2,1,0:T(8,128)S(1)} fusion(f32[512,256,8]{1,0,2:T(8,128)} %get-tuple-element.495, f32[8,256]{1,0:T(8,128)S(1)} %bitcast.98, pred[256,512]{0,1:T(8,128)(4,1)S(1)} %or_and_fusion.2, f32[1,8,256,128]{3,2,1,0:T(8,128)S(1)} %get-tuple-element.517, f32[8,256]{1,0:T(8,128)S(1)} %get-tuple-element.496, pred[]{:T(512)S(6)} %compare.3, ...), kind=kOutput, calls=%fused_computation.11.clone.1 | convolution fusion | flops 273416192 | bytes 6569989 | tf_op jit(solution)/shard_map/while/body/eval_jaxpr/gjqk,kgd->gjqd/dot_general | solution.py:57
  160.1 0.9 fusion.38
  161.1 0.8 dynamic_slice.49
  161.8 0.8 slice_bitcast_fusion.5
  163.0 3.6 %fusion.36 = (f32[8,256]{1,0:T(8,128)S(1)}, f32[512,256,8]{1,0,2:T(8,128)}) fusion(pred[256,512]{0,1:T(8,128)(4,1)S(1)} %or_and_fusion.2, bf16[256,1,8,128]{3,0,2,1:T(8,128)(2,1)S(1)} %get-tuple-element.542, bf16[4096,128]{1,0:T(8,128)(2,1)} %get-tuple-element.541, s32[]{:T(128)S(6)} %select_n.79), kind=kOutput, calls=%fused_computation.2.clone.1 | convolution fusion | flops 271579136 | bytes 4988932 | tf_op jit(solution)/shard_map/while/body/eval_jaxpr/qgjd,kgd->gjqk/dot_general | solution.py:49
  166.7 3.8 %fusion.39 = f32[1,8,256,128]{3,2,1,0:T(8,128)S(1)} fusion(f32[512,256,8]{1,0,2:T(8,128)} %get-tuple-element.495, f32[8,256]{1,0:T(8,128)S(1)} %bitcast.98, pred[256,512]{0,1:T(8,128)(4,1)S(1)} %or_and_fusion.2, f32[1,8,256,128]{3,2,1,0:T(8,128)S(1)} %get-tuple-element.517, f32[8,256]{1,0:T(8,128)S(1)} %get-tuple-element.496, pred[]{:T(512)S(6)} %compare.3, ...), kind=kOutput, calls=%fused_computation.11.clone.1 | convolution fusion | flops 273416192 | bytes 6569989 | tf_op jit(solution)/shard_map/while/body/eval_jaxpr/gjqk,kgd->gjqd/dot_general | solution.py:57
  170.5 0.9 fusion.38
  171.4 0.8 dynamic_slice.49
  172.2 0.8 slice_bitcast_fusion.5
  173.4 3.6 %fusion.36 = (f32[8,256]{1,0:T(8,128)S(1)}, f32[512,256,8]{1,0,2:T(8,128)}) fusion(pred[256,512]{0,1:T(8,128)(4,1)S(1)} %or_and_fusion.2, bf16[256,1,8,128]{3,0,2,1:T(8,128)(2,1)S(1)} %get-tuple-element.542, bf16[4096,128]{1,0:T(8,128)(2,1)} %get-tuple-element.541, s32[]{:T(128)S(6)} %select_n.79), kind=kOutput, calls=%fused_computation.2.clone.1 | convolution fusion | flops 271579136 | bytes 4988932 | tf_op jit(solution)/shard_map/while/body/eval_jaxpr/qgjd,kgd->gjqk/dot_general | solution.py:49
  177.0 4.0 %fusion.39 = f32[1,8,256,128]{3,2,1,0:T(8,128)S(1)} fusion(f32[512,256,8]{1,0,2:T(8,128)} %get-tuple-element.495, f32[8,256]{1,0:T(8,128)S(1)} %bitcast.98, pred[256,512]{0,1:T(8,128)(4,1)S(1)} %or_and_fusion.2, f32[1,8,256,128]{3,2,1,0:T(8,128)S(1)} %get-tuple-element.517, f32[8,256]{1,0:T(8,128)S(1)} %get-tuple-element.496, pred[]{:T(512)S(6)} %compare.3, ...), kind=kOutput, calls=%fused_computation.11.clone.1 | convolution fusion | flops 273416192 | bytes 6569989 | tf_op jit(solution)/shard_map/while/body/eval_jaxpr/gjqk,kgd->gjqd/dot_general | solution.py:57
  181.0 0.9 fusion.38
  182.4 38.9 %all-gather.8.cloned.1.call-done = bf16[1024,8192]{1,0:T(8,128)(2,1)} async-done(((bf16[1024,512]{1,0:T(8,128)(2,1)}), bf16[1024,8192]{1,0:T(8,128)(2,1)}) %all-gather.8.cloned.1.call-update) | async-done | bytes 16777232 | tf_op jit(solution)/shard_map/all_gather | solution.py:94
  221.3 12.0 %convolution_convert_fusion = bf16[256,8192]{1,0:T(8,128)(2,1)} fusion(bf16[256,1024]{0,1:T(8,128)(2,1)S(1)} %bitcast.101, bf16[1024,8192]{1,0:T(8,128)(2,1)} %all-gather.8.cloned.1.call-done), kind=kOutput, calls=%fused_computation.35 | convolution fusion | flops 4297064448 | bytes 21495808 | tf_op jit(solution)/shard_map/dot_general | solution.py:92
  233.3 37.5 %reduce-scatter.2.cloned.1.call-done = bf16[256,1024]{1,0:T(8,128)(2,1)} async-done(((bf16[256,8192]{1,0:T(8,128)(2,1)}), bf16[256,1024]{1,0:T(8,128)(2,1)}) %reduce-scatter.2.cloned.1.call-update) | async-done | bytes 524304 | tf_op jit(solution)/shard_map/reduce_scatter | solution.py:97
  (99 shorter events, 8.5 us)
Async XLA Ops:
  6.5 47.9 %all-gather.4.cloned.1.call-start = ((), (), s32[]{:S(2)}) async-start(), calls=%async_computation.1 | async-start | bytes 1114112 | tf_op jit(solution)/shard_map/all_gather | solution.py:77
  7.3 91.4 %all-gather.6.cloned.1.call-start = ((), (), s32[]{:S(2)}) async-start(), calls=%async_computation.2 | async-start | bytes 1114112 | tf_op jit(solution)/shard_map/all_gather | solution.py:78
  8.0 213.3 %all-gather.8.cloned.1.call-start = ((), (), s32[]{:S(2)}) async-start(), calls=%async_computation.3 | async-start | bytes 17825792 | tf_op jit(solution)/shard_map/all_gather | solution.py:94
  8.7 262.1 %reduce-scatter.2.cloned.1.call-start = ((), (), s32[]{:S(2)}) async-start(), calls=%async_computation.4 | async-start | bytes 4718592 | tf_op jit(solution)/shard_map/reduce_scatter | solution.py:97
  104.3 3.8 %copy-start = (f32[512,256,8]{1,0,2:T(8,128)S(1)}, f32[512,256,8]{1,0,2:T(8,128)}, u32[]{:S(2)}) copy-start(f32[512,256,8]{1,0,2:T(8,128)} %get-tuple-element.495) | copy-start | bytes 12582916 | tf_op jit(solution)/shard_map/while
  114.6 3.8 %copy-start = (f32[512,256,8]{1,0,2:T(8,128)S(1)}, f32[512,256,8]{1,0,2:T(8,128)}, u32[]{:S(2)}) copy-start(f32[512,256,8]{1,0,2:T(8,128)} %get-tuple-element.495) | copy-start | bytes 12582916 | tf_op jit(solution)/shard_map/while
  125.0 3.8 %copy-start = (f32[512,256,8]{1,0,2:T(8,128)S(1)}, f32[512,256,8]{1,0,2:T(8,128)}, u32[]{:S(2)}) copy-start(f32[512,256,8]{1,0,2:T(8,128)} %get-tuple-element.495) | copy-start | bytes 12582916 | tf_op jit(solution)/shard_map/while
  135.4 3.8 %copy-start = (f32[512,256,8]{1,0,2:T(8,128)S(1)}, f32[512,256,8]{1,0,2:T(8,128)}, u32[]{:S(2)}) copy-start(f32[512,256,8]{1,0,2:T(8,128)} %get-tuple-element.495) | copy-start | bytes 12582916 | tf_op jit(solution)/shard_map/while
  145.7 4.0 %copy-start = (f32[512,256,8]{1,0,2:T(8,128)S(1)}, f32[512,256,8]{1,0,2:T(8,128)}, u32[]{:S(2)}) copy-start(f32[512,256,8]{1,0,2:T(8,128)} %get-tuple-element.495) | copy-start | bytes 12582916 | tf_op jit(solution)/shard_map/while
  156.3 3.8 %copy-start = (f32[512,256,8]{1,0,2:T(8,128)S(1)}, f32[512,256,8]{1,0,2:T(8,128)}, u32[]{:S(2)}) copy-start(f32[512,256,8]{1,0,2:T(8,128)} %get-tuple-element.495) | copy-start | bytes 12582916 | tf_op jit(solution)/shard_map/while
  166.7 3.8 %copy-start = (f32[512,256,8]{1,0,2:T(8,128)S(1)}, f32[512,256,8]{1,0,2:T(8,128)}, u32[]{:S(2)}) copy-start(f32[512,256,8]{1,0,2:T(8,128)} %get-tuple-element.495) | copy-start | bytes 12582916 | tf_op jit(solution)/shard_map/while
  177.0 4.0 %copy-start = (f32[512,256,8]{1,0,2:T(8,128)S(1)}, f32[512,256,8]{1,0,2:T(8,128)}, u32[]{:S(2)}) copy-start(f32[512,256,8]{1,0,2:T(8,128)} %get-tuple-element.495) | copy-start | bytes 12582916 | tf_op jit(solution)/shard_map/while
Sparse Core Ops, SparseCore 0:
  9.5 44.8 all-gather.3
  56.5 42.0 all-gather.5
  100.8 120.4 all-gather.7
  233.4 37.3 reduce-scatter.1
where the time goes:
time: 278 us; the launch traced here: 277 us
  waiting for transfers between devices  164 us (59%)
  matrix products  71.7 us (26%)
  local copies, waits for them, and re-layouts  15.6 us (6%)
  between operations  13.2 us (5%)
  other arithmetic  12 us (4%)
    all_gather x1, waiting for transfers between devices, shards(): value_part = lax.all_gather(values, ('outer', 'inner'), axis=0, tiled=True)  44.3 us
    all_gather x1, waiting for transfers between devices, shards(): key_part = lax.all_gather(keys, ('outer', 'inner'), axis=0, tiled=True)  41.5 us
    all_gather x1, waiting for transfers between devices, shards(): lax.all_gather(out_weight, ('outer', 'inner'), axis=1, tiled=True)  38.9 us
    reduce_scatter x1, waiting for transfers between devices, shards(): lax.psum_scatter(partial_out.astype(jnp.bfloat16), 'tensor', scatter_dime...  37.5 us
    dot_general x8, matrix products, update(): jnp.einsum('gjqk,kgd->gjqd', expo.astype(jnp.bfloat16), value_grid, prefe...  30.7 us
    dot_general x8, matrix products, update(): jnp.einsum('qgjd,kgd->gjqk', query_grid, key_grid, preferred_element_type...  28.9 us
    dot_general x1, matrix products, shards(): jnp.dot(flat, lax.all_gather(out_weight, ('outer', 'inner'), axis=1, tile...  12 us
    reduce_sum x8, other arithmetic, update(): new_total = running_total * shrink + jnp.sum(expo, axis=-1)  7.06 us
  transfers between devices with their start and end apart: 4, of which 4 were waited for; matrix products, arithmetic and copies ran while one was open for 31% of the time, Pallas kernels for 0%

commit v1 on v0

v1 whole, which is shorter than its diff:
```python
import functools
import math

import jax
import jax.numpy as jnp
from jax import lax
from jax.experimental import pallas as pl
from jax.experimental.pallas import tpu as pltpu
from jax.sharding import Mesh
from jax.sharding import PartitionSpec as P

DH = 128
RUN = 64
CHUNK = 256
MAX_CHUNKS = 10
NEGATIVE = -1e30
Z = ("zh", "zl")
Z_ORDER = (0, -1, 1, 2)


def z_index():
    return lax.axis_index("zh") * 2 + lax.axis_index("zl")


def shift(value, axis, step):
    return lax.ppermute(value, axis, [(i, (i + step) % 4) for i in range(4)])


def swap_cores(value):
    return lax.ppermute(value, "c", [(0, 1), (1, 0)])


def attend_kernel(pos, lengths, spans, q, kv, left, right, left2, right2, out, ks, vs, ss, top, tot, acc):
    z, x = z_index(), lax.axis_index("x")
    rows, heads = q.shape[0], q.shape[1] // DH
    runs = rows // RUN

    def place(ref, row, group):
        for i in range(runs):
            at = pl.multiple_of(pos[(group * runs + i) * RUN], RUN)
            ks[pl.ds(at, RUN), :] = ref[row + RUN * i : row + RUN * (i + 1), :]
            vs[pl.ds(at, RUN), :] = ref[row + rows + RUN * i : row + rows + RUN * (i + 1), :]

    for ref, step, held in (
        (kv, 0, (0, 1, 2, 3)),
        (left, -1, (0, 1, 2, 3)),
        (right, 1, (0, 1, 2, 3)),
        (left2, 2, (0, 1)),
        (right2, 2, (2, 3)),
    ):
        for n, j in enumerate(held):
            group = lax.rem(z + Z_ORDER[j] + 4, 4) * 4 + lax.rem(x + step + 4, 4)
            place(ref, 2 * rows * n, group)

    ends = []
    for d in range(lengths.shape[0]):
        ends.append(lengths[d] + (ends[-1] if ends else 0))
    starts = [0] + ends[:-1]
    span_list = [(spans[0, k], spans[1, k]) for k in range(spans.shape[1])]

    def interval(at):
        low = jnp.zeros_like(at)
        end = jnp.zeros_like(at)
        for first, last in zip(starts, ends):
            inside = (at >= first) & (at < last)
            low = jnp.where(inside, first, low)
            end = jnp.where(inside, last, end)
        high = at + 1
        for first, last in span_list:
            inside = (at >= first) & (at < last)
            high = jnp.where(inside, jnp.maximum(high, jnp.minimum(last, end)), high)
        return low, high

    scale = math.log2(math.e) / math.sqrt(DH)
    first_group = (z * 4 + x) * runs

    def block(i, _):
        p0 = pos[(first_group + i) * RUN]
        row = pl.multiple_of(i * RUN, RUN)
        at = p0 + lax.broadcasted_iota(jnp.int32, (RUN, DH), 0)
        low, high = interval(at)
        width = high - low
        first_low, _ = interval(p0)
        _, last_high = interval(p0 + RUN - 1)
        first_chunk = first_low // CHUNK
        end_chunk = (last_high + CHUNK - 1) // CHUNK
        lanes = lax.broadcasted_iota(jnp.int32, (RUN, DH), 1) - low
        queries = jnp.concatenate([q[pl.ds(row, RUN), h * DH : (h + 1) * DH] for h in range(heads)], axis=0)
        top[...] = jnp.full_like(top, NEGATIVE)
        tot[...] = jnp.zeros_like(tot)
        acc[...] = jnp.zeros_like(acc)

        def score(j, _):
            start = pl.multiple_of(j * CHUNK, CHUNK)
            keys = ks[pl.ds(start, CHUNK), :]
            s = lax.dot_general(queries, keys, (((1,), (1,)), ((), ())), preferred_element_type=jnp.float32)
            for n in range(CHUNK // DH):
                t = lanes + (start + n * DH)
                allowed = (t >= 0) & (t < width)
                part = s[:, n * DH : (n + 1) * DH].reshape(heads, RUN, DH)
                part = jnp.where(allowed[None], part, NEGATIVE).reshape(heads * RUN, DH)
                ss[j - first_chunk, :, n * DH : (n + 1) * DH] = part
                top[...] = jnp.maximum(top[...], part)
            return 0

        lax.fori_loop(first_chunk, end_chunk, score, 0)
        highest = jnp.max(top[...], axis=1, keepdims=True)

        def mix(j, _):
            start = pl.multiple_of(j * CHUNK, CHUNK)
            expo = jnp.exp2((ss[j - first_chunk] - highest) * scale)
            total = tot[...]
            for n in range(CHUNK // DH):
                total = total + expo[:, n * DH : (n + 1) * DH]
            tot[...] = total
            acc[...] += jnp.dot(expo.astype(jnp.bfloat16), vs[pl.ds(start, CHUNK), :], preferred_element_type=jnp.float32)
            return 0

        lax.fori_loop(first_chunk, end_chunk, mix, 0)
        total = jnp.sum(tot[...], axis=1, keepdims=True)
        mixed = (acc[...] / total).astype(jnp.bfloat16)
        for h in range(heads):
            out[pl.ds(row, RUN), h * DH : (h + 1) * DH] = mixed[h * RUN : (h + 1) * RUN]
        return 0

    lax.fori_loop(0, runs, block, 0)


def attend(positions, lengths, spans, q, pieces):
    rows = q.shape[0]
    stacked = q.shape[1] // DH * RUN
    smem = pl.BlockSpec(memory_space=pltpu.SMEM)
    vmem = pl.BlockSpec(memory_space=pltpu.VMEM)
    slots = positions.shape[0]
    return pl.pallas_call(
        attend_kernel,
        out_shape=jax.ShapeDtypeStruct(q.shape, jnp.bfloat16),
        in_specs=[smem] * 3 + [vmem] * (1 + len(pieces)),
        out_specs=vmem,
        scratch_shapes=[
            pltpu.VMEM((slots, DH), jnp.bfloat16),
            pltpu.VMEM((slots, DH), jnp.bfloat16),
            pltpu.VMEM((MAX_CHUNKS, stacked, CHUNK), jnp.float32),
            pltpu.VMEM((stacked, DH), jnp.float32),
            pltpu.VMEM((stacked, DH), jnp.float32),
            pltpu.VMEM((stacked, DH), jnp.float32),
        ],
        compiler_params=pltpu.CompilerParams(vmem_limit_bytes=40 * 2**20),
        cost_estimate=pl.CostEstimate(
            flops=4 * rows * slots // 4 * q.shape[1], bytes_accessed=4 * 2**20, transcendentals=rows * slots * 2
        ),
        name="attend",
    )(positions, lengths, spans, q, *pieces)


def project_kernel(steps, *refs):
    own, left, right, left2, right2, w0, wl, wr, wl2, wr2 = refs[:10]
    outs = refs[10 : 10 + 2 * len(steps)]
    rows, weights, row_sems, weight_sems = refs[10 + 2 * len(steps) :]
    z, x, y, core = z_index(), lax.axis_index("x"), lax.axis_index("y"), lax.axis_index("c")
    count, half = own.shape[0], own.shape[0] // 2
    depth = w0.shape[0] // 2

    copies = []
    x2 = lax.rem(x + 2, 4)
    for n, (ref, target) in enumerate(
        (
            (own, rows.at[x]),
            (left, rows.at[lax.rem(x + 3, 4)]),
            (right, rows.at[lax.rem(x + 1, 4)]),
            (left2, rows.at[x2, pl.ds(0, half)]),
            (right2, rows.at[x2, pl.ds(half, half)]),
        )
    ):
        copies.append(pltpu.make_async_copy(ref, target, row_sems.at[n]))
    for copy in copies:
        copy.start()

    def weight_copies(n, offset):
        if offset == 2:
            return [
                pltpu.make_async_copy(wl2, weights.at[n, pl.ds(0, depth)], weight_sems.at[n, 0]),
                pltpu.make_async_copy(wr2, weights.at[n, pl.ds(depth, depth)], weight_sems.at[n, 1]),
            ]
        ref = {0: w0, 1: wr, 3: wl}[offset]
        return [pltpu.make_async_copy(ref, weights.at[n], weight_sems.at[n, 0])]

    for n, step in enumerate(steps):
        wanted = lax.rem(y + step + 4 - z + 4, 4)
        for offset in range(4):

            @pl.when(wanted == offset)
            def _():
                for copy in weight_copies(n, offset):
                    copy.start()

    for copy in copies:
        copy.wait()
    for n, step in enumerate(steps):
        wanted = lax.rem(y + step + 4 - z + 4, 4)
        for offset in range(4):

            @pl.when(wanted == offset)
            def _():
                for copy in weight_copies(n, offset):
                    copy.wait()

        for which, first in ((1, 2 - 2 * core), (0, 2 * core)):
            for j in range(2):
                outs[2 * n + which][j * count : (j + 1) * count, :] = jnp.dot(
                    rows[first + j], weights[n], preferred_element_type=jnp.float32
                ).astype(jnp.bfloat16)


def project(steps, att_pieces, w_pieces):
    any_ = pl.BlockSpec(memory_space=pl.ANY)
    vmem = pl.BlockSpec(memory_space=pltpu.VMEM)
    count, depth = att_pieces[0].shape
    width = w_pieces[0].shape[1]
    n = len(steps)
    return pl.pallas_call(
        functools.partial(project_kernel, steps),
        out_shape=[jax.ShapeDtypeStruct((2 * count, width), jnp.bfloat16)] * (2 * n),
        in_specs=[any_] * 10,
        out_specs=[vmem] * (2 * n),
        scratch_shapes=[
            pltpu.VMEM((4, count, depth), jnp.bfloat16),
            pltpu.VMEM((n, depth, width), jnp.bfloat16),
            pltpu.SemaphoreType.DMA((5,)),
            pltpu.SemaphoreType.DMA((n, 2)),
        ],
        compiler_params=pltpu.CompilerParams(vmem_limit_bytes=40 * 2**20),
        cost_estimate=pl.CostEstimate(
            flops=2 * 4 * count * depth * width * n, bytes_accessed=(4 + 2 * n) * 2**20, transcendentals=0
        ),
        name="project",
    )(*att_pieces, *w_pieces)


def plus(*parts):
    total = parts[0].astype(jnp.float32)
    for part in parts[1:]:
        total = total + part.astype(jnp.float32)
    return total.astype(jnp.bfloat16)


def ring_gather(value, axis):
    half = value.shape[0] // 2
    left = shift(value, axis, 1)
    right = shift(value, axis, -1)
    left2 = shift(left[:half], axis, 1)
    right2 = shift(right[half:], axis, -1)
    return value, left, right, left2, right2


def shards(queries, keys, values, positions, lengths, spans, weight):
    count = queries.shape[0]
    kv = jnp.concatenate([keys, values], axis=0)
    line = [kv, shift(kv, Z, 1), shift(kv, Z, -1), shift(kv, Z, 2)]
    line = jnp.concatenate(line, axis=0)
    line, weight = lax.optimization_barrier((line, weight))
    pieces = ring_gather(line, "x")
    w_pieces = ring_gather(weight, Z)
    attended = attend(positions, lengths, spans, queries, pieces)
    att_pieces = ring_gather(attended, "x")

    keep2, send2 = project((2,), att_pieces, w_pieces)
    far = plus(keep2, swap_cores(send2))
    from_left = shift(far[:count], "y", 1)
    from_right = shift(far[count:], "y", -1)
    keep_up, send_up, keep_down, send_down = project((1, -1), att_pieces, w_pieces)
    up = plus(keep_up, swap_cores(send_up))
    down = plus(keep_down, swap_cores(send_down))
    up = jnp.concatenate([plus(up[:count], from_left), up[count:]], axis=0)
    down = jnp.concatenate([down[:count], plus(down[count:], from_right)], axis=0)
    from_below = shift(up, "y", 1)
    from_above = shift(down, "y", -1)
    keep0, send0 = project((0,), att_pieces, w_pieces)
    total = plus(keep0, swap_cores(send0), from_below, from_above)

    low = lax.rem(lax.axis_index("x"), 2)
    same = lax.dynamic_slice_in_dim(total, low * count, count, 0)
    other = lax.dynamic_slice_in_dim(total, (1 - low) * count, count, 0)

    def pairs(flip):
        return [
            ((2 * a + b) * 2 + c, (2 * c + (b ^ flip)) * 2 + a) for a in range(2) for b in range(2) for c in range(2)
        ]

    same = lax.ppermute(same, ("x", "c"), pairs(0))
    other = lax.ppermute(other, ("x", "c"), pairs(1))
    return jnp.where(
        low == 0, jnp.concatenate([same, other], axis=1), jnp.concatenate([other, same], axis=1)
    )


def solution(mesh):
    fine = Mesh(mesh.devices.reshape(2, 2, 4, 4, 2), ("zh", "zl", "x", "y", "c"))
    rows, columns = ("zh", "zl", "x"), ("y", "c")
    return jax.shard_map(
        shards,
        mesh=fine,
        in_specs=(P(rows, columns), P(rows, columns), P(rows, columns), P(), P(), P(), P(columns, rows)),
        out_specs=P(rows, columns),
        check_vma=False,
    )
```

time: 278 us -> 115 us (0.41)
  the two profiles are of different devices: /device:TPU:6 before, /device:TPU:1 now
where the time goes in v1:
time: 115 us; the launch traced here: 114 us
  waiting for transfers between devices  52.5 us (46%)
  starting transfers between devices  45 us (39%)
  Pallas kernels  12.7 us (11%)
  other arithmetic  2.61 us (2%)
  local copies, waits for them, and re-layouts  1.32 us (1%)
    ppermute x19, waiting for transfers between devices, shift(): return lax.ppermute(value, axis, [(i, (i + step) % 4) for i in range(4)])  45.2 us
    ppermute x19, starting transfers between devices, shift(): return lax.ppermute(value, axis, [(i, (i + step) % 4) for i in range(4)])  31.4 us
    pallas_call x1, Pallas kernels, attend(): pl.pallas_call(attend_kernel, out_shape=jax.ShapeDtypeStruct(q.shape, jnp...  6.61 us
    ppermute x4, starting transfers between devices, swap_cores(): return lax.ppermute(value, 'c', [(0, 1), (1, 0)])  6.23 us
    pallas_call x3, Pallas kernels, project(): pl.pallas_call(functools.partial(project_kernel, steps), out_shape=[jax.S...  6.06 us
    ppermute x1, starting transfers between devices, shards(): other = lax.ppermute(other, ('x', 'c'), pairs(1))  5.43 us
    ppermute x1, waiting for transfers between devices, shards(): other = lax.ppermute(other, ('x', 'c'), pairs(1))  4.2 us
    ppermute x1, waiting for transfers between devices, shards(): same = lax.ppermute(same, ('x', 'c'), pairs(0))  3.06 us
  transfers between devices with their start and end apart: 25, of which 11 were waited for; matrix products, arithmetic and copies ran while one was open for 1% of the time, Pallas kernels for 10%

profile of v1, /device:TPU:1, one launch (start us, length us, event | category | flops | bytes accessed | tf_op | source)
XLA Modules:
  0.0 114.4 jit_solution(8262381118227371775)
XLA Ops:
  0.0 0.9 constant_dynamic-update-slice_fusion.1
  1.0 2.5 %collective-permute-start = (bf16[512,128]{1,0:T(8,128)(2,1)S(1)}, bf16[512,128]{1,0:T(8,128)(2,1)S(1)}, u32[]{:S(2)}, u32[]{:S(2)}) collective-permute-start(bf16[512,128]{1,0:T(8,128)(2,1)S(1)} %get-tuple-element.29), channel_id=1, source_target_pairs={{0,32},{32,64},{64,96},{96,0},{1,33},{33,65},{65,97},{97,1},{2,34}... | collective-permute-start | bytes 393224 | tf_op jit(solution)/shard_map/ppermute | solution.py:26
  3.5 2.2 %collective-permute-start.1 = (bf16[512,128]{1,0:T(8,128)(2,1)S(1)}, bf16[512,128]{1,0:T(8,128)(2,1)S(1)}, u32[]{:S(2)}, u32[]{:S(2)}) collective-permute-start(bf16[512,128]{1,0:T(8,128)(2,1)S(1)} %get-tuple-element.29), channel_id=1, source_target_pairs={{0,96},{32,0},{64,32},{96,64},{1,97},{33,1},{65,33},{97,65},{2,98}... | collective-permute-start | bytes 393224 | tf_op jit(solution)/shard_map/ppermute | solution.py:26
  5.7 1.2 %collective-permute-start.2 = (bf16[512,128]{1,0:T(8,128)(2,1)S(1)}, bf16[512,128]{1,0:T(8,128)(2,1)S(1)}, u32[]{:S(2)}, u32[]{:S(2)}) collective-permute-start(bf16[512,128]{1,0:T(8,128)(2,1)S(1)} %get-tuple-element.29), channel_id=1, source_target_pairs={{0,64},{32,96},{64,0},{96,32},{1,65},{33,97},{65,1},{97,33},{2,66}... | collective-permute-start | bytes 393224 | tf_op jit(solution)/shard_map/ppermute | solution.py:26
  7.0 1.9 %collective-permute-done = bf16[512,128]{1,0:T(8,128)(2,1)S(1)} collective-permute-done((bf16[512,128]{1,0:T(8,128)(2,1)S(1)}, bf16[512,128]{1,0:T(8,128)(2,1)S(1)}, u32[]{:S(2)}, u32[]{:S(2)}) %collective-permute-start) | collective-permute-done | bytes 131104 | tf_op jit(solution)/shard_map/ppermute | solution.py:26
  8.9 3.8 %collective-permute-done.2 = bf16[512,128]{1,0:T(8,128)(2,1)S(1)} collective-permute-done((bf16[512,128]{1,0:T(8,128)(2,1)S(1)}, bf16[512,128]{1,0:T(8,128)(2,1)S(1)}, u32[]{:S(2)}, u32[]{:S(2)}) %collective-permute-start.2) | collective-permute-done | bytes 131104 | tf_op jit(solution)/shard_map/ppermute | solution.py:26
  12.7 1.3 %collective-permute-start.3 = (bf16[2048,128]{1,0:T(8,128)(2,1)S(1)}, bf16[2048,128]{1,0:T(8,128)(2,1)S(1)}, u32[]{:S(2)}, u32[]{:S(2)}) collective-permute-start(bf16[2048,128]{1,0:T(8,128)(2,1)S(1)} %constant_dynamic-update-slice_fusion.2.kv), channel_id=1, source_target_pairs={{0,8},{8,16},{16,24},{24,0},{1,9},{9,17},{17,25},{25,1},{2,10},{10... | collective-permute-start | bytes 1572872 | tf_op jit(solution)/shard_map/ppermute | solution.py:26
  14.0 1.5 %collective-permute-start.4 = (bf16[2048,128]{1,0:T(8,128)(2,1)S(1)}, bf16[2048,128]{1,0:T(8,128)(2,1)S(1)}, u32[]{:S(2)}, u32[]{:S(2)}) collective-permute-start(bf16[2048,128]{1,0:T(8,128)(2,1)S(1)} %constant_dynamic-update-slice_fusion.2.kv), channel_id=1, source_target_pairs={{0,24},{8,0},{16,8},{24,16},{1,25},{9,1},{17,9},{25,17},{2,26},{10... | collective-permute-start | bytes 1572872 | tf_op jit(solution)/shard_map/ppermute | solution.py:26
  15.5 0.1 collective-permute-start.11
  15.6 2.6 %collective-permute-start.12 = (bf16[1024,512]{1,0:T(8,128)(2,1)S(1)}, bf16[1024,512]{1,0:T(8,128)(2,1)S(1)}, u32[]{:S(2)}, u32[]{:S(2)}) collective-permute-start(bf16[1024,512]{1,0:T(8,128)(2,1)S(1)} %copy-done), channel_id=1, source_target_pairs={{0,96},{32,0},{64,32},{96,64},{1,97},{33,1},{65,33},{97,65},{2,98}... | collective-permute-start | bytes 3145736 | tf_op jit(solution)/shard_map/ppermute | solution.py:26
  18.2 7.9 %collective-permute-done.3.left = bf16[2048,128]{1,0:T(8,128)(2,1)S(1)} collective-permute-done((bf16[2048,128]{1,0:T(8,128)(2,1)S(1)}, bf16[2048,128]{1,0:T(8,128)(2,1)S(1)}, u32[]{:S(2)}, u32[]{:S(2)}) %collective-permute-start.3) | collective-permute-done | bytes 524320 | tf_op jit(solution)/shard_map/ppermute | solution.py:26
  26.1 0.1 collective-permute-start.5
  26.2 2.7 %collective-permute-start.6 = (bf16[1024,128]{1,0:T(8,128)(2,1)S(1)}, bf16[1024,128]{1,0:T(8,128)(2,1)S(1)}, u32[]{:S(2)}, u32[]{:S(2)}) collective-permute-start(bf16[1024,128]{1,0:T(8,128)(2,1)S(1)} %slice.49), channel_id=1, source_target_pairs={{0,24},{8,0},{16,8},{24,16},{1,25},{9,1},{17,9},{25,17},{2,26},{10... | collective-permute-start | bytes 786440 | tf_op jit(solution)/shard_map/ppermute | solution.py:26
  29.0 4.0 %collective-permute-done.5.left2 = bf16[1024,128]{1,0:T(8,128)(2,1)S(1)} collective-permute-done((bf16[1024,128]{1,0:T(8,128)(2,1)S(1)}, bf16[1024,128]{1,0:T(8,128)(2,1)S(1)}, u32[]{:S(2)}, u32[]{:S(2)}) %collective-permute-start.5) | collective-permute-done | bytes 262176 | tf_op jit(solution)/shard_map/ppermute | solution.py:26
  33.0 6.6 %attend.1.refs_0_ = bf16[256,1024]{1,0:T(8,128)(2,1)S(1)} custom-call(s32[4096]{0:T(1024)S(1)} %copy-done.2, s32[8]{0:T(128)S(1)} %copy-done.4, s32[2,4]{1,0:T(2,128)S(1)} %copy-done.3, bf16[256,1024]{1,0:T(8,128)(2,1)S(1)} %copy-done.1, bf16[2048,128]{1,0:T(8,128)(2,1)S(1)} %constant_dynamic-update-slice_fusion.2.kv, ...), custom_call_target="tpu_custom_call" | custom-call | flops 1073741824 | bytes 4194304 | tf_op jit(solution)/shard_map/attend/pallas_call | solution.py:135
  39.6 1.1 collective-permute-start.7
  40.7 4.2 %collective-permute-start.8 = (bf16[256,1024]{1,0:T(8,128)(2,1)S(1)}, bf16[256,1024]{1,0:T(8,128)(2,1)S(1)}, u32[]{:S(2)}, u32[]{:S(2)}) collective-permute-start(bf16[256,1024]{1,0:T(8,128)(2,1)S(1)} %attend.1.refs_0_), channel_id=1, source_target_pairs={{0,24},{8,0},{16,8},{24,16},{1,25},{9,1},{17,9},{25,17},{2,26},{10... | collective-permute-start | bytes 1572872 | tf_op jit(solution)/shard_map/ppermute | solution.py:26
  44.9 0.1 collective-permute-start.13
  45.0 2.7 %collective-permute-start.14 = (bf16[512,512]{1,0:T(8,128)(2,1)S(1)}, bf16[512,512]{1,0:T(8,128)(2,1)S(1)}, u32[]{:S(2)}, u32[]{:S(2)}) collective-permute-start(bf16[512,512]{1,0:T(8,128)(2,1)S(1)} %slice.53), channel_id=1, source_target_pairs={{0,96},{32,0},{64,32},{96,64},{1,97},{33,1},{65,33},{97,65},{2,98}... | collective-permute-start | bytes 1572872 | tf_op jit(solution)/shard_map/ppermute | solution.py:26
  47.7 5.8 %collective-permute-done.7.refs_1_ = bf16[256,1024]{1,0:T(8,128)(2,1)S(1)} collective-permute-done((bf16[256,1024]{1,0:T(8,128)(2,1)S(1)}, bf16[256,1024]{1,0:T(8,128)(2,1)S(1)}, u32[]{:S(2)}, u32[]{:S(2)}) %collective-permute-start.7) | collective-permute-done | bytes 524320 | tf_op jit(solution)/shard_map/ppermute | solution.py:26
  53.5 0.1 collective-permute-start.9
  53.7 2.7 %collective-permute-start.10 = (bf16[128,1024]{1,0:T(8,128)(2,1)S(1)}, bf16[128,1024]{1,0:T(8,128)(2,1)S(1)}, u32[]{:S(2)}, u32[]{:S(2)}) collective-permute-start(bf16[128,1024]{1,0:T(8,128)(2,1)S(1)} %slice.51), channel_id=1, source_target_pairs={{0,24},{8,0},{16,8},{24,16},{1,25},{9,1},{17,9},{25,17},{2,26},{10... | collective-permute-start | bytes 786440 | tf_op jit(solution)/shard_map/ppermute | solution.py:26
  56.4 3.7 %collective-permute-done.9.refs_3_ = bf16[128,1024]{1,0:T(8,128)(2,1)S(1)} collective-permute-done((bf16[128,1024]{1,0:T(8,128)(2,1)S(1)}, bf16[128,1024]{1,0:T(8,128)(2,1)S(1)}, u32[]{:S(2)}, u32[]{:S(2)}) %collective-permute-start.9) | collective-permute-done | bytes 262176 | tf_op jit(solution)/shard_map/ppermute | solution.py:26
  60.1 1.6 %project.5 = (bf16[512,512]{1,0:T(8,128)(2,1)S(1)}, bf16[512,512]{1,0:T(8,128)(2,1)S(1)}) custom-call(bf16[256,1024]{1,0:T(8,128)(2,1)S(1)} %attend.1.refs_0_, bf16[256,1024]{1,0:T(8,128)(2,1)S(1)} %collective-permute-done.7.refs_1_, bf16[256,1024]{1,0:T(8,128)(2,1)S(1)} %collective-permute-done.8.refs_2_, ...), custom_call_target="tpu_custom_call" | custom-call | flops 1073741824 | bytes 6291456 | tf_op jit(solution)/shard_map/project/pallas_call | solution.py:221
  61.7 5.3 %collective-permute-start.17 = (bf16[512,512]{1,0:T(8,128)(2,1)S(1)}, bf16[512,512]{1,0:T(8,128)(2,1)S(1)}, u32[]{:S(2)}, u32[]{:S(2)}) collective-permute-start(bf16[512,512]{1,0:T(8,128)(2,1)S(1)} %get-tuple-element.22), channel_id=1, source_target_pairs={{0,1},{1,0},{2,3},{3,2},{4,5},{5,4},{6,7},{7,6},{8,9},{9,8},{10,11... | collective-permute-start | bytes 1572872 | tf_op jit(solution)/shard_map/ppermute | solution.py:30
  67.0 2.9 %project.4 = (bf16[512,512]{1,0:T(8,128)(2,1)S(1)}, bf16[512,512]{1,0:T(8,128)(2,1)S(1)}, bf16[512,512]{1,0:T(8,128)(2,1)S(1)}, bf16[512,512]{1,0:T(8,128)(2,1)S(1)}) custom-call(bf16[256,1024]{1,0:T(8,128)(2,1)S(1)} %attend.1.refs_0_, bf16[256,1024]{1,0:T(8,128)(2,1)S(1)} %collective-permute-done.7.refs_1_, ...), custom_call_target="tpu_custom_call" | custom-call | flops 2147483648 | bytes 8388608 | tf_op jit(solution)/shard_map/project/pallas_call | solution.py:221
  69.9 0.1 collective-permute-start.20
  70.0 0.5 collective-permute-start.16
  70.5 1.6 %project.3 = (bf16[512,512]{1,0:T(8,128)(2,1)S(1)}, bf16[512,512]{1,0:T(8,128)(2,1)S(1)}) custom-call(bf16[256,1024]{1,0:T(8,128)(2,1)S(1)} %attend.1.refs_0_, bf16[256,1024]{1,0:T(8,128)(2,1)S(1)} %collective-permute-done.7.refs_1_, bf16[256,1024]{1,0:T(8,128)(2,1)S(1)} %collective-permute-done.8.refs_2_, ...), custom_call_target="tpu_custom_call" | custom-call | flops 1073741824 | bytes 6291456 | tf_op jit(solution)/shard_map/project/pallas_call | solution.py:221
  72.1 0.4 collective-permute-start.15
  72.4 0.1 add_convert_fusion.2
  72.6 2.8 %collective-permute-start.21 = (bf16[256,512]{1,0:T(8,128)(2,1)S(1)}, bf16[256,512]{1,0:T(8,128)(2,1)S(1)}, u32[]{:S(2)}, u32[]{:S(2)}) collective-permute-start(bf16[256,512]{1,0:T(8,128)(2,1)S(1)} %get-tuple-element.28), channel_id=1, source_target_pairs={{0,6},{2,0},{4,2},{6,4},{1,7},{3,1},{5,3},{7,5},{8,14},{10,8},{12,... | collective-permute-start | bytes 786440 | tf_op jit(solution)/shard_map/ppermute | solution.py:26
  75.4 0.1 add_convert_fusion.1
  75.6 0.1 add_convert_fusion.3
  75.8 0.1 collective-permute-start.18
  75.9 4.8 %collective-permute-done.21 = bf16[256,512]{1,0:T(8,128)(2,1)S(1)} collective-permute-done((bf16[256,512]{1,0:T(8,128)(2,1)S(1)}, bf16[256,512]{1,0:T(8,128)(2,1)S(1)}, u32[]{:S(2)}, u32[]{:S(2)}) %collective-permute-start.21) | collective-permute-done | bytes 262176 | tf_op jit(solution)/shard_map/ppermute | solution.py:26
  80.7 0.1 add_convert_fusion.4
  80.8 3.5 %collective-permute-start.22 = (bf16[512,512]{1,0:T(8,128)(2,1)S(1)}, bf16[512,512]{1,0:T(8,128)(2,1)S(1)}, u32[]{:S(2)}, u32[]{:S(2)}) collective-permute-start(bf16[512,512]{1,0:T(8,128)(2,1)S(1)} %pad_maximum_fusion.1), channel_id=1, source_target_pairs={{0,6},{2,0},{4,2},{6,4},{1,7},{3,1},{5,3},{7,5},{8,14},{10,8},{12,... | collective-permute-start | bytes 1572872 | tf_op jit(solution)/shard_map/ppermute | solution.py:26
  84.3 0.1 add_convert_fusion.5
  84.4 0.8 pad_maximum_fusion
  85.2 9.1 %collective-permute-done.22 = bf16[512,512]{1,0:T(8,128)(2,1)S(1)} collective-permute-done((bf16[512,512]{1,0:T(8,128)(2,1)S(1)}, bf16[512,512]{1,0:T(8,128)(2,1)S(1)}, u32[]{:S(2)}, u32[]{:S(2)}) %collective-permute-start.22) | collective-permute-done | bytes 524320 | tf_op jit(solution)/shard_map/ppermute | solution.py:26
  94.3 4.2 %collective-permute-done.19 = bf16[512,512]{1,0:T(8,128)(2,1)S(1)} collective-permute-done((bf16[512,512]{1,0:T(8,128)(2,1)}, bf16[512,512]{1,0:T(8,128)(2,1)S(1)}, u32[]{:S(2)}, u32[]{:S(2)}) %collective-permute-start.19) | collective-permute-done | bytes 524320 | tf_op jit(solution)/shard_map/ppermute | solution.py:26
  98.5 0.3 add_convert_fusion
  98.8 5.4 %collective-permute-start.24 = (bf16[256,512]{1,0:T(8,128)(2,1)S(1)}, bf16[256,512]{1,0:T(8,128)(2,1)S(1)}, u32[]{:S(2)}, u32[]{:S(2)}) collective-permute-start(bf16[256,512]{1,0:T(8,128)(2,1)S(1)} %get-tuple-element.26), channel_id=1, source_target_pairs={{0,8},{1,24},{8,0},{9,16},{16,9},{17,25},{24,1},{25,17},{2,10},{3,... | collective-permute-start | bytes 786440 | tf_op jit(solution)/shard_map/ppermute | solution.py:291
  104.3 1.9 %collective-permute-start.23 = (bf16[256,512]{1,0:T(8,128)(2,1)S(1)}, bf16[256,512]{1,0:T(8,128)(2,1)S(1)}, u32[]{:S(2)}, u32[]{:S(2)}) collective-permute-start(bf16[256,512]{1,0:T(8,128)(2,1)S(1)} %get-tuple-element.25), channel_id=1, source_target_pairs={{0,0},{1,16},{8,8},{9,24},{16,1},{17,17},{24,9},{25,25},{2,2},{3,1... | collective-permute-start | bytes 786440 | tf_op jit(solution)/shard_map/ppermute | solution.py:290
  106.2 4.2 %collective-permute-done.24 = bf16[256,512]{1,0:T(8,128)(2,1)S(1)} collective-permute-done((bf16[256,512]{1,0:T(8,128)(2,1)S(1)}, bf16[256,512]{1,0:T(8,128)(2,1)S(1)}, u32[]{:S(2)}, u32[]{:S(2)}) %collective-permute-start.24) | collective-permute-done | bytes 262176 | tf_op jit(solution)/shard_map/ppermute | solution.py:291
  110.4 3.1 %collective-permute-done.23 = bf16[256,512]{1,0:T(8,128)(2,1)S(1)} collective-permute-done((bf16[256,512]{1,0:T(8,128)(2,1)S(1)}, bf16[256,512]{1,0:T(8,128)(2,1)S(1)}, u32[]{:S(2)}, u32[]{:S(2)}) %collective-permute-start.23) | collective-permute-done | bytes 262176 | tf_op jit(solution)/shard_map/ppermute | solution.py:290
  113.5 0.9 maximum_select_fusion
  (42 shorter events, 0.5 us)
Async XLA Ops:
  0.0 1.0 copy-start.5
  0.0 15.5 %copy-start = (bf16[1024,512]{1,0:T(8,128)(2,1)S(1)}, bf16[1024,512]{1,0:T(8,128)(2,1)}, u32[]{:S(2)}) copy-start(bf16[1024,512]{1,0:T(8,128)(2,1)} %refs_5_.2) | copy-start | bytes 3145732
  1.0 7.9 %collective-permute-start = (bf16[512,128]{1,0:T(8,128)(2,1)S(1)}, bf16[512,128]{1,0:T(8,128)(2,1)S(1)}, u32[]{:S(2)}, u32[]{:S(2)}) collective-permute-start(bf16[512,128]{1,0:T(8,128)(2,1)S(1)} %get-tuple-element.29), channel_id=1, source_target_pairs={{0,32},{32,64},{64,96},{96,0},{1,33},{33,65},{65,97},{97,1},{2,34}... | collective-permute-start | bytes 393224 | tf_op jit(solution)/shard_map/ppermute | solution.py:26
  3.5 5.4 %collective-permute-start.1 = (bf16[512,128]{1,0:T(8,128)(2,1)S(1)}, bf16[512,128]{1,0:T(8,128)(2,1)S(1)}, u32[]{:S(2)}, u32[]{:S(2)}) collective-permute-start(bf16[512,128]{1,0:T(8,128)(2,1)S(1)} %get-tuple-element.29), channel_id=1, source_target_pairs={{0,96},{32,0},{64,32},{96,64},{1,97},{33,1},{65,33},{97,65},{2,98}... | collective-permute-start | bytes 393224 | tf_op jit(solution)/shard_map/ppermute | solution.py:26
  5.7 7.0 %collective-permute-start.2 = (bf16[512,128]{1,0:T(8,128)(2,1)S(1)}, bf16[512,128]{1,0:T(8,128)(2,1)S(1)}, u32[]{:S(2)}, u32[]{:S(2)}) collective-permute-start(bf16[512,128]{1,0:T(8,128)(2,1)S(1)} %get-tuple-element.29), channel_id=1, source_target_pairs={{0,64},{32,96},{64,0},{96,32},{1,65},{33,97},{65,1},{97,33},{2,66}... | collective-permute-start | bytes 393224 | tf_op jit(solution)/shard_map/ppermute | solution.py:26
  12.7 20.2 %copy-start.1 = (bf16[256,1024]{1,0:T(8,128)(2,1)S(1)}, bf16[256,1024]{1,0:T(8,128)(2,1)}, u32[]{:S(2)}) copy-start(bf16[256,1024]{1,0:T(8,128)(2,1)} %q.1) | copy-start | bytes 1572868
  12.7 13.3 %collective-permute-start.3 = (bf16[2048,128]{1,0:T(8,128)(2,1)S(1)}, bf16[2048,128]{1,0:T(8,128)(2,1)S(1)}, u32[]{:S(2)}, u32[]{:S(2)}) collective-permute-start(bf16[2048,128]{1,0:T(8,128)(2,1)S(1)} %constant_dynamic-update-slice_fusion.2.kv), channel_id=1, source_target_pairs={{0,8},{8,16},{16,24},{24,0},{1,9},{9,17},{17,25},{25,1},{2,10},{10... | collective-permute-start | bytes 1572872 | tf_op jit(solution)/shard_map/ppermute | solution.py:26
  14.0 12.2 %collective-permute-start.4 = (bf16[2048,128]{1,0:T(8,128)(2,1)S(1)}, bf16[2048,128]{1,0:T(8,128)(2,1)S(1)}, u32[]{:S(2)}, u32[]{:S(2)}) collective-permute-start(bf16[2048,128]{1,0:T(8,128)(2,1)S(1)} %constant_dynamic-update-slice_fusion.2.kv), channel_id=1, source_target_pairs={{0,24},{8,0},{16,8},{24,16},{1,25},{9,1},{17,9},{25,17},{2,26},{10... | collective-permute-start | bytes 1572872 | tf_op jit(solution)/shard_map/ppermute | solution.py:26
  15.5 29.3 %collective-permute-start.11 = (bf16[1024,512]{1,0:T(8,128)(2,1)S(1)}, bf16[1024,512]{1,0:T(8,128)(2,1)S(1)}, u32[]{:S(2)}, u32[]{:S(2)}) collective-permute-start(bf16[1024,512]{1,0:T(8,128)(2,1)S(1)} %copy-done), channel_id=1, source_target_pairs={{0,32},{32,64},{64,96},{96,0},{1,33},{33,65},{65,97},{97,1},{2,34}... | collective-permute-start | bytes 3145736 | tf_op jit(solution)/shard_map/ppermute | solution.py:26
  15.6 29.4 %collective-permute-start.12 = (bf16[1024,512]{1,0:T(8,128)(2,1)S(1)}, bf16[1024,512]{1,0:T(8,128)(2,1)S(1)}, u32[]{:S(2)}, u32[]{:S(2)}) collective-permute-start(bf16[1024,512]{1,0:T(8,128)(2,1)S(1)} %copy-done), channel_id=1, source_target_pairs={{0,96},{32,0},{64,32},{96,64},{1,97},{33,1},{65,33},{97,65},{2,98}... | collective-permute-start | bytes 3145736 | tf_op jit(solution)/shard_map/ppermute | solution.py:26
  26.1 6.8 %copy-start.2 = (s32[4096]{0:T(1024)S(1)}, s32[4096]{0:T(1024)}, u32[]{:S(2)}) copy-start(s32[4096]{0:T(1024)} %pos.1) | copy-start | bytes 49156
  26.1 6.8 %copy-start.3 = (s32[2,4]{1,0:T(2,128)S(1)}, s32[2,4]{1,0:T(2,128)}, u32[]{:S(2)}) copy-start(s32[2,4]{1,0:T(2,128)} %spans.1) | copy-start | bytes 100
  26.1 6.8 %copy-start.4 = (s32[8]{0:T(128)S(1)}, s32[8]{0:T(128)}, u32[]{:S(2)}) copy-start(s32[8]{0:T(128)} %lengths.1) | copy-start | bytes 100
  26.1 6.8 %collective-permute-start.5 = (bf16[1024,128]{1,0:T(8,128)(2,1)S(1)}, bf16[1024,128]{1,0:T(8,128)(2,1)S(1)}, u32[]{:S(2)}, u32[]{:S(2)}) collective-permute-start(bf16[1024,128]{1,0:T(8,128)(2,1)S(1)} %slice.48), channel_id=1, source_target_pairs={{0,8},{8,16},{16,24},{24,0},{1,9},{9,17},{17,25},{25,1},{2,10},{10... | collective-permute-start | bytes 786440 | tf_op jit(solution)/shard_map/ppermute | solution.py:26
  26.2 6.7 %collective-permute-start.6 = (bf16[1024,128]{1,0:T(8,128)(2,1)S(1)}, bf16[1024,128]{1,0:T(8,128)(2,1)S(1)}, u32[]{:S(2)}, u32[]{:S(2)}) collective-permute-start(bf16[1024,128]{1,0:T(8,128)(2,1)S(1)} %slice.49), channel_id=1, source_target_pairs={{0,24},{8,0},{16,8},{24,16},{1,25},{9,1},{17,9},{25,17},{2,26},{10... | collective-permute-start | bytes 786440 | tf_op jit(solution)/shard_map/ppermute | solution.py:26
  39.6 13.9 %collective-permute-start.7 = (bf16[256,1024]{1,0:T(8,128)(2,1)S(1)}, bf16[256,1024]{1,0:T(8,128)(2,1)S(1)}, u32[]{:S(2)}, u32[]{:S(2)}) collective-permute-start(bf16[256,1024]{1,0:T(8,128)(2,1)S(1)} %attend.1.refs_0_), channel_id=1, source_target_pairs={{0,8},{8,16},{16,24},{24,0},{1,9},{9,17},{17,25},{25,1},{2,10},{10... | collective-permute-start | bytes 1572872 | tf_op jit(solution)/shard_map/ppermute | solution.py:26
  40.7 13.0 %collective-permute-start.8 = (bf16[256,1024]{1,0:T(8,128)(2,1)S(1)}, bf16[256,1024]{1,0:T(8,128)(2,1)S(1)}, u32[]{:S(2)}, u32[]{:S(2)}) collective-permute-start(bf16[256,1024]{1,0:T(8,128)(2,1)S(1)} %attend.1.refs_0_), channel_id=1, source_target_pairs={{0,24},{8,0},{16,8},{24,16},{1,25},{9,1},{17,9},{25,17},{2,26},{10... | collective-permute-start | bytes 1572872 | tf_op jit(solution)/shard_map/ppermute | solution.py:26
  44.9 15.2 %collective-permute-start.13 = (bf16[512,512]{1,0:T(8,128)(2,1)S(1)}, bf16[512,512]{1,0:T(8,128)(2,1)S(1)}, u32[]{:S(2)}, u32[]{:S(2)}) collective-permute-start(bf16[512,512]{1,0:T(8,128)(2,1)S(1)} %slice.52), channel_id=1, source_target_pairs={{0,32},{32,64},{64,96},{96,0},{1,33},{33,65},{65,97},{97,1},{2,34}... | collective-permute-start | bytes 1572872 | tf_op jit(solution)/shard_map/ppermute | solution.py:26
  45.0 15.1 %collective-permute-start.14 = (bf16[512,512]{1,0:T(8,128)(2,1)S(1)}, bf16[512,512]{1,0:T(8,128)(2,1)S(1)}, u32[]{:S(2)}, u32[]{:S(2)}) collective-permute-start(bf16[512,512]{1,0:T(8,128)(2,1)S(1)} %slice.53), channel_id=1, source_target_pairs={{0,96},{32,0},{64,32},{96,64},{1,97},{33,1},{65,33},{97,65},{2,98}... | collective-permute-start | bytes 1572872 | tf_op jit(solution)/shard_map/ppermute | solution.py:26
  53.5 6.6 %collective-permute-start.9 = (bf16[128,1024]{1,0:T(8,128)(2,1)S(1)}, bf16[128,1024]{1,0:T(8,128)(2,1)S(1)}, u32[]{:S(2)}, u32[]{:S(2)}) collective-permute-start(bf16[128,1024]{1,0:T(8,128)(2,1)S(1)} %slice.50), channel_id=1, source_target_pairs={{0,8},{8,16},{16,24},{24,0},{1,9},{9,17},{17,25},{25,1},{2,10},{10... | collective-permute-start | bytes 786440 | tf_op jit(solution)/shard_map/ppermute | solution.py:26
  53.7 6.4 %collective-permute-start.10 = (bf16[128,1024]{1,0:T(8,128)(2,1)S(1)}, bf16[128,1024]{1,0:T(8,128)(2,1)S(1)}, u32[]{:S(2)}, u32[]{:S(2)}) collective-permute-start(bf16[128,1024]{1,0:T(8,128)(2,1)S(1)} %slice.51), channel_id=1, source_target_pairs={{0,24},{8,0},{16,8},{24,16},{1,25},{9,1},{17,9},{25,17},{2,26},{10... | collective-permute-start | bytes 786440 | tf_op jit(solution)/shard_map/ppermute | solution.py:26
  61.7 10.7 %collective-permute-start.17 = (bf16[512,512]{1,0:T(8,128)(2,1)S(1)}, bf16[512,512]{1,0:T(8,128)(2,1)S(1)}, u32[]{:S(2)}, u32[]{:S(2)}) collective-permute-start(bf16[512,512]{1,0:T(8,128)(2,1)S(1)} %get-tuple-element.22), channel_id=1, source_target_pairs={{0,1},{1,0},{2,3},{3,2},{4,5},{5,4},{6,7},{7,6},{8,9},{9,8},{10,11... | collective-permute-start | bytes 1572872 | tf_op jit(solution)/shard_map/ppermute | solution.py:30
  69.9 5.5 %collective-permute-start.20 = (bf16[512,512]{1,0:T(8,128)(2,1)S(1)}, bf16[512,512]{1,0:T(8,128)(2,1)S(1)}, u32[]{:S(2)}, u32[]{:S(2)}) collective-permute-start(bf16[512,512]{1,0:T(8,128)(2,1)S(1)} %get-tuple-element.24), channel_id=1, source_target_pairs={{0,1},{1,0},{2,3},{3,2},{4,5},{5,4},{6,7},{7,6},{8,9},{9,8},{10,11... | collective-permute-start | bytes 1572872 | tf_op jit(solution)/shard_map/ppermute | solution.py:30
  70.0 5.6 %collective-permute-start.16 = (bf16[512,512]{1,0:T(8,128)(2,1)S(1)}, bf16[512,512]{1,0:T(8,128)(2,1)S(1)}, u32[]{:S(2)}, u32[]{:S(2)}) collective-permute-start(bf16[512,512]{1,0:T(8,128)(2,1)S(1)} %get-tuple-element.20), channel_id=1, source_target_pairs={{0,1},{1,0},{2,3},{3,2},{4,5},{5,4},{6,7},{7,6},{8,9},{9,8},{10,11... | collective-permute-start | bytes 1572872 | tf_op jit(solution)/shard_map/ppermute | solution.py:30
  72.1 13.1 %collective-permute-start.15 = (bf16[512,512]{1,0:T(8,128)(2,1)S(1)}, bf16[512,512]{1,0:T(8,128)(2,1)S(1)}, u32[]{:S(2)}, u32[]{:S(2)}) collective-permute-start(bf16[512,512]{1,0:T(8,128)(2,1)S(1)} %get-tuple-element.18), channel_id=1, source_target_pairs={{0,1},{1,0},{2,3},{3,2},{4,5},{5,4},{6,7},{7,6},{8,9},{9,8},{10,11... | collective-permute-start | bytes 1572872 | tf_op jit(solution)/shard_map/ppermute | solution.py:30
  72.6 8.1 %collective-permute-start.21 = (bf16[256,512]{1,0:T(8,128)(2,1)S(1)}, bf16[256,512]{1,0:T(8,128)(2,1)S(1)}, u32[]{:S(2)}, u32[]{:S(2)}) collective-permute-start(bf16[256,512]{1,0:T(8,128)(2,1)S(1)} %get-tuple-element.28), channel_id=1, source_target_pairs={{0,6},{2,0},{4,2},{6,4},{1,7},{3,1},{5,3},{7,5},{8,14},{10,8},{12,... | collective-permute-start | bytes 786440 | tf_op jit(solution)/shard_map/ppermute | solution.py:26
  75.8 8.5 %collective-permute-start.18 = (bf16[256,512]{1,0:T(8,128)(2,1)S(1)}, bf16[256,512]{1,0:T(8,128)(2,1)S(1)}, u32[]{:S(2)}, u32[]{:S(2)}) collective-permute-start(bf16[256,512]{1,0:T(8,128)(2,1)S(1)} %get-tuple-element.27), channel_id=1, source_target_pairs={{0,2},{2,4},{4,6},{6,0},{1,3},{3,5},{5,7},{7,1},{8,10},{10,12},{12... | collective-permute-start | bytes 786440 | tf_op jit(solution)/shard_map/ppermute | solution.py:26
  80.8 13.4 %collective-permute-start.22 = (bf16[512,512]{1,0:T(8,128)(2,1)S(1)}, bf16[512,512]{1,0:T(8,128)(2,1)S(1)}, u32[]{:S(2)}, u32[]{:S(2)}) collective-permute-start(bf16[512,512]{1,0:T(8,128)(2,1)S(1)} %pad_maximum_fusion.1), channel_id=1, source_target_pairs={{0,6},{2,0},{4,2},{6,4},{1,7},{3,1},{5,3},{7,5},{8,14},{10,8},{12,... | collective-permute-start | bytes 1572872 | tf_op jit(solution)/shard_map/ppermute | solution.py:26
  85.2 13.3 %collective-permute-start.19 = (bf16[512,512]{1,0:T(8,128)(2,1)}, bf16[512,512]{1,0:T(8,128)(2,1)S(1)}, u32[]{:S(2)}, u32[]{:S(2)}) collective-permute-start(bf16[512,512]{1,0:T(8,128)(2,1)} %pad_maximum_fusion), channel_id=1, source_target_pairs={{0,2},{2,4},{4,6},{6,0},{1,3},{3,5},{5,7},{7,1},{8,10},{10,12},{12... | collective-permute-start | bytes 1572872 | tf_op jit(solution)/shard_map/ppermute | solution.py:26
  98.8 11.6 %collective-permute-start.24 = (bf16[256,512]{1,0:T(8,128)(2,1)S(1)}, bf16[256,512]{1,0:T(8,128)(2,1)S(1)}, u32[]{:S(2)}, u32[]{:S(2)}) collective-permute-start(bf16[256,512]{1,0:T(8,128)(2,1)S(1)} %get-tuple-element.26), channel_id=1, source_target_pairs={{0,8},{1,24},{8,0},{9,16},{16,9},{17,25},{24,1},{25,17},{2,10},{3,... | collective-permute-start | bytes 786440 | tf_op jit(solution)/shard_map/ppermute | solution.py:291
  104.3 9.2 %collective-permute-start.23 = (bf16[256,512]{1,0:T(8,128)(2,1)S(1)}, bf16[256,512]{1,0:T(8,128)(2,1)S(1)}, u32[]{:S(2)}, u32[]{:S(2)}) collective-permute-start(bf16[256,512]{1,0:T(8,128)(2,1)S(1)} %get-tuple-element.25), channel_id=1, source_target_pairs={{0,0},{1,16},{8,8},{9,24},{16,1},{17,17},{24,9},{25,25},{2,2},{3,1... | collective-permute-start | bytes 786440 | tf_op jit(solution)/shard_map/ppermute | solution.py:290

commit v2 on v0

v2 whole, which is shorter than its diff:
```python
import functools
import math

import jax
import jax.numpy as jnp
from jax import lax
from jax.experimental import pallas as pl
from jax.experimental.pallas import tpu as pltpu
from jax.sharding import Mesh
from jax.sharding import PartitionSpec as P

DH = 128
RUN = 64
SIZES = (256, 512, 768, 1024, 1152, 1536, 2304)
NEGATIVE = -1e30
Z = ("zh", "zl")


def z_index():
    return lax.axis_index("zh") * 2 + lax.axis_index("zl")


def shift(value, axis, step):
    return lax.ppermute(value, axis, [(i, (i + step) % 4) for i in range(4)])


def swap_cores(value):
    return lax.ppermute(value, "c", [(0, 1), (1, 0)])


def plus(first, second):
    return (first.astype(jnp.float32) + second.astype(jnp.float32)).astype(jnp.bfloat16)


SMEM = pl.BlockSpec(memory_space=pltpu.SMEM)
VMEM = pl.BlockSpec(memory_space=pltpu.VMEM)


def place_kernel(held, pos, *refs):
    blocks, outs = refs[: len(held)], refs[-2:]
    z, x = z_index(), lax.axis_index("x")
    for ref, items in zip(blocks, held):
        rows = ref.shape[0] // len(items)
        runs = rows // RUN
        for n, (dz, dx, which) in enumerate(items):
            group = lax.rem(z + dz, 4) * 4 + lax.rem(x + dx, 4)
            for i in range(runs):
                at = pl.multiple_of(pos[group * runs + i], RUN)
                row = n * rows + i * RUN
                outs[which][pl.ds(at, RUN), :] = ref[row : row + RUN, :]


def place(positions, held, blocks, ordered=None):
    shape = jax.ShapeDtypeStruct((positions.shape[0] * RUN, DH), jnp.bfloat16)
    old = list(ordered or ())
    at = 1 + len(blocks)
    return pl.pallas_call(
        functools.partial(place_kernel, held),
        out_shape=[shape, shape],
        in_specs=[SMEM] + [VMEM] * (len(blocks) + len(old)),
        out_specs=[VMEM, VMEM],
        input_output_aliases={at: 0, at + 1: 1} if old else {},
        compiler_params=pltpu.CompilerParams(vmem_limit_bytes=8 * 2**20),
        cost_estimate=pl.CostEstimate(flops=0, bytes_accessed=2 * 2**20, transcendentals=0),
        name="place",
    )(positions, *blocks, *old)


def attend_kernel(first_row, pos, lengths, spans, q, ks, vs, out):
    z, x = z_index(), lax.axis_index("x")
    heads, slots = out.shape[1] // DH, ks.shape[0]
    runs = out.shape[0] // RUN

    ends = []
    for d in range(lengths.shape[0]):
        ends.append(lengths[d] + (ends[-1] if ends else 0))
    starts = [0] + ends[:-1]
    span_list = [(spans[0, k], spans[1, k]) for k in range(spans.shape[1])]

    def interval(at):
        low = jnp.zeros_like(at)
        end = jnp.zeros_like(at)
        for first, last in zip(starts, ends):
            inside = (at >= first) & (at < last)
            low = jnp.where(inside, first, low)
            end = jnp.where(inside, last, end)
        high = at + 1
        for first, last in span_list:
            inside = (at >= first) & (at < last)
            high = jnp.where(inside, jnp.maximum(high, jnp.minimum(last, end)), high)
        return low, high

    scale = math.log2(math.e) / math.sqrt(DH)
    first_run = (z * 4 + x) * (q.shape[0] // RUN) + first_row // RUN

    def block(i, _):
        p0 = pos[first_run + i]
        row = pl.multiple_of(i * RUN, RUN)
        low, high = interval(p0 + lax.broadcasted_iota(jnp.int32, (RUN, DH), 0))
        width = high - low
        lanes = lax.broadcasted_iota(jnp.int32, (RUN, DH), 1) - low
        first_low, _ = interval(p0)
        _, last_high = interval(p0 + RUN - 1)
        base = first_low // RUN * RUN
        need = last_high - base

        def work(size, groups):
            start = pl.multiple_of(jnp.minimum(base, slots - size), RUN)
            allowed = []
            for n in range(size // DH):
                t = lanes + (start + n * DH)
                allowed.append((t >= 0) & (t < width))
            per = heads // groups
            for g in range(groups):
                columns = [(g * per + h) * DH for h in range(per)]
                queries = jnp.concatenate(
                    [q[pl.ds(first_row + row, RUN), c : c + DH] for c in columns], axis=0
                )
                s = lax.dot_general(
                    queries,
                    ks[pl.ds(start, size), :],
                    (((1,), (1,)), ((), ())),
                    preferred_element_type=jnp.float32,
                )
                parts = [
                    jnp.where(
                        allowed[n][None], s[:, n * DH : (n + 1) * DH].reshape(per, RUN, DH), NEGATIVE
                    ).reshape(per * RUN, DH)
                    for n in range(size // DH)
                ]
                top = jnp.max(functools.reduce(jnp.maximum, parts), axis=1, keepdims=True)
                expo = [jnp.exp2((part - top) * scale) for part in parts]
                total = jnp.sum(functools.reduce(jnp.add, expo), axis=1, keepdims=True)
                weights = jnp.concatenate([e.astype(jnp.bfloat16) for e in expo], axis=1)
                mixed = jnp.dot(weights, vs[pl.ds(start, size), :], preferred_element_type=jnp.float32)
                mixed = (mixed / total).astype(jnp.bfloat16)
                for h, c in enumerate(columns):
                    out[pl.ds(row, RUN), c : c + DH] = mixed[h * RUN : (h + 1) * RUN]

        below = 0
        for size in SIZES:

            @pl.when((need > below) & (need <= size))
            def _():
                work(size, 2 if size <= 1152 else 4)

            below = size
        return 0

    lax.fori_loop(0, runs, block, 0)


def attend(first_row, rows, positions, lengths, spans, q, ordered):
    width = q.shape[1]
    return pl.pallas_call(
        functools.partial(attend_kernel, first_row),
        out_shape=jax.ShapeDtypeStruct((rows, width), jnp.bfloat16),
        in_specs=[SMEM] * 3 + [VMEM] * 3,
        out_specs=VMEM,
        compiler_params=pltpu.CompilerParams(vmem_limit_bytes=16 * 2**20),
        cost_estimate=pl.CostEstimate(
            flops=4 * rows * 1024 * width, bytes_accessed=4 * 2**20, transcendentals=rows * 8 * width
        ),
        name="attend",
    )(positions, lengths, spans, q, *ordered)


def join_kernel(ranges, *refs):
    row = 0
    for ref, (first, last) in zip(refs, ranges):
        refs[-1][row : row + last - first, :] = ref[first:last, :]
        row += last - first


def join(pieces, ranges):
    rows = sum(last - first for first, last in ranges)
    return pl.pallas_call(
        functools.partial(join_kernel, ranges),
        out_shape=jax.ShapeDtypeStruct((rows, pieces[0].shape[1]), pieces[0].dtype),
        in_specs=[VMEM] * len(pieces),
        out_specs=VMEM,
        compiler_params=pltpu.CompilerParams(vmem_limit_bytes=4 * 2**20),
        cost_estimate=pl.CostEstimate(flops=0, bytes_accessed=2**20, transcendentals=0),
        name="join",
    )(*pieces)


def project_kernel(core_zero, core_one, *refs):
    pieces = refs[: len(core_zero) + len(core_one)]
    weights = refs[len(pieces) : -3]
    keep, send, rows = refs[-3:]
    core = lax.axis_index("c")
    for mine, names in ((core, core_zero), (1 - core, core_one)):
        at = 0
        for n in names:
            rows[mine, at : at + pieces[n].shape[0], :] = pieces[n][...]
            at += pieces[n].shape[0]
    for target, which in ((send, 1), (keep, 0)):
        for n, parts in enumerate(BLOCKS):
            total, at = None, 0
            for part in parts:
                depth = weights[part].shape[0]
                share = jnp.dot(rows[which, :, at : at + depth], weights[part][...], preferred_element_type=jnp.float32)
                total = share if total is None else total + share
                at += depth
            target[n] = total.astype(jnp.bfloat16)


BLOCKS = ((0,), (1,), (2,), (3, 4))


def project(pieces, core_zero, core_one, weights):
    count, depth = sum(pieces[n].shape[0] for n in core_zero), pieces[0].shape[1]
    width = weights[0].shape[1]
    result = jax.ShapeDtypeStruct((len(BLOCKS), count, width), jnp.bfloat16)
    return pl.pallas_call(
        functools.partial(project_kernel, core_zero, core_one),
        out_shape=[result, result],
        in_specs=[VMEM] * (len(pieces) + len(weights)),
        out_specs=[VMEM, VMEM],
        scratch_shapes=[pltpu.VMEM((2, count, depth), jnp.bfloat16)],
        compiler_params=pltpu.CompilerParams(vmem_limit_bytes=16 * 2**20),
        cost_estimate=pl.CostEstimate(
            flops=4 * count * depth * width * len(BLOCKS), bytes_accessed=4 * 2**20, transcendentals=0
        ),
        name="project",
    )(*pieces, *weights)


def combine_kernel(keep, got, *refs):
    outs, stack = refs[:-1], refs[-1]
    z, y, core = z_index(), lax.axis_index("y"), lax.axis_index("c")
    for block, away in enumerate((0, 3, 1, 2)):
        ahead = lax.rem(away + z - y + 4, 4)
        turn = lax.rem(jnp.where(core == 0, 3 - ahead, ahead + 3), 4)
        stack[turn] = plus(keep[block], got[block])
    for n, out in enumerate(outs):
        out[...] = stack[n]


def combine(keep, got):
    _, rows, width = keep.shape
    result = jax.ShapeDtypeStruct((rows, width), jnp.bfloat16)
    return pl.pallas_call(
        combine_kernel,
        out_shape=[result] * 4,
        in_specs=[VMEM] * 2,
        out_specs=[VMEM] * 4,
        scratch_shapes=[pltpu.VMEM(keep.shape, jnp.bfloat16)],
        compiler_params=pltpu.CompilerParams(vmem_limit_bytes=8 * 2**20),
        cost_estimate=pl.CostEstimate(flops=0, bytes_accessed=3 * 2**20, transcendentals=0),
        name="combine",
    )(keep, got)


def relay(value, axis):
    pairs = [(2 * i + c, 2 * ((i + 1 - 2 * c) % 4) + c) for i in range(4) for c in range(2)]
    return lax.ppermute(value, (axis, "c"), pairs)


def home(value, away, turn):
    pairs = []
    for x in range(4):
        for y in range(4):
            for c in range(2):
                to_y = (y + (1 - 2 * c) * turn) % 4
                pairs.append(((x * 4 + y) * 2 + c, (((x + away[c]) % 4) * 4 + to_y) * 2 + x // 2))
    return lax.ppermute(value, ("x", "y", "c"), pairs)


def sum_shares(turns, away):
    stay = home(turns[3], away, 0)
    passed = relay(turns[0], "y")
    passed = relay(plus(turns[1], passed), "y")
    return stay, home(plus(turns[2], passed), away, 1)


def after(value, *others):
    return lax.optimization_barrier((value, *others))[0]


def shards(queries, keys, values, positions, lengths, spans, weight):
    x = lax.axis_index("x")
    count = keys.shape[0]
    kv = jnp.concatenate([keys, values], axis=0)
    line = [shift(kv, Z, 1), shift(kv, Z, -1), shift(kv, Z, 2)]
    left, right = shift(kv, "x", 1), shift(kv, "x", -1)
    line = jnp.concatenate(line, axis=0)
    line, weight, left, right = lax.optimization_barrier((line, weight, left, right))
    line_left, line_right = shift(line, "x", 1), shift(line, "x", -1)
    weight_left, weight_right = shift(weight, Z, 1), shift(weight, Z, -1)

    runs = positions.reshape(-1, RUN)[:, 0]
    line_blocks = [(dz, which) for dz in (3, 1, 2) for which in (0, 1)]

    def at_x(dx, blocks=line_blocks):
        return [(dz, dx, which) for dz, which in blocks]

    own = [(0, 0), (0, 1)]
    ordered = place(runs, (at_x(0, own), at_x(0), at_x(3, own), at_x(1, own)), (kv, line, left, right))
    left2 = shift(join((line_left, left), ((0, 3 * count), (0, count))), "x", 1)
    right2 = shift(join((line_right, right), ((3 * count, 6 * count), (count, 2 * count))), "x", -1)
    ordered = place(runs, (at_x(3), at_x(1)), (line_left, line_right), ordered)
    ordered = place(
        runs,
        (at_x(2, line_blocks[:3] + own[:1]), at_x(2, line_blocks[3:] + own[1:])),
        (left2, right2),
        ordered,
    )

    half = count // 2
    upper = attend(0, half, runs, lengths, spans, queries, ordered)
    lower = attend(half, half, runs, lengths, spans, after(queries, upper), ordered)
    upper_left, upper_right = shift(upper, "x", 1), shift(upper, "x", -1)
    lower_left, lower_right = shift(lower, "x", 1), shift(lower, "x", -1)

    middle = weight.shape[0] // 2
    weight_left_far = shift(join((after(weight_left, lower),), ((0, middle),)), Z, 1)
    weight_right_far = shift(join((after(weight_right, lower),), ((middle, 2 * middle),)), Z, -1)
    upper_far, lower_far = shift(upper_left, "x", 1), shift(lower_right, "x", -1)

    weights = (weight, weight_left, weight_right, weight_left_far, weight_right_far)
    rows = (upper_left, lower_left, upper_right, lower_right)
    keep, send = project(rows, (0, 1), (2, 3), weights)
    near = combine(keep, swap_cores(send))
    rows = (upper, lower, after(upper_far, near[0]), lower_far)
    keep, send = project(rows, (0, 1), (2, 3), weights)
    mixed = combine(keep, swap_cores(send))

    near = plus(*sum_shares(near, (-1, 1)))
    mixed = plus(*sum_shares(mixed, (0, 2)))
    return jnp.where(
        lax.rem(x, 2) == 0,
        jnp.concatenate([mixed, near], axis=1),
        jnp.concatenate([near, mixed], axis=1),
    )


def solution(mesh):
    fine = Mesh(mesh.devices.reshape(2, 2, 4, 4, 2), ("zh", "zl", "x", "y", "c"))
    rows, columns = ("zh", "zl", "x"), ("y", "c")
    return jax.shard_map(
        shards,
        mesh=fine,
        in_specs=(P(rows, columns), P(rows, columns), P(rows, columns), P(), P(), P(), P(columns, rows)),
        out_specs=P(rows, columns),
        check_vma=False,
    )
```

time: 278 us -> 107 us (0.38)
  waiting for transfers between devices: 164 us -> 50.6 us
  matrix products: 71.7 us -> 0 us
  starting transfers between devices: 0.12 us -> 35.4 us
  Pallas kernels: 0 us -> 15 us
  between operations: 13.2 us -> 0.3 us
  local copies, waits for them, and re-layouts: 15.6 us -> 4 us
  other arithmetic: 12 us -> 1.36 us
    all_gather x3 -> x0, waiting for transfers between devices: 125 us -> none  [the longest x1 44.3 us: shards(): value_part = lax.all_gather(values, ('outer', 'inner'), axis=0, tiled=True)]
    dot_general x17 -> x0, matrix products: 71.7 us -> none  [the longest x8 30.7 us: update(): jnp.einsum('gjqk,kgd->gjqd', expo.astype(jnp.bfloat16), value_grid, prefe...]
    ppermute x0 -> x29, waiting for transfers between devices: none -> 50.6 us  [the longest x19 30.8 us: shift(): return lax.ppermute(value, axis, [(i, (i + step) % 4) for i in range(4)])]
    reduce_scatter x1 -> x0, waiting for transfers between devices: 37.5 us -> none  [shards(): lax.psum_scatter(partial_out.astype(jnp.bfloat16), 'tensor', scatter_dime...]
    ppermute x0 -> x29, starting transfers between devices: none -> 35.4 us  [the longest x19 24.5 us: shift(): return lax.ppermute(value, axis, [(i, (i + step) % 4) for i in range(4)])]
    pallas_call x0 -> x13, Pallas kernels: none -> 15 us  [the longest x2 5.17 us: attend(): pl.pallas_call(functools.partial(attend_kernel, first_row), out_shape=jax...]
    reduce_sum x26 -> x0, other arithmetic: 8.62 us -> none  [the longest x8 7.06 us: update(): new_total = running_total * shrink + jnp.sum(expo, axis=-1)]
    dynamic_slice x9 -> x0, local copies, waits for them, and re-layouts: 6.89 us -> none  [the longest x8 6.12 us: attend(): places = lax.dynamic_slice_in_dim(positions, block_start, size)]
  transfers between devices with their start and end apart: 4 -> 29, of which waited for: 4 -> 18; matrix products, arithmetic and copies ran while one was open for 31% -> 2% of each run, Pallas kernels for 0% -> 10%
where the time goes in v2:
time: 107 us
  waiting for transfers between devices  50.6 us (47%)
  starting transfers between devices  35.4 us (33%)
  Pallas kernels  15 us (14%)
  local copies, waits for them, and re-layouts  4 us (4%)
  other arithmetic  1.36 us (1%)
    ppermute x19, waiting for transfers between devices, shift(): return lax.ppermute(value, axis, [(i, (i + step) % 4) for i in range(4)])  30.8 us
    ppermute x19, starting transfers between devices, shift(): return lax.ppermute(value, axis, [(i, (i + step) % 4) for i in range(4)])  24.5 us
    ppermute x4, waiting for transfers between devices, home(): return lax.ppermute(value, ('x', 'y', 'c'), pairs)  9.73 us
    ppermute x4, waiting for transfers between devices, relay(): return lax.ppermute(value, (axis, 'c'), pairs)  8.57 us
    ppermute x4, starting transfers between devices, home(): return lax.ppermute(value, ('x', 'y', 'c'), pairs)  6.54 us
    pallas_call x2, Pallas kernels, attend(): pl.pallas_call(functools.partial(attend_kernel, first_row), out_shape=jax...  5.17 us
    pallas_call x2, Pallas kernels, project(): pl.pallas_call(functools.partial(project_kernel, core_zero, core_one), ou...  4.74 us
    ppermute x4, starting transfers between devices, relay(): return lax.ppermute(value, (axis, 'c'), pairs)  4.16 us
  transfers between devices with their start and end apart: 29, of which 18 were waited for; matrix products, arithmetic and copies ran while one was open for 2% of the time, Pallas kernels for 10%

profile of v2, /device:TPU:6, one launch (start us, length us, event | category | flops | bytes accessed | tf_op | source)
XLA Modules:
  0.0 106.7 jit_solution(7491956713596036769)
XLA Ops:
  0.0 0.9 constant_dynamic-update-slice_fusion.1
  0.9 4.0 %collective-permute-start.2 = (bf16[512,128]{1,0:T(8,128)(2,1)S(1)}, bf16[512,128]{1,0:T(8,128)(2,1)S(1)}, u32[]{:S(2)}, u32[]{:S(2)}) collective-permute-start(bf16[512,128]{1,0:T(8,128)(2,1)S(1)} %constant_dynamic-update-slice_fusion.refs_0_), channel_id=1, source_target_pairs={{0,64},{32,96},{64,0},{96,32},{1,65},{33,97},{65,1},{97,33},{2,66}... | collective-permute-start | bytes 393224 | tf_op jit(solution)/shard_map/ppermute | solution.py:24
  4.9 0.7 collective-permute-start.1
  5.6 1.3 %collective-permute-start = (bf16[512,128]{1,0:T(8,128)(2,1)S(1)}, bf16[512,128]{1,0:T(8,128)(2,1)S(1)}, u32[]{:S(2)}, u32[]{:S(2)}) collective-permute-start(bf16[512,128]{1,0:T(8,128)(2,1)S(1)} %constant_dynamic-update-slice_fusion.refs_0_), channel_id=1, source_target_pairs={{0,32},{32,64},{64,96},{96,0},{1,33},{33,65},{65,97},{97,1},{2,34}... | collective-permute-start | bytes 393224 | tf_op jit(solution)/shard_map/ppermute | solution.py:24
  7.4 1.5 %collective-permute-start.4 = (bf16[512,128]{1,0:T(8,128)(2,1)S(1)}, bf16[512,128]{1,0:T(8,128)(2,1)S(1)}, u32[]{:S(2)}, u32[]{:S(2)}) collective-permute-start(bf16[512,128]{1,0:T(8,128)(2,1)S(1)} %constant_dynamic-update-slice_fusion.refs_0_), channel_id=1, source_target_pairs={{0,24},{8,0},{16,8},{24,16},{1,25},{9,1},{17,9},{25,17},{2,26},{10... | collective-permute-start | bytes 393224 | tf_op jit(solution)/shard_map/ppermute | solution.py:24
  8.9 3.0 %collective-permute-done.1 = bf16[512,128]{1,0:T(8,128)(2,1)S(1)} collective-permute-done((bf16[512,128]{1,0:T(8,128)(2,1)S(1)}, bf16[512,128]{1,0:T(8,128)(2,1)S(1)}, u32[]{:S(2)}, u32[]{:S(2)}) %collective-permute-start.1) | collective-permute-done | bytes 131104 | tf_op jit(solution)/shard_map/ppermute | solution.py:24
  12.0 1.5 %collective-permute-done.4.refs_1_.refs_3_ = bf16[512,128]{1,0:T(8,128)(2,1)S(1)} collective-permute-done((bf16[512,128]{1,0:T(8,128)(2,1)S(1)}, bf16[512,128]{1,0:T(8,128)(2,1)S(1)}, u32[]{:S(2)}, u32[]{:S(2)}) %collective-permute-start.4) | collective-permute-done | bytes 131104 | tf_op jit(solution)/shard_map/ppermute | solution.py:24
  13.5 1.0 collective-permute-start.14
  14.6 2.2 %collective-permute-start.15 = (bf16[1024,512]{1,0:T(8,128)(2,1)}, bf16[1024,512]{1,0:T(8,128)(2,1)S(1)}, u32[]{:S(2)}, u32[]{:S(2)}) collective-permute-start(bf16[1024,512]{1,0:T(8,128)(2,1)} %refs_4_.1), channel_id=1, source_target_pairs={{0,96},{32,0},{64,32},{96,64},{1,97},{33,1},{65,33},{97,65},{2,98}... | collective-permute-start | bytes 3145736 | tf_op jit(solution)/shard_map/ppermute | solution.py:24
  17.1 1.7 %collective-permute-start.7 = (bf16[1536,128]{1,0:T(8,128)(2,1)S(1)}, bf16[1536,128]{1,0:T(8,128)(2,1)S(1)}, u32[]{:S(2)}, u32[]{:S(2)}) collective-permute-start(bf16[1536,128]{1,0:T(8,128)(2,1)S(1)} %pad_maximum_fusion.refs_1_), channel_id=1, source_target_pairs={{0,24},{8,0},{16,8},{24,16},{1,25},{9,1},{17,9},{25,17},{2,26},{10... | collective-permute-start | bytes 1179656 | tf_op jit(solution)/shard_map/ppermute | solution.py:24
  18.8 6.7 %collective-permute-done.5.refs_0_ = bf16[1536,128]{1,0:T(8,128)(2,1)S(1)} collective-permute-done((bf16[1536,128]{1,0:T(8,128)(2,1)S(1)}, bf16[1536,128]{1,0:T(8,128)(2,1)S(1)}, u32[]{:S(2)}, u32[]{:S(2)}) %collective-permute-start.5) | collective-permute-done | bytes 393248 | tf_op jit(solution)/shard_map/ppermute | solution.py:24
  25.5 0.7 join.4
  26.2 1.7 %collective-permute-start.6 = (bf16[1024,128]{1,0:T(8,128)(2,1)}, bf16[1024,128]{1,0:T(8,128)(2,1)}, u32[]{:S(2)}, u32[]{:S(2)}) collective-permute-start(bf16[1024,128]{1,0:T(8,128)(2,1)} %join.4), channel_id=1, source_target_pairs={{0,8},{8,16},{16,24},{24,0},{1,9},{9,17},{17,25},{25,1},{2,10},{10... | collective-permute-start | bytes 786440 | tf_op jit(solution)/shard_map/ppermute | solution.py:24
  27.9 0.7 join.5
  29.0 0.7 reshape.3
  29.7 0.9 slice_reduce_fusion.pos
  30.5 0.9 copy-done.2
  31.4 0.7 place.3
  32.1 0.7 place.4
  32.9 3.6 %collective-permute-done.8.refs_1_ = bf16[1024,128]{1,0:T(8,128)(2,1)} collective-permute-done((bf16[1024,128]{1,0:T(8,128)(2,1)}, bf16[1024,128]{1,0:T(8,128)(2,1)}, u32[]{:S(2)}, u32[]{:S(2)}) %collective-permute-start.8) | collective-permute-done | bytes 262176 | tf_op jit(solution)/shard_map/ppermute | solution.py:24
  36.5 1.2 %place.5 = (bf16[4096,128]{1,0:T(8,128)(2,1)S(1)}, bf16[4096,128]{1,0:T(8,128)(2,1)S(1)}) custom-call(s32[64]{0:T(128)S(1)} %slice_reduce_fusion.pos, bf16[1024,128]{1,0:T(8,128)(2,1)} %collective-permute-done.6.refs_0_, bf16[1024,128]{1,0:T(8,128)(2,1)} %collective-permute-done.8.refs_1_, ...), custom_call_target="tpu_custom_call", output_to_operand_aliasing={{0}: (3, {}), {1}: (4, {})} | custom-call | bytes 2097152 | tf_op jit(solution)/shard_map/place/pallas_call | solution.py:57
  37.8 0.6 copy-done.3
  38.4 2.3 %attend.2.refs_0_ = bf16[128,1024]{1,0:T(8,128)(2,1)S(1)} custom-call(s32[64]{0:T(128)S(1)} %slice_reduce_fusion.pos, s32[8]{0:T(128)S(1)} %copy-done.4, s32[2,4]{1,0:T(2,128)S(1)} %copy-done.3, bf16[256,1024]{1,0:T(8,128)(2,1)S(1)} %copy-done, bf16[4096,128]{1,0:T(8,128)(2,1)S(1)} %get-tuple-element.38.ks, bf16[4096,128]{1,0:T(8,128)(2,1)S(1)} %get-tuple-element.39.vs), custom_call_target="tpu_custom_call" | custom-call | flops 536870912 | bytes 4194304 | tf_op jit(solution)/shard_map/attend/pallas_call | solution.py:155
  41.0 2.9 %attend.3.refs_1_ = bf16[128,1024]{1,0:T(8,128)(2,1)S(1)} custom-call(s32[64]{0:T(128)S(1)} %slice_reduce_fusion.pos, s32[8]{0:T(128)S(1)} %copy-done.4, s32[2,4]{1,0:T(2,128)S(1)} %copy-done.3, bf16[256,1024]{1,0:T(8,128)(2,1)S(1)} %copy-done, bf16[4096,128]{1,0:T(8,128)(2,1)S(1)} %get-tuple-element.38.ks, bf16[4096,128]{1,0:T(8,128)(2,1)S(1)} %get-tuple-element.39.vs), custom_call_target="tpu_custom_call" | custom-call | flops 536870912 | bytes 4194304 | tf_op jit(solution)/shard_map/attend/pallas_call | solution.py:155
  44.1 3.3 %collective-permute-start.17 = (bf16[512,512]{1,0:T(8,128)(2,1)S(1)}, bf16[512,512]{1,0:T(8,128)(2,1)S(1)}, u32[]{:S(2)}, u32[]{:S(2)}) collective-permute-start(bf16[512,512]{1,0:T(8,128)(2,1)S(1)} %join.7), channel_id=1, source_target_pairs={{0,96},{32,0},{64,32},{96,64},{1,97},{33,1},{65,33},{97,65},{2,98}... | collective-permute-start | bytes 1572872 | tf_op jit(solution)/shard_map/ppermute | solution.py:24
  47.4 2.0 %collective-permute-start.11 = (bf16[128,1024]{1,0:T(8,128)(2,1)S(1)}, bf16[128,1024]{1,0:T(8,128)(2,1)S(1)}, u32[]{:S(2)}, u32[]{:S(2)}) collective-permute-start(bf16[128,1024]{1,0:T(8,128)(2,1)S(1)} %attend.3.refs_1_), channel_id=1, source_target_pairs={{0,8},{8,16},{16,24},{24,0},{1,9},{9,17},{17,25},{25,1},{2,10},{10... | collective-permute-start | bytes 786440 | tf_op jit(solution)/shard_map/ppermute | solution.py:24
  49.6 1.5 %collective-permute-start.13 = (bf16[128,1024]{1,0:T(8,128)(2,1)S(1)}, bf16[128,1024]{1,0:T(8,128)(2,1)S(1)}, u32[]{:S(2)}, u32[]{:S(2)}) collective-permute-start(bf16[128,1024]{1,0:T(8,128)(2,1)S(1)} %attend.3.refs_1_), channel_id=1, source_target_pairs={{0,24},{8,0},{16,8},{24,16},{1,25},{9,1},{17,9},{25,17},{2,26},{10... | collective-permute-start | bytes 786440 | tf_op jit(solution)/shard_map/ppermute | solution.py:24
  51.1 2.7 %collective-permute-done.11.refs_1_ = bf16[128,1024]{1,0:T(8,128)(2,1)S(1)} collective-permute-done((bf16[128,1024]{1,0:T(8,128)(2,1)S(1)}, bf16[128,1024]{1,0:T(8,128)(2,1)S(1)}, u32[]{:S(2)}, u32[]{:S(2)}) %collective-permute-start.11) | collective-permute-done | bytes 262176 | tf_op jit(solution)/shard_map/ppermute | solution.py:24
  53.8 3.3 %collective-permute-done.12.refs_2_ = bf16[128,1024]{1,0:T(8,128)(2,1)S(1)} collective-permute-done((bf16[128,1024]{1,0:T(8,128)(2,1)S(1)}, bf16[128,1024]{1,0:T(8,128)(2,1)S(1)}, u32[]{:S(2)}, u32[]{:S(2)}) %collective-permute-start.12) | collective-permute-done | bytes 262176 | tf_op jit(solution)/shard_map/ppermute | solution.py:24
  57.1 2.8 %collective-permute-done.13.refs_3_ = bf16[128,1024]{1,0:T(8,128)(2,1)S(1)} collective-permute-done((bf16[128,1024]{1,0:T(8,128)(2,1)S(1)}, bf16[128,1024]{1,0:T(8,128)(2,1)S(1)}, u32[]{:S(2)}, u32[]{:S(2)}) %collective-permute-start.13) | collective-permute-done | bytes 262176 | tf_op jit(solution)/shard_map/ppermute | solution.py:24
  59.9 2.4 %project.2 = (bf16[4,256,512]{2,1,0:T(8,128)(2,1)S(1)}, bf16[4,256,512]{2,1,0:T(8,128)(2,1)S(1)}) custom-call(bf16[128,1024]{1,0:T(8,128)(2,1)S(1)} %collective-permute-done.9.refs_0_, bf16[128,1024]{1,0:T(8,128)(2,1)S(1)} %collective-permute-done.11.refs_1_, bf16[128,1024]{1,0:T(8,128)(2,1)S(1)} %collective-permute-done.12.refs_2_, ...), custom_call_target="tpu_custom_call" | custom-call | flops 2147483648 | bytes 4194304 | tf_op jit(solution)/shard_map/project/pallas_call | solution.py:216
  62.4 2.0 %collective-permute-start.19 = (bf16[128,1024]{1,0:T(8,128)(2,1)S(1)}, bf16[128,1024]{1,0:T(8,128)(2,1)S(1)}, u32[]{:S(2)}, u32[]{:S(2)}) collective-permute-start(bf16[128,1024]{1,0:T(8,128)(2,1)S(1)} %collective-permute-done.13.refs_3_), channel_id=1, source_target_pairs={{0,24},{8,0},{16,8},{24,16},{1,25},{9,1},{17,9},{25,17},{2,26},{10... | collective-permute-start | bytes 786440 | tf_op jit(solution)/shard_map/ppermute | solution.py:24
  64.5 0.6 collective-permute-done.18.got
  65.5 5.6 %collective-permute-done.10.refs_2_ = bf16[128,1024]{1,0:T(8,128)(2,1)S(1)} collective-permute-done((bf16[128,1024]{1,0:T(8,128)(2,1)S(1)}, bf16[128,1024]{1,0:T(8,128)(2,1)S(1)}, u32[]{:S(2)}, u32[]{:S(2)}) %collective-permute-start.10) | collective-permute-done | bytes 262176 | tf_op jit(solution)/shard_map/ppermute | solution.py:24
  71.1 1.2 %collective-permute-done.19.refs_3_ = bf16[128,1024]{1,0:T(8,128)(2,1)S(1)} collective-permute-done((bf16[128,1024]{1,0:T(8,128)(2,1)S(1)}, bf16[128,1024]{1,0:T(8,128)(2,1)S(1)}, u32[]{:S(2)}, u32[]{:S(2)}) %collective-permute-start.19) | collective-permute-done | bytes 262176 | tf_op jit(solution)/shard_map/ppermute | solution.py:24
  72.3 2.4 %project.3 = (bf16[4,256,512]{2,1,0:T(8,128)(2,1)S(1)}, bf16[4,256,512]{2,1,0:T(8,128)(2,1)S(1)}) custom-call(bf16[128,1024]{1,0:T(8,128)(2,1)S(1)} %attend.2.refs_0_, bf16[128,1024]{1,0:T(8,128)(2,1)S(1)} %attend.3.refs_1_, bf16[128,1024]{1,0:T(8,128)(2,1)S(1)} %collective-permute-done.10.refs_2_, bf16[128,1024]{1,0:T(8,128)(2,1)S(1)} %collective-permute-done.19.refs_3_, ...), custom_call_target="tpu_custom_call" | custom-call | flops 2147483648 | bytes 4194304 | tf_op jit(solution)/shard_map/project/pallas_call | solution.py:216
  74.8 1.6 %collective-permute-start.26 = (bf16[256,512]{1,0:T(8,128)(2,1)S(1)}, bf16[256,512]{1,0:T(8,128)(2,1)S(1)}, u32[]{:S(2)}, u32[]{:S(2)}) collective-permute-start(bf16[256,512]{1,0:T(8,128)(2,1)S(1)} %get-tuple-element.46), channel_id=1, source_target_pairs={{0,2},{1,7},{2,4},{3,1},{4,6},{5,3},{6,0},{7,5},{8,10},{9,15},{10,... | collective-permute-start | bytes 786440 | tf_op jit(solution)/shard_map/ppermute | solution.py:258
  76.4 1.0 collective-permute-done.20.got
  77.9 1.6 %collective-permute-start.22 = (bf16[256,512]{1,0:T(8,128)(2,1)S(1)}, bf16[256,512]{1,0:T(8,128)(2,1)S(1)}, u32[]{:S(2)}, u32[]{:S(2)}) collective-permute-start(bf16[256,512]{1,0:T(8,128)(2,1)S(1)} %get-tuple-element.53), channel_id=1, source_target_pairs={{0,2},{1,7},{2,4},{3,1},{4,6},{5,3},{6,0},{7,5},{8,10},{9,15},{10,... | collective-permute-start | bytes 786440 | tf_op jit(solution)/shard_map/ppermute | solution.py:258
  79.6 2.8 %collective-permute-done.26 = bf16[256,512]{1,0:T(8,128)(2,1)S(1)} collective-permute-done((bf16[256,512]{1,0:T(8,128)(2,1)S(1)}, bf16[256,512]{1,0:T(8,128)(2,1)S(1)}, u32[]{:S(2)}, u32[]{:S(2)}) %collective-permute-start.26) | collective-permute-done | bytes 262176 | tf_op jit(solution)/shard_map/ppermute | solution.py:258
  82.9 2.7 %collective-permute-done.22 = bf16[256,512]{1,0:T(8,128)(2,1)S(1)} collective-permute-done((bf16[256,512]{1,0:T(8,128)(2,1)S(1)}, bf16[256,512]{1,0:T(8,128)(2,1)S(1)}, u32[]{:S(2)}, u32[]{:S(2)}) %collective-permute-start.22) | collective-permute-done | bytes 262176 | tf_op jit(solution)/shard_map/ppermute | solution.py:258
  86.1 1.5 %collective-permute-start.25 = (bf16[256,512]{1,0:T(8,128)(2,1)S(1)}, bf16[256,512]{1,0:T(8,128)(2,1)S(1)}, u32[]{:S(2)}, u32[]{:S(2)}) collective-permute-start(bf16[256,512]{1,0:T(8,128)(2,1)S(1)} %get-tuple-element.54), channel_id=1, source_target_pairs={{0,24},{1,8},{2,26},{3,10},{4,28},{5,12},{6,30},{7,14},{8,0},{9,16... | collective-permute-start | bytes 786440 | tf_op jit(solution)/shard_map/ppermute | solution.py:268
  87.6 2.5 %collective-permute-done.27 = bf16[256,512]{1,0:T(8,128)(2,1)S(1)} collective-permute-done((bf16[256,512]{1,0:T(8,128)(2,1)S(1)}, bf16[256,512]{1,0:T(8,128)(2,1)S(1)}, u32[]{:S(2)}, u32[]{:S(2)}) %collective-permute-start.27) | collective-permute-done | bytes 262176 | tf_op jit(solution)/shard_map/ppermute | solution.py:258
  90.3 2.5 %collective-permute-start.21 = (bf16[256,512]{1,0:T(8,128)(2,1)S(1)}, bf16[256,512]{1,0:T(8,128)(2,1)S(1)}, u32[]{:S(2)}, u32[]{:S(2)}) collective-permute-start(bf16[256,512]{1,0:T(8,128)(2,1)S(1)} %get-tuple-element.50), channel_id=1, source_target_pairs={{0,0},{1,16},{2,2},{3,18},{4,4},{5,20},{6,6},{7,22},{8,8},{9,24},{... | collective-permute-start | bytes 786440 | tf_op jit(solution)/shard_map/ppermute | solution.py:268
  92.8 0.5 collective-permute-done.23
  93.4 2.5 %collective-permute-start.24 = (bf16[256,512]{1,0:T(8,128)(2,1)S(1)}, bf16[256,512]{1,0:T(8,128)(2,1)S(1)}, u32[]{:S(2)}, u32[]{:S(2)}) collective-permute-start(bf16[256,512]{1,0:T(8,128)(2,1)S(1)} %add_convert_fusion.4), channel_id=1, source_target_pairs={{0,2},{1,22},{2,4},{3,16},{4,6},{5,18},{6,0},{7,20},{8,10},{9,30},... | collective-permute-start | bytes 786440 | tf_op jit(solution)/shard_map/ppermute | solution.py:268
  95.9 9.7 %collective-permute-done.28 = bf16[256,512]{1,0:T(8,128)(2,1)S(1)} collective-permute-done((bf16[256,512]{1,0:T(8,128)(2,1)S(1)}, bf16[256,512]{1,0:T(8,128)(2,1)S(1)}, u32[]{:S(2)}, u32[]{:S(2)}) %collective-permute-start.28) | collective-permute-done | bytes 262176 | tf_op jit(solution)/shard_map/ppermute | solution.py:268
  105.7 0.9 maximum_select_fusion
  (51 shorter events, 4.6 us)
Async XLA Ops:
  0.0 0.9 copy-start.6
  0.9 11.1 %copy-start.1 = (bf16[512,128]{1,0:T(8,128)(2,1)}, bf16[512,128]{1,0:T(8,128)(2,1)S(1)}, u32[]{:S(2)}) copy-start(bf16[512,128]{1,0:T(8,128)(2,1)S(1)} %constant_dynamic-update-slice_fusion.refs_0_) | copy-start | bytes 393220
  0.9 8.0 %collective-permute-start.2 = (bf16[512,128]{1,0:T(8,128)(2,1)S(1)}, bf16[512,128]{1,0:T(8,128)(2,1)S(1)}, u32[]{:S(2)}, u32[]{:S(2)}) collective-permute-start(bf16[512,128]{1,0:T(8,128)(2,1)S(1)} %constant_dynamic-update-slice_fusion.refs_0_), channel_id=1, source_target_pairs={{0,64},{32,96},{64,0},{96,32},{1,65},{33,97},{65,1},{97,33},{2,66}... | collective-permute-start | bytes 393224 | tf_op jit(solution)/shard_map/ppermute | solution.py:24
  4.9 7.1 %collective-permute-start.1 = (bf16[512,128]{1,0:T(8,128)(2,1)S(1)}, bf16[512,128]{1,0:T(8,128)(2,1)S(1)}, u32[]{:S(2)}, u32[]{:S(2)}) collective-permute-start(bf16[512,128]{1,0:T(8,128)(2,1)S(1)} %constant_dynamic-update-slice_fusion.refs_0_), channel_id=1, source_target_pairs={{0,96},{32,0},{64,32},{96,64},{1,97},{33,1},{65,33},{97,65},{2,98}... | collective-permute-start | bytes 393224 | tf_op jit(solution)/shard_map/ppermute | solution.py:24
  5.6 6.4 %collective-permute-start = (bf16[512,128]{1,0:T(8,128)(2,1)S(1)}, bf16[512,128]{1,0:T(8,128)(2,1)S(1)}, u32[]{:S(2)}, u32[]{:S(2)}) collective-permute-start(bf16[512,128]{1,0:T(8,128)(2,1)S(1)} %constant_dynamic-update-slice_fusion.refs_0_), channel_id=1, source_target_pairs={{0,32},{32,64},{64,96},{96,0},{1,33},{33,65},{65,97},{97,1},{2,34}... | collective-permute-start | bytes 393224 | tf_op jit(solution)/shard_map/ppermute | solution.py:24
  6.9 5.1 %collective-permute-start.3 = (bf16[512,128]{1,0:T(8,128)(2,1)S(1)}, bf16[512,128]{1,0:T(8,128)(2,1)S(1)}, u32[]{:S(2)}, u32[]{:S(2)}) collective-permute-start(bf16[512,128]{1,0:T(8,128)(2,1)S(1)} %constant_dynamic-update-slice_fusion.refs_0_), channel_id=1, source_target_pairs={{0,8},{8,16},{16,24},{24,0},{1,9},{9,17},{17,25},{25,1},{2,10},{10... | collective-permute-start | bytes 393224 | tf_op jit(solution)/shard_map/ppermute | solution.py:24
  7.4 6.2 %collective-permute-start.4 = (bf16[512,128]{1,0:T(8,128)(2,1)S(1)}, bf16[512,128]{1,0:T(8,128)(2,1)S(1)}, u32[]{:S(2)}, u32[]{:S(2)}) collective-permute-start(bf16[512,128]{1,0:T(8,128)(2,1)S(1)} %constant_dynamic-update-slice_fusion.refs_0_), channel_id=1, source_target_pairs={{0,24},{8,0},{16,8},{24,16},{1,25},{9,1},{17,9},{25,17},{2,26},{10... | collective-permute-start | bytes 393224 | tf_op jit(solution)/shard_map/ppermute | solution.py:24
  13.5 30.4 %collective-permute-start.14 = (bf16[1024,512]{1,0:T(8,128)(2,1)}, bf16[1024,512]{1,0:T(8,128)(2,1)S(1)}, u32[]{:S(2)}, u32[]{:S(2)}) collective-permute-start(bf16[1024,512]{1,0:T(8,128)(2,1)} %refs_4_.1), channel_id=1, source_target_pairs={{0,32},{32,64},{64,96},{96,0},{1,33},{33,65},{65,97},{97,1},{2,34}... | collective-permute-start | bytes 3145736 | tf_op jit(solution)/shard_map/ppermute | solution.py:24
  14.6 29.5 %collective-permute-start.15 = (bf16[1024,512]{1,0:T(8,128)(2,1)}, bf16[1024,512]{1,0:T(8,128)(2,1)S(1)}, u32[]{:S(2)}, u32[]{:S(2)}) collective-permute-start(bf16[1024,512]{1,0:T(8,128)(2,1)} %refs_4_.1), channel_id=1, source_target_pairs={{0,96},{32,0},{64,32},{96,64},{1,97},{33,1},{65,33},{97,65},{2,98}... | collective-permute-start | bytes 3145736 | tf_op jit(solution)/shard_map/ppermute | solution.py:24
  16.8 8.7 %collective-permute-start.5 = (bf16[1536,128]{1,0:T(8,128)(2,1)S(1)}, bf16[1536,128]{1,0:T(8,128)(2,1)S(1)}, u32[]{:S(2)}, u32[]{:S(2)}) collective-permute-start(bf16[1536,128]{1,0:T(8,128)(2,1)S(1)} %pad_maximum_fusion.refs_1_), channel_id=1, source_target_pairs={{0,8},{8,16},{16,24},{24,0},{1,9},{9,17},{17,25},{25,1},{2,10},{10... | collective-permute-start | bytes 1179656 | tf_op jit(solution)/shard_map/ppermute | solution.py:24
  17.1 10.9 %collective-permute-start.7 = (bf16[1536,128]{1,0:T(8,128)(2,1)S(1)}, bf16[1536,128]{1,0:T(8,128)(2,1)S(1)}, u32[]{:S(2)}, u32[]{:S(2)}) collective-permute-start(bf16[1536,128]{1,0:T(8,128)(2,1)S(1)} %pad_maximum_fusion.refs_1_), channel_id=1, source_target_pairs={{0,24},{8,0},{16,8},{24,16},{1,25},{9,1},{17,9},{25,17},{2,26},{10... | collective-permute-start | bytes 1179656 | tf_op jit(solution)/shard_map/ppermute | solution.py:24
  26.2 2.8 %copy-start.7 = (s32[4096]{0:T(1024)S(1)}, s32[4096]{0:T(1024)}, u32[]{:S(2)}) copy-start(s32[4096]{0:T(1024)} %param.10) | copy-start | bytes 49156
  26.2 6.7 %collective-permute-start.6 = (bf16[1024,128]{1,0:T(8,128)(2,1)}, bf16[1024,128]{1,0:T(8,128)(2,1)}, u32[]{:S(2)}, u32[]{:S(2)}) collective-permute-start(bf16[1024,128]{1,0:T(8,128)(2,1)} %join.4), channel_id=1, source_target_pairs={{0,8},{8,16},{16,24},{24,0},{1,9},{9,17},{17,25},{25,1},{2,10},{10... | collective-permute-start | bytes 786440 | tf_op jit(solution)/shard_map/ppermute | solution.py:24
  28.6 7.9 %collective-permute-start.8 = (bf16[1024,128]{1,0:T(8,128)(2,1)}, bf16[1024,128]{1,0:T(8,128)(2,1)}, u32[]{:S(2)}, u32[]{:S(2)}) collective-permute-start(bf16[1024,128]{1,0:T(8,128)(2,1)} %join.5), channel_id=1, source_target_pairs={{0,24},{8,0},{16,8},{24,16},{1,25},{9,1},{17,9},{25,17},{2,26},{10... | collective-permute-start | bytes 786440 | tf_op jit(solution)/shard_map/ppermute | solution.py:24
  30.5 0.9 copy-start.2
  36.5 1.2 %copy-start = (bf16[256,1024]{1,0:T(8,128)(2,1)S(1)}, bf16[256,1024]{1,0:T(8,128)(2,1)}, u32[]{:S(2)}) copy-start(bf16[256,1024]{1,0:T(8,128)(2,1)} %q.2) | copy-start | bytes 1572868
  37.7 0.7 copy-start.3
  37.8 0.7 copy-start.4
  40.7 8.9 %collective-permute-start.9 = (bf16[128,1024]{1,0:T(8,128)(2,1)S(1)}, bf16[128,1024]{1,0:T(8,128)(2,1)S(1)}, u32[]{:S(2)}, u32[]{:S(2)}) collective-permute-start(bf16[128,1024]{1,0:T(8,128)(2,1)S(1)} %attend.2.refs_0_), channel_id=1, source_target_pairs={{0,8},{8,16},{16,24},{24,0},{1,9},{9,17},{17,25},{25,1},{2,10},{10... | collective-permute-start | bytes 786440 | tf_op jit(solution)/shard_map/ppermute | solution.py:24
  44.0 15.9 %copy-start.5 = (bf16[1024,512]{1,0:T(8,128)(2,1)S(1)}, bf16[1024,512]{1,0:T(8,128)(2,1)}, u32[]{:S(2)}) copy-start(bf16[1024,512]{1,0:T(8,128)(2,1)} %refs_4_.1) | copy-start | bytes 3145732
  44.0 15.9 %collective-permute-start.16 = (bf16[512,512]{1,0:T(8,128)(2,1)S(1)}, bf16[512,512]{1,0:T(8,128)(2,1)S(1)}, u32[]{:S(2)}, u32[]{:S(2)}) collective-permute-start(bf16[512,512]{1,0:T(8,128)(2,1)S(1)} %join.6), channel_id=1, source_target_pairs={{0,32},{32,64},{64,96},{96,0},{1,33},{33,65},{65,97},{97,1},{2,34}... | collective-permute-start | bytes 1572872 | tf_op jit(solution)/shard_map/ppermute | solution.py:24
  44.1 15.8 %collective-permute-start.17 = (bf16[512,512]{1,0:T(8,128)(2,1)S(1)}, bf16[512,512]{1,0:T(8,128)(2,1)S(1)}, u32[]{:S(2)}, u32[]{:S(2)}) collective-permute-start(bf16[512,512]{1,0:T(8,128)(2,1)S(1)} %join.7), channel_id=1, source_target_pairs={{0,96},{32,0},{64,32},{96,64},{1,97},{33,1},{65,33},{97,65},{2,98}... | collective-permute-start | bytes 1572872 | tf_op jit(solution)/shard_map/ppermute | solution.py:24
  47.4 6.4 %collective-permute-start.11 = (bf16[128,1024]{1,0:T(8,128)(2,1)S(1)}, bf16[128,1024]{1,0:T(8,128)(2,1)S(1)}, u32[]{:S(2)}, u32[]{:S(2)}) collective-permute-start(bf16[128,1024]{1,0:T(8,128)(2,1)S(1)} %attend.3.refs_1_), channel_id=1, source_target_pairs={{0,8},{8,16},{16,24},{24,0},{1,9},{9,17},{17,25},{25,1},{2,10},{10... | collective-permute-start | bytes 786440 | tf_op jit(solution)/shard_map/ppermute | solution.py:24
  49.4 7.7 %collective-permute-start.12 = (bf16[128,1024]{1,0:T(8,128)(2,1)S(1)}, bf16[128,1024]{1,0:T(8,128)(2,1)S(1)}, u32[]{:S(2)}, u32[]{:S(2)}) collective-permute-start(bf16[128,1024]{1,0:T(8,128)(2,1)S(1)} %attend.2.refs_0_), channel_id=1, source_target_pairs={{0,24},{8,0},{16,8},{24,16},{1,25},{9,1},{17,9},{25,17},{2,26},{10... | collective-permute-start | bytes 786440 | tf_op jit(solution)/shard_map/ppermute | solution.py:24
  49.6 10.3 %collective-permute-start.13 = (bf16[128,1024]{1,0:T(8,128)(2,1)S(1)}, bf16[128,1024]{1,0:T(8,128)(2,1)S(1)}, u32[]{:S(2)}, u32[]{:S(2)}) collective-permute-start(bf16[128,1024]{1,0:T(8,128)(2,1)S(1)} %attend.3.refs_1_), channel_id=1, source_target_pairs={{0,24},{8,0},{16,8},{24,16},{1,25},{9,1},{17,9},{25,17},{2,26},{10... | collective-permute-start | bytes 786440 | tf_op jit(solution)/shard_map/ppermute | solution.py:24
  62.3 2.7 %collective-permute-start.18 = (bf16[4,256,512]{2,1,0:T(8,128)(2,1)S(1)}, bf16[4,256,512]{2,1,0:T(8,128)(2,1)S(1)}, u32[]{:S(2)}, u32[]{:S(2)}) collective-permute-start(bf16[4,256,512]{2,1,0:T(8,128)(2,1)S(1)} %get-tuple-element.45), channel_id=1, source_target_pairs={{0,1},{1,0},{2,3},{3,2},{4,5},{5,4},{6,7},{7,6},{8,9},{9,8},{10,11... | collective-permute-start | bytes 3145736 | tf_op jit(solution)/shard_map/ppermute | solution.py:28
  62.4 8.7 %collective-permute-start.10 = (bf16[128,1024]{1,0:T(8,128)(2,1)S(1)}, bf16[128,1024]{1,0:T(8,128)(2,1)S(1)}, u32[]{:S(2)}, u32[]{:S(2)}) collective-permute-start(bf16[128,1024]{1,0:T(8,128)(2,1)S(1)} %collective-permute-done.9.refs_0_), channel_id=1, source_target_pairs={{0,8},{8,16},{16,24},{24,0},{1,9},{9,17},{17,25},{25,1},{2,10},{10... | collective-permute-start | bytes 786440 | tf_op jit(solution)/shard_map/ppermute | solution.py:24
  62.4 9.8 %collective-permute-start.19 = (bf16[128,1024]{1,0:T(8,128)(2,1)S(1)}, bf16[128,1024]{1,0:T(8,128)(2,1)S(1)}, u32[]{:S(2)}, u32[]{:S(2)}) collective-permute-start(bf16[128,1024]{1,0:T(8,128)(2,1)S(1)} %collective-permute-done.13.refs_3_), channel_id=1, source_target_pairs={{0,24},{8,0},{16,8},{24,16},{1,25},{9,1},{17,9},{25,17},{2,26},{10... | collective-permute-start | bytes 786440 | tf_op jit(solution)/shard_map/ppermute | solution.py:24
  74.7 2.7 %collective-permute-start.20 = (bf16[4,256,512]{2,1,0:T(8,128)(2,1)S(1)}, bf16[4,256,512]{2,1,0:T(8,128)(2,1)S(1)}, u32[]{:S(2)}, u32[]{:S(2)}) collective-permute-start(bf16[4,256,512]{2,1,0:T(8,128)(2,1)S(1)} %get-tuple-element.49), channel_id=1, source_target_pairs={{0,1},{1,0},{2,3},{3,2},{4,5},{5,4},{6,7},{7,6},{8,9},{9,8},{10,11... | collective-permute-start | bytes 3145736 | tf_op jit(solution)/shard_map/ppermute | solution.py:28
  74.8 7.7 %collective-permute-start.26 = (bf16[256,512]{1,0:T(8,128)(2,1)S(1)}, bf16[256,512]{1,0:T(8,128)(2,1)S(1)}, u32[]{:S(2)}, u32[]{:S(2)}) collective-permute-start(bf16[256,512]{1,0:T(8,128)(2,1)S(1)} %get-tuple-element.46), channel_id=1, source_target_pairs={{0,2},{1,7},{2,4},{3,1},{4,6},{5,3},{6,0},{7,5},{8,10},{9,15},{10,... | collective-permute-start | bytes 786440 | tf_op jit(solution)/shard_map/ppermute | solution.py:258
  77.9 7.7 %collective-permute-start.22 = (bf16[256,512]{1,0:T(8,128)(2,1)S(1)}, bf16[256,512]{1,0:T(8,128)(2,1)S(1)}, u32[]{:S(2)}, u32[]{:S(2)}) collective-permute-start(bf16[256,512]{1,0:T(8,128)(2,1)S(1)} %get-tuple-element.53), channel_id=1, source_target_pairs={{0,2},{1,7},{2,4},{3,1},{4,6},{5,3},{6,0},{7,5},{8,10},{9,15},{10,... | collective-permute-start | bytes 786440 | tf_op jit(solution)/shard_map/ppermute | solution.py:258
  82.5 7.7 %collective-permute-start.27 = (bf16[256,512]{1,0:T(8,128)(2,1)S(1)}, bf16[256,512]{1,0:T(8,128)(2,1)S(1)}, u32[]{:S(2)}, u32[]{:S(2)}) collective-permute-start(bf16[256,512]{1,0:T(8,128)(2,1)S(1)} %add_convert_fusion.2), channel_id=1, source_target_pairs={{0,2},{1,7},{2,4},{3,1},{4,6},{5,3},{6,0},{7,5},{8,10},{9,15},{10,... | collective-permute-start | bytes 786440 | tf_op jit(solution)/shard_map/ppermute | solution.py:258
  85.6 7.7 %collective-permute-start.23 = (bf16[256,512]{1,0:T(8,128)(2,1)S(1)}, bf16[256,512]{1,0:T(8,128)(2,1)S(1)}, u32[]{:S(2)}, u32[]{:S(2)}) collective-permute-start(bf16[256,512]{1,0:T(8,128)(2,1)S(1)} %add_convert_fusion.5), channel_id=1, source_target_pairs={{0,2},{1,7},{2,4},{3,1},{4,6},{5,3},{6,0},{7,5},{8,10},{9,15},{10,... | collective-permute-start | bytes 786440 | tf_op jit(solution)/shard_map/ppermute | solution.py:258
  86.1 9.8 %collective-permute-start.25 = (bf16[256,512]{1,0:T(8,128)(2,1)S(1)}, bf16[256,512]{1,0:T(8,128)(2,1)S(1)}, u32[]{:S(2)}, u32[]{:S(2)}) collective-permute-start(bf16[256,512]{1,0:T(8,128)(2,1)S(1)} %get-tuple-element.54), channel_id=1, source_target_pairs={{0,24},{1,8},{2,26},{3,10},{4,28},{5,12},{6,30},{7,14},{8,0},{9,16... | collective-permute-start | bytes 786440 | tf_op jit(solution)/shard_map/ppermute | solution.py:268
  90.2 15.4 %collective-permute-start.28 = (bf16[256,512]{1,0:T(8,128)(2,1)S(1)}, bf16[256,512]{1,0:T(8,128)(2,1)S(1)}, u32[]{:S(2)}, u32[]{:S(2)}) collective-permute-start(bf16[256,512]{1,0:T(8,128)(2,1)S(1)} %add_convert_fusion.1), channel_id=1, source_target_pairs={{0,26},{1,14},{2,28},{3,8},{4,30},{5,10},{6,24},{7,12},{8,2},{9,22... | collective-permute-start | bytes 786440 | tf_op jit(solution)/shard_map/ppermute | solution.py:268
  90.3 15.4 %collective-permute-start.21 = (bf16[256,512]{1,0:T(8,128)(2,1)S(1)}, bf16[256,512]{1,0:T(8,128)(2,1)S(1)}, u32[]{:S(2)}, u32[]{:S(2)}) collective-permute-start(bf16[256,512]{1,0:T(8,128)(2,1)S(1)} %get-tuple-element.50), channel_id=1, source_target_pairs={{0,0},{1,16},{2,2},{3,18},{4,4},{5,20},{6,6},{7,22},{8,8},{9,24},{... | collective-permute-start | bytes 786440 | tf_op jit(solution)/shard_map/ppermute | solution.py:268
  93.4 12.3 %collective-permute-start.24 = (bf16[256,512]{1,0:T(8,128)(2,1)S(1)}, bf16[256,512]{1,0:T(8,128)(2,1)S(1)}, u32[]{:S(2)}, u32[]{:S(2)}) collective-permute-start(bf16[256,512]{1,0:T(8,128)(2,1)S(1)} %add_convert_fusion.4), channel_id=1, source_target_pairs={{0,2},{1,22},{2,4},{3,16},{4,6},{5,18},{6,0},{7,20},{8,10},{9,30},... | collective-permute-start | bytes 786440 | tf_op jit(solution)/shard_map/ppermute | solution.py:268

commit v3 on v2

--- a/solution.py
+++ b/solution.py
@@ -159,7 +159,7 @@
         out_specs=VMEM,
         compiler_params=pltpu.CompilerParams(vmem_limit_bytes=16 * 2**20),
         cost_estimate=pl.CostEstimate(
-            flops=4 * rows * 1024 * width, bytes_accessed=4 * 2**20, transcendentals=rows * 8 * width
+            flops=24 * rows * 1024 * width, bytes_accessed=4 * 2**20, transcendentals=rows * 8 * width
         ),
         name="attend",
     )(positions, lengths, spans, q, *ordered)
@@ -323,7 +323,7 @@
     rows = (upper_left, lower_left, upper_right, lower_right)
     keep, send = project(rows, (0, 1), (2, 3), weights)
     near = combine(keep, swap_cores(send))
-    rows = (upper, lower, after(upper_far, near[0]), lower_far)
+    rows = (upper, lower, upper_far, lower_far)
     keep, send = project(rows, (0, 1), (2, 3), weights)
     mixed = combine(keep, swap_cores(send))
 

time: 107 us -> 97.2 us (0.908)
  waiting for transfers between devices: 50.6 us -> 41.9 us
    ppermute x19, waiting for transfers between devices: 30.8 us -> 23.1 us  [shift(): return lax.ppermute(value, axis, [(i, (i + step) % 4) for i in range(4)])]
    ppermute x2, waiting for transfers between devices: 1.55 us -> 0.47 us  [swap_cores(): return lax.ppermute(value, 'c', [(0, 1), (1, 0)])]
  transfers between devices with their start and end apart: 29 -> 29, of which waited for: 18 -> 16; matrix products, arithmetic and copies ran while one was open for 2% -> 2% of each run, Pallas kernels for 10% -> 16%
where the time goes in v3:
time: 97.2 us; the launch traced here: 97.1 us
  waiting for transfers between devices  41.9 us (43%)
  starting transfers between devices  34.4 us (35%)
  Pallas kernels  15.2 us (16%)
  local copies, waits for them, and re-layouts  4 us (4%)
  other arithmetic  1.36 us (1%)
    ppermute x19, starting transfers between devices, shift(): return lax.ppermute(value, axis, [(i, (i + step) % 4) for i in range(4)])  24.5 us
    ppermute x19, waiting for transfers between devices, shift(): return lax.ppermute(value, axis, [(i, (i + step) % 4) for i in range(4)])  23.1 us
    ppermute x4, waiting for transfers between devices, home(): return lax.ppermute(value, ('x', 'y', 'c'), pairs)  10 us
    ppermute x4, waiting for transfers between devices, relay(): return lax.ppermute(value, (axis, 'c'), pairs)  8.35 us
    ppermute x4, starting transfers between devices, home(): return lax.ppermute(value, ('x', 'y', 'c'), pairs)  5.5 us
    pallas_call x2, Pallas kernels, attend(): pl.pallas_call(functools.partial(attend_kernel, first_row), out_shape=jax...  5.35 us
    pallas_call x2, Pallas kernels, project(): pl.pallas_call(functools.partial(project_kernel, core_zero, core_one), ou...  4.74 us
    ppermute x4, starting transfers between devices, relay(): return lax.ppermute(value, (axis, 'c'), pairs)  4.15 us
  transfers between devices with their start and end apart: 29, of which 16 were waited for; matrix products, arithmetic and copies ran while one was open for 2% of the time, Pallas kernels for 16%

profile of v3, /device:TPU:6, one launch (start us, length us, event | category | flops | bytes accessed | tf_op | source)
XLA Modules:
  0.0 97.1 jit_solution(11509674435884473885)
XLA Ops:
  0.0 0.9 constant_dynamic-update-slice_fusion.1
  0.9 4.0 %collective-permute-start.2 = (bf16[512,128]{1,0:T(8,128)(2,1)S(1)}, bf16[512,128]{1,0:T(8,128)(2,1)S(1)}, u32[]{:S(2)}, u32[]{:S(2)}) collective-permute-start(bf16[512,128]{1,0:T(8,128)(2,1)S(1)} %constant_dynamic-update-slice_fusion.refs_0_), channel_id=1, source_target_pairs={{0,64},{32,96},{64,0},{96,32},{1,65},{33,97},{65,1},{97,33},{2,66}... | collective-permute-start | bytes 393224 | tf_op jit(solution)/shard_map/ppermute | solution.py:24
  4.9 0.7 collective-permute-start.1
  5.6 1.3 %collective-permute-start = (bf16[512,128]{1,0:T(8,128)(2,1)S(1)}, bf16[512,128]{1,0:T(8,128)(2,1)S(1)}, u32[]{:S(2)}, u32[]{:S(2)}) collective-permute-start(bf16[512,128]{1,0:T(8,128)(2,1)S(1)} %constant_dynamic-update-slice_fusion.refs_0_), channel_id=1, source_target_pairs={{0,32},{32,64},{64,96},{96,0},{1,33},{33,65},{65,97},{97,1},{2,34}... | collective-permute-start | bytes 393224 | tf_op jit(solution)/shard_map/ppermute | solution.py:24
  7.4 1.5 %collective-permute-start.4 = (bf16[512,128]{1,0:T(8,128)(2,1)S(1)}, bf16[512,128]{1,0:T(8,128)(2,1)S(1)}, u32[]{:S(2)}, u32[]{:S(2)}) collective-permute-start(bf16[512,128]{1,0:T(8,128)(2,1)S(1)} %constant_dynamic-update-slice_fusion.refs_0_), channel_id=1, source_target_pairs={{0,24},{8,0},{16,8},{24,16},{1,25},{9,1},{17,9},{25,17},{2,26},{10... | collective-permute-start | bytes 393224 | tf_op jit(solution)/shard_map/ppermute | solution.py:24
  8.9 3.0 %collective-permute-done.1 = bf16[512,128]{1,0:T(8,128)(2,1)S(1)} collective-permute-done((bf16[512,128]{1,0:T(8,128)(2,1)S(1)}, bf16[512,128]{1,0:T(8,128)(2,1)S(1)}, u32[]{:S(2)}, u32[]{:S(2)}) %collective-permute-start.1) | collective-permute-done | bytes 131104 | tf_op jit(solution)/shard_map/ppermute | solution.py:24
  12.0 1.5 %collective-permute-done.4.refs_1_.refs_3_ = bf16[512,128]{1,0:T(8,128)(2,1)S(1)} collective-permute-done((bf16[512,128]{1,0:T(8,128)(2,1)S(1)}, bf16[512,128]{1,0:T(8,128)(2,1)S(1)}, u32[]{:S(2)}, u32[]{:S(2)}) %collective-permute-start.4) | collective-permute-done | bytes 131104 | tf_op jit(solution)/shard_map/ppermute | solution.py:24
  13.8 1.7 %collective-permute-start.7 = (bf16[1536,128]{1,0:T(8,128)(2,1)S(1)}, bf16[1536,128]{1,0:T(8,128)(2,1)S(1)}, u32[]{:S(2)}, u32[]{:S(2)}) collective-permute-start(bf16[1536,128]{1,0:T(8,128)(2,1)S(1)} %pad_maximum_fusion.refs_1_), channel_id=1, source_target_pairs={{0,24},{8,0},{16,8},{24,16},{1,25},{9,1},{17,9},{25,17},{2,26},{10... | collective-permute-start | bytes 1179656 | tf_op jit(solution)/shard_map/ppermute | solution.py:24
  15.6 1.0 %collective-permute-start.13 = (bf16[1024,512]{1,0:T(8,128)(2,1)}, bf16[1024,512]{1,0:T(8,128)(2,1)S(1)}, u32[]{:S(2)}, u32[]{:S(2)}) collective-permute-start(bf16[1024,512]{1,0:T(8,128)(2,1)} %refs_4_.1), channel_id=1, source_target_pairs={{0,32},{32,64},{64,96},{96,0},{1,33},{33,65},{65,97},{97,1},{2,34}... | collective-permute-start | bytes 3145736 | tf_op jit(solution)/shard_map/ppermute | solution.py:24
  16.6 2.2 %collective-permute-start.14 = (bf16[1024,512]{1,0:T(8,128)(2,1)}, bf16[1024,512]{1,0:T(8,128)(2,1)S(1)}, u32[]{:S(2)}, u32[]{:S(2)}) collective-permute-start(bf16[1024,512]{1,0:T(8,128)(2,1)} %refs_4_.1), channel_id=1, source_target_pairs={{0,96},{32,0},{64,32},{96,64},{1,97},{33,1},{65,33},{97,65},{2,98}... | collective-permute-start | bytes 3145736 | tf_op jit(solution)/shard_map/ppermute | solution.py:24
  18.8 3.6 %collective-permute-done.5.refs_0_ = bf16[1536,128]{1,0:T(8,128)(2,1)S(1)} collective-permute-done((bf16[1536,128]{1,0:T(8,128)(2,1)S(1)}, bf16[1536,128]{1,0:T(8,128)(2,1)S(1)}, u32[]{:S(2)}, u32[]{:S(2)}) %collective-permute-start.5) | collective-permute-done | bytes 393248 | tf_op jit(solution)/shard_map/ppermute | solution.py:24
  22.4 0.7 join.4
  23.1 1.5 %collective-permute-start.6 = (bf16[1024,128]{1,0:T(8,128)(2,1)}, bf16[1024,128]{1,0:T(8,128)(2,1)}, u32[]{:S(2)}, u32[]{:S(2)}) collective-permute-start(bf16[1024,128]{1,0:T(8,128)(2,1)} %join.4), channel_id=1, source_target_pairs={{0,8},{8,16},{16,24},{24,0},{1,9},{9,17},{17,25},{25,1},{2,10},{10... | collective-permute-start | bytes 786440 | tf_op jit(solution)/shard_map/ppermute | solution.py:24
  24.6 0.7 join.5
  25.9 0.7 reshape.3
  26.6 0.9 slice_reduce_fusion.pos
  27.5 0.9 copy-done.1
  28.4 0.7 place.3
  29.0 0.7 place.4
  29.8 3.4 %collective-permute-done.8.refs_1_ = bf16[1024,128]{1,0:T(8,128)(2,1)} collective-permute-done((bf16[1024,128]{1,0:T(8,128)(2,1)}, bf16[1024,128]{1,0:T(8,128)(2,1)}, u32[]{:S(2)}, u32[]{:S(2)}) %collective-permute-start.8) | collective-permute-done | bytes 262176 | tf_op jit(solution)/shard_map/ppermute | solution.py:24
  33.3 1.2 %place.5 = (bf16[4096,128]{1,0:T(8,128)(2,1)S(1)}, bf16[4096,128]{1,0:T(8,128)(2,1)S(1)}) custom-call(s32[64]{0:T(128)S(1)} %slice_reduce_fusion.pos, bf16[1024,128]{1,0:T(8,128)(2,1)} %collective-permute-done.6.refs_0_, bf16[1024,128]{1,0:T(8,128)(2,1)} %collective-permute-done.8.refs_1_, ...), custom_call_target="tpu_custom_call", output_to_operand_aliasing={{0}: (3, {}), {1}: (4, {})} | custom-call | bytes 2097152 | tf_op jit(solution)/shard_map/place/pallas_call | solution.py:57
  34.5 0.6 copy-done.4
  35.2 2.7 %attend.2.refs_0_ = bf16[128,1024]{1,0:T(8,128)(2,1)S(1)} custom-call(s32[64]{0:T(128)S(1)} %slice_reduce_fusion.pos, s32[8]{0:T(128)S(1)} %copy-done.5, s32[2,4]{1,0:T(2,128)S(1)} %copy-done.4, bf16[256,1024]{1,0:T(8,128)(2,1)S(1)} %copy-done.3, bf16[4096,128]{1,0:T(8,128)(2,1)S(1)} %get-tuple-element.37.ks, bf16[4096,128]{1,0:T(8,128)(2,1)S(1)} %get-tuple-element.38.vs), custom_call_target="tpu_custom_call" | custom-call | flops 3221225472 | bytes 4194304 | tf_op jit(solution)/shard_map/attend/pallas_call | solution.py:155
  38.2 2.6 %attend.3.refs_1_ = bf16[128,1024]{1,0:T(8,128)(2,1)S(1)} custom-call(s32[64]{0:T(128)S(1)} %slice_reduce_fusion.pos, s32[8]{0:T(128)S(1)} %copy-done.5, s32[2,4]{1,0:T(2,128)S(1)} %copy-done.4, bf16[256,1024]{1,0:T(8,128)(2,1)S(1)} %copy-done.3, bf16[4096,128]{1,0:T(8,128)(2,1)S(1)} %get-tuple-element.37.ks, bf16[4096,128]{1,0:T(8,128)(2,1)S(1)} %get-tuple-element.38.vs), custom_call_target="tpu_custom_call" | custom-call | flops 3221225472 | bytes 4194304 | tf_op jit(solution)/shard_map/attend/pallas_call | solution.py:155
  40.9 1.1 %collective-permute-start.15 = (bf16[512,512]{1,0:T(8,128)(2,1)S(1)}, bf16[512,512]{1,0:T(8,128)(2,1)S(1)}, u32[]{:S(2)}, u32[]{:S(2)}) collective-permute-start(bf16[512,512]{1,0:T(8,128)(2,1)S(1)} %join.6), channel_id=1, source_target_pairs={{0,32},{32,64},{64,96},{96,0},{1,33},{33,65},{65,97},{97,1},{2,34}... | collective-permute-start | bytes 1572872 | tf_op jit(solution)/shard_map/ppermute | solution.py:24
  42.0 2.4 %collective-permute-start.16 = (bf16[512,512]{1,0:T(8,128)(2,1)S(1)}, bf16[512,512]{1,0:T(8,128)(2,1)S(1)}, u32[]{:S(2)}, u32[]{:S(2)}) collective-permute-start(bf16[512,512]{1,0:T(8,128)(2,1)S(1)} %join.7), channel_id=1, source_target_pairs={{0,96},{32,0},{64,32},{96,64},{1,97},{33,1},{65,33},{97,65},{2,98}... | collective-permute-start | bytes 1572872 | tf_op jit(solution)/shard_map/ppermute | solution.py:24
  44.4 1.3 %collective-permute-start.22 = (bf16[128,1024]{1,0:T(8,128)(2,1)S(1)}, bf16[128,1024]{1,0:T(8,128)(2,1)S(1)}, u32[]{:S(2)}, u32[]{:S(2)}) collective-permute-start(bf16[128,1024]{1,0:T(8,128)(2,1)S(1)} %attend.3.refs_1_), channel_id=1, source_target_pairs={{0,8},{8,16},{16,24},{24,0},{1,9},{9,17},{17,25},{25,1},{2,10},{10... | collective-permute-start | bytes 786440 | tf_op jit(solution)/shard_map/ppermute | solution.py:24
  45.7 1.4 %collective-permute-start.11 = (bf16[128,1024]{1,0:T(8,128)(2,1)S(1)}, bf16[128,1024]{1,0:T(8,128)(2,1)S(1)}, u32[]{:S(2)}, u32[]{:S(2)}) collective-permute-start(bf16[128,1024]{1,0:T(8,128)(2,1)S(1)} %attend.3.refs_1_), channel_id=1, source_target_pairs={{0,24},{8,0},{16,8},{24,16},{1,25},{9,1},{17,9},{25,17},{2,26},{10... | collective-permute-start | bytes 786440 | tf_op jit(solution)/shard_map/ppermute | solution.py:24
  47.1 2.0 %collective-permute-start.23 = (bf16[128,1024]{1,0:T(8,128)(2,1)S(1)}, bf16[128,1024]{1,0:T(8,128)(2,1)S(1)}, u32[]{:S(2)}, u32[]{:S(2)}) collective-permute-start(bf16[128,1024]{1,0:T(8,128)(2,1)S(1)} %attend.2.refs_0_), channel_id=1, source_target_pairs={{0,24},{8,0},{16,8},{24,16},{1,25},{9,1},{17,9},{25,17},{2,26},{10... | collective-permute-start | bytes 786440 | tf_op jit(solution)/shard_map/ppermute | solution.py:24
  49.1 3.6 %collective-permute-done.22.refs_1_ = bf16[128,1024]{1,0:T(8,128)(2,1)S(1)} collective-permute-done((bf16[128,1024]{1,0:T(8,128)(2,1)S(1)}, bf16[128,1024]{1,0:T(8,128)(2,1)S(1)}, u32[]{:S(2)}, u32[]{:S(2)}) %collective-permute-start.22) | collective-permute-done | bytes 262176 | tf_op jit(solution)/shard_map/ppermute | solution.py:24
  53.3 2.9 %collective-permute-done.11.refs_3_ = bf16[128,1024]{1,0:T(8,128)(2,1)S(1)} collective-permute-done((bf16[128,1024]{1,0:T(8,128)(2,1)S(1)}, bf16[128,1024]{1,0:T(8,128)(2,1)S(1)}, u32[]{:S(2)}, u32[]{:S(2)}) %collective-permute-start.11) | collective-permute-done | bytes 262176 | tf_op jit(solution)/shard_map/ppermute | solution.py:24
  56.3 3.9 %collective-permute-done.23.refs_2_ = bf16[128,1024]{1,0:T(8,128)(2,1)S(1)} collective-permute-done((bf16[128,1024]{1,0:T(8,128)(2,1)S(1)}, bf16[128,1024]{1,0:T(8,128)(2,1)S(1)}, u32[]{:S(2)}, u32[]{:S(2)}) %collective-permute-start.23) | collective-permute-done | bytes 262176 | tf_op jit(solution)/shard_map/ppermute | solution.py:24
  60.3 2.4 %project.3 = (bf16[4,256,512]{2,1,0:T(8,128)(2,1)S(1)}, bf16[4,256,512]{2,1,0:T(8,128)(2,1)S(1)}) custom-call(bf16[128,1024]{1,0:T(8,128)(2,1)S(1)} %collective-permute-done.9.refs_0_, bf16[128,1024]{1,0:T(8,128)(2,1)S(1)} %collective-permute-done.22.refs_1_, bf16[128,1024]{1,0:T(8,128)(2,1)S(1)} %collective-permute-done.23.refs_2_, ...), custom_call_target="tpu_custom_call" | custom-call | flops 2147483648 | bytes 4194304 | tf_op jit(solution)/shard_map/project/pallas_call | solution.py:216
  62.8 0.9 collective-permute-done.12.refs_3_
  63.7 2.4 %project.2 = (bf16[4,256,512]{2,1,0:T(8,128)(2,1)S(1)}, bf16[4,256,512]{2,1,0:T(8,128)(2,1)S(1)}) custom-call(bf16[128,1024]{1,0:T(8,128)(2,1)S(1)} %attend.2.refs_0_, bf16[128,1024]{1,0:T(8,128)(2,1)S(1)} %attend.3.refs_1_, bf16[128,1024]{1,0:T(8,128)(2,1)S(1)} %collective-permute-done.10.refs_2_, bf16[128,1024]{1,0:T(8,128)(2,1)S(1)} %collective-permute-done.12.refs_3_, ...), custom_call_target="tpu_custom_call" | custom-call | flops 2147483648 | bytes 4194304 | tf_op jit(solution)/shard_map/project/pallas_call | solution.py:216
  66.7 1.6 %collective-permute-start.26 = (bf16[256,512]{1,0:T(8,128)(2,1)S(1)}, bf16[256,512]{1,0:T(8,128)(2,1)S(1)}, u32[]{:S(2)}, u32[]{:S(2)}) collective-permute-start(bf16[256,512]{1,0:T(8,128)(2,1)S(1)} %get-tuple-element.54), channel_id=1, source_target_pairs={{0,2},{1,7},{2,4},{3,1},{4,6},{5,3},{6,0},{7,5},{8,10},{9,15},{10,... | collective-permute-start | bytes 786440 | tf_op jit(solution)/shard_map/ppermute | solution.py:258
  69.4 1.6 %collective-permute-start.19 = (bf16[256,512]{1,0:T(8,128)(2,1)S(1)}, bf16[256,512]{1,0:T(8,128)(2,1)S(1)}, u32[]{:S(2)}, u32[]{:S(2)}) collective-permute-start(bf16[256,512]{1,0:T(8,128)(2,1)S(1)} %get-tuple-element.48), channel_id=1, source_target_pairs={{0,2},{1,7},{2,4},{3,1},{4,6},{5,3},{6,0},{7,5},{8,10},{9,15},{10,... | collective-permute-start | bytes 786440 | tf_op jit(solution)/shard_map/ppermute | solution.py:258
  71.0 3.4 %collective-permute-done.26 = bf16[256,512]{1,0:T(8,128)(2,1)S(1)} collective-permute-done((bf16[256,512]{1,0:T(8,128)(2,1)S(1)}, bf16[256,512]{1,0:T(8,128)(2,1)S(1)}, u32[]{:S(2)}, u32[]{:S(2)}) %collective-permute-start.26) | collective-permute-done | bytes 262176 | tf_op jit(solution)/shard_map/ppermute | solution.py:258
  74.9 2.3 %collective-permute-done.19 = bf16[256,512]{1,0:T(8,128)(2,1)S(1)} collective-permute-done((bf16[256,512]{1,0:T(8,128)(2,1)S(1)}, bf16[256,512]{1,0:T(8,128)(2,1)S(1)}, u32[]{:S(2)}, u32[]{:S(2)}) %collective-permute-start.19) | collective-permute-done | bytes 262176 | tf_op jit(solution)/shard_map/ppermute | solution.py:258
  77.7 0.8 collective-permute-start.25
  78.5 2.8 %collective-permute-start.18 = (bf16[256,512]{1,0:T(8,128)(2,1)S(1)}, bf16[256,512]{1,0:T(8,128)(2,1)S(1)}, u32[]{:S(2)}, u32[]{:S(2)}) collective-permute-start(bf16[256,512]{1,0:T(8,128)(2,1)S(1)} %get-tuple-element.45), channel_id=1, source_target_pairs={{0,0},{1,16},{2,2},{3,18},{4,4},{5,20},{6,6},{7,22},{8,8},{9,24},{... | collective-permute-start | bytes 786440 | tf_op jit(solution)/shard_map/ppermute | solution.py:268
  81.3 0.8 collective-permute-done.27
  82.2 0.9 collective-permute-start.28
  83.0 1.9 %collective-permute-done.20 = bf16[256,512]{1,0:T(8,128)(2,1)S(1)} collective-permute-done((bf16[256,512]{1,0:T(8,128)(2,1)S(1)}, bf16[256,512]{1,0:T(8,128)(2,1)S(1)}, u32[]{:S(2)}, u32[]{:S(2)}) %collective-permute-start.20) | collective-permute-done | bytes 262176 | tf_op jit(solution)/shard_map/ppermute | solution.py:258
  85.0 1.0 %collective-permute-start.21 = (bf16[256,512]{1,0:T(8,128)(2,1)S(1)}, bf16[256,512]{1,0:T(8,128)(2,1)S(1)}, u32[]{:S(2)}, u32[]{:S(2)}) collective-permute-start(bf16[256,512]{1,0:T(8,128)(2,1)S(1)} %add_convert_fusion.4), channel_id=1, source_target_pairs={{0,2},{1,22},{2,4},{3,16},{4,6},{5,18},{6,0},{7,20},{8,10},{9,30},... | collective-permute-start | bytes 786440 | tf_op jit(solution)/shard_map/ppermute | solution.py:268
  86.0 0.6 collective-permute-done.25
  86.6 9.4 %collective-permute-done.28 = bf16[256,512]{1,0:T(8,128)(2,1)S(1)} collective-permute-done((bf16[256,512]{1,0:T(8,128)(2,1)S(1)}, bf16[256,512]{1,0:T(8,128)(2,1)S(1)}, u32[]{:S(2)}, u32[]{:S(2)}) %collective-permute-start.28) | collective-permute-done | bytes 262176 | tf_op jit(solution)/shard_map/ppermute | solution.py:268
  96.2 0.9 maximum_select_fusion
  (51 shorter events, 5.6 us)
Async XLA Ops:
  0.0 0.9 copy-start.6
  0.9 11.1 %copy-start = (bf16[512,128]{1,0:T(8,128)(2,1)}, bf16[512,128]{1,0:T(8,128)(2,1)S(1)}, u32[]{:S(2)}) copy-start(bf16[512,128]{1,0:T(8,128)(2,1)S(1)} %constant_dynamic-update-slice_fusion.refs_0_) | copy-start | bytes 393220
  0.9 8.0 %collective-permute-start.2 = (bf16[512,128]{1,0:T(8,128)(2,1)S(1)}, bf16[512,128]{1,0:T(8,128)(2,1)S(1)}, u32[]{:S(2)}, u32[]{:S(2)}) collective-permute-start(bf16[512,128]{1,0:T(8,128)(2,1)S(1)} %constant_dynamic-update-slice_fusion.refs_0_), channel_id=1, source_target_pairs={{0,64},{32,96},{64,0},{96,32},{1,65},{33,97},{65,1},{97,33},{2,66}... | collective-permute-start | bytes 393224 | tf_op jit(solution)/shard_map/ppermute | solution.py:24
  4.9 7.1 %collective-permute-start.1 = (bf16[512,128]{1,0:T(8,128)(2,1)S(1)}, bf16[512,128]{1,0:T(8,128)(2,1)S(1)}, u32[]{:S(2)}, u32[]{:S(2)}) collective-permute-start(bf16[512,128]{1,0:T(8,128)(2,1)S(1)} %constant_dynamic-update-slice_fusion.refs_0_), channel_id=1, source_target_pairs={{0,96},{32,0},{64,32},{96,64},{1,97},{33,1},{65,33},{97,65},{2,98}... | collective-permute-start | bytes 393224 | tf_op jit(solution)/shard_map/ppermute | solution.py:24
  5.6 6.4 %collective-permute-start = (bf16[512,128]{1,0:T(8,128)(2,1)S(1)}, bf16[512,128]{1,0:T(8,128)(2,1)S(1)}, u32[]{:S(2)}, u32[]{:S(2)}) collective-permute-start(bf16[512,128]{1,0:T(8,128)(2,1)S(1)} %constant_dynamic-update-slice_fusion.refs_0_), channel_id=1, source_target_pairs={{0,32},{32,64},{64,96},{96,0},{1,33},{33,65},{65,97},{97,1},{2,34}... | collective-permute-start | bytes 393224 | tf_op jit(solution)/shard_map/ppermute | solution.py:24
  6.9 5.1 %collective-permute-start.3 = (bf16[512,128]{1,0:T(8,128)(2,1)S(1)}, bf16[512,128]{1,0:T(8,128)(2,1)S(1)}, u32[]{:S(2)}, u32[]{:S(2)}) collective-permute-start(bf16[512,128]{1,0:T(8,128)(2,1)S(1)} %constant_dynamic-update-slice_fusion.refs_0_), channel_id=1, source_target_pairs={{0,8},{8,16},{16,24},{24,0},{1,9},{9,17},{17,25},{25,1},{2,10},{10... | collective-permute-start | bytes 393224 | tf_op jit(solution)/shard_map/ppermute | solution.py:24
  7.4 6.2 %collective-permute-start.4 = (bf16[512,128]{1,0:T(8,128)(2,1)S(1)}, bf16[512,128]{1,0:T(8,128)(2,1)S(1)}, u32[]{:S(2)}, u32[]{:S(2)}) collective-permute-start(bf16[512,128]{1,0:T(8,128)(2,1)S(1)} %constant_dynamic-update-slice_fusion.refs_0_), channel_id=1, source_target_pairs={{0,24},{8,0},{16,8},{24,16},{1,25},{9,1},{17,9},{25,17},{2,26},{10... | collective-permute-start | bytes 393224 | tf_op jit(solution)/shard_map/ppermute | solution.py:24
  13.5 8.9 %collective-permute-start.5 = (bf16[1536,128]{1,0:T(8,128)(2,1)S(1)}, bf16[1536,128]{1,0:T(8,128)(2,1)S(1)}, u32[]{:S(2)}, u32[]{:S(2)}) collective-permute-start(bf16[1536,128]{1,0:T(8,128)(2,1)S(1)} %pad_maximum_fusion.refs_1_), channel_id=1, source_target_pairs={{0,8},{8,16},{16,24},{24,0},{1,9},{9,17},{17,25},{25,1},{2,10},{10... | collective-permute-start | bytes 1179656 | tf_op jit(solution)/shard_map/ppermute | solution.py:24
  13.8 10.8 %collective-permute-start.7 = (bf16[1536,128]{1,0:T(8,128)(2,1)S(1)}, bf16[1536,128]{1,0:T(8,128)(2,1)S(1)}, u32[]{:S(2)}, u32[]{:S(2)}) collective-permute-start(bf16[1536,128]{1,0:T(8,128)(2,1)S(1)} %pad_maximum_fusion.refs_1_), channel_id=1, source_target_pairs={{0,24},{8,0},{16,8},{24,16},{1,25},{9,1},{17,9},{25,17},{2,26},{10... | collective-permute-start | bytes 1179656 | tf_op jit(solution)/shard_map/ppermute | solution.py:24
  15.6 25.3 %collective-permute-start.13 = (bf16[1024,512]{1,0:T(8,128)(2,1)}, bf16[1024,512]{1,0:T(8,128)(2,1)S(1)}, u32[]{:S(2)}, u32[]{:S(2)}) collective-permute-start(bf16[1024,512]{1,0:T(8,128)(2,1)} %refs_4_.1), channel_id=1, source_target_pairs={{0,32},{32,64},{64,96},{96,0},{1,33},{33,65},{65,97},{97,1},{2,34}... | collective-permute-start | bytes 3145736 | tf_op jit(solution)/shard_map/ppermute | solution.py:24
  16.6 25.4 %collective-permute-start.14 = (bf16[1024,512]{1,0:T(8,128)(2,1)}, bf16[1024,512]{1,0:T(8,128)(2,1)S(1)}, u32[]{:S(2)}, u32[]{:S(2)}) collective-permute-start(bf16[1024,512]{1,0:T(8,128)(2,1)} %refs_4_.1), channel_id=1, source_target_pairs={{0,96},{32,0},{64,32},{96,64},{1,97},{33,1},{65,33},{97,65},{2,98}... | collective-permute-start | bytes 3145736 | tf_op jit(solution)/shard_map/ppermute | solution.py:24
  23.1 2.8 %copy-start.7 = (s32[4096]{0:T(1024)S(1)}, s32[4096]{0:T(1024)}, u32[]{:S(2)}) copy-start(s32[4096]{0:T(1024)} %param.10) | copy-start | bytes 49156
  23.1 6.7 %collective-permute-start.6 = (bf16[1024,128]{1,0:T(8,128)(2,1)}, bf16[1024,128]{1,0:T(8,128)(2,1)}, u32[]{:S(2)}, u32[]{:S(2)}) collective-permute-start(bf16[1024,128]{1,0:T(8,128)(2,1)} %join.4), channel_id=1, source_target_pairs={{0,8},{8,16},{16,24},{24,0},{1,9},{9,17},{17,25},{25,1},{2,10},{10... | collective-permute-start | bytes 786440 | tf_op jit(solution)/shard_map/ppermute | solution.py:24
  25.4 7.9 %collective-permute-start.8 = (bf16[1024,128]{1,0:T(8,128)(2,1)}, bf16[1024,128]{1,0:T(8,128)(2,1)}, u32[]{:S(2)}, u32[]{:S(2)}) collective-permute-start(bf16[1024,128]{1,0:T(8,128)(2,1)} %join.5), channel_id=1, source_target_pairs={{0,24},{8,0},{16,8},{24,16},{1,25},{9,1},{17,9},{25,17},{2,26},{10... | collective-permute-start | bytes 786440 | tf_op jit(solution)/shard_map/ppermute | solution.py:24
  27.4 0.9 copy-start.1
  33.3 1.2 %copy-start.3 = (bf16[256,1024]{1,0:T(8,128)(2,1)S(1)}, bf16[256,1024]{1,0:T(8,128)(2,1)}, u32[]{:S(2)}) copy-start(bf16[256,1024]{1,0:T(8,128)(2,1)} %q.2) | copy-start | bytes 1572868
  34.5 0.7 copy-start.4
  34.5 0.7 copy-start.5
  37.9 9.2 %collective-permute-start.9 = (bf16[128,1024]{1,0:T(8,128)(2,1)S(1)}, bf16[128,1024]{1,0:T(8,128)(2,1)S(1)}, u32[]{:S(2)}, u32[]{:S(2)}) collective-permute-start(bf16[128,1024]{1,0:T(8,128)(2,1)S(1)} %attend.2.refs_0_), channel_id=1, source_target_pairs={{0,8},{8,16},{16,24},{24,0},{1,9},{9,17},{17,25},{25,1},{2,10},{10... | collective-permute-start | bytes 786440 | tf_op jit(solution)/shard_map/ppermute | solution.py:24
  40.9 19.4 %copy-start.2 = (bf16[1024,512]{1,0:T(8,128)(2,1)S(1)}, bf16[1024,512]{1,0:T(8,128)(2,1)}, u32[]{:S(2)}) copy-start(bf16[1024,512]{1,0:T(8,128)(2,1)} %refs_4_.1) | copy-start | bytes 3145732
  40.9 19.4 %collective-permute-start.15 = (bf16[512,512]{1,0:T(8,128)(2,1)S(1)}, bf16[512,512]{1,0:T(8,128)(2,1)S(1)}, u32[]{:S(2)}, u32[]{:S(2)}) collective-permute-start(bf16[512,512]{1,0:T(8,128)(2,1)S(1)} %join.6), channel_id=1, source_target_pairs={{0,32},{32,64},{64,96},{96,0},{1,33},{33,65},{65,97},{97,1},{2,34}... | collective-permute-start | bytes 1572872 | tf_op jit(solution)/shard_map/ppermute | solution.py:24
  42.0 18.3 %collective-permute-start.16 = (bf16[512,512]{1,0:T(8,128)(2,1)S(1)}, bf16[512,512]{1,0:T(8,128)(2,1)S(1)}, u32[]{:S(2)}, u32[]{:S(2)}) collective-permute-start(bf16[512,512]{1,0:T(8,128)(2,1)S(1)} %join.7), channel_id=1, source_target_pairs={{0,96},{32,0},{64,32},{96,64},{1,97},{33,1},{65,33},{97,65},{2,98}... | collective-permute-start | bytes 1572872 | tf_op jit(solution)/shard_map/ppermute | solution.py:24
  44.4 8.3 %collective-permute-start.22 = (bf16[128,1024]{1,0:T(8,128)(2,1)S(1)}, bf16[128,1024]{1,0:T(8,128)(2,1)S(1)}, u32[]{:S(2)}, u32[]{:S(2)}) collective-permute-start(bf16[128,1024]{1,0:T(8,128)(2,1)S(1)} %attend.3.refs_1_), channel_id=1, source_target_pairs={{0,8},{8,16},{16,24},{24,0},{1,9},{9,17},{17,25},{25,1},{2,10},{10... | collective-permute-start | bytes 786440 | tf_op jit(solution)/shard_map/ppermute | solution.py:24
  45.7 10.5 %collective-permute-start.11 = (bf16[128,1024]{1,0:T(8,128)(2,1)S(1)}, bf16[128,1024]{1,0:T(8,128)(2,1)S(1)}, u32[]{:S(2)}, u32[]{:S(2)}) collective-permute-start(bf16[128,1024]{1,0:T(8,128)(2,1)S(1)} %attend.3.refs_1_), channel_id=1, source_target_pairs={{0,24},{8,0},{16,8},{24,16},{1,25},{9,1},{17,9},{25,17},{2,26},{10... | collective-permute-start | bytes 786440 | tf_op jit(solution)/shard_map/ppermute | solution.py:24
  47.1 13.2 %collective-permute-start.23 = (bf16[128,1024]{1,0:T(8,128)(2,1)S(1)}, bf16[128,1024]{1,0:T(8,128)(2,1)S(1)}, u32[]{:S(2)}, u32[]{:S(2)}) collective-permute-start(bf16[128,1024]{1,0:T(8,128)(2,1)S(1)} %attend.2.refs_0_), channel_id=1, source_target_pairs={{0,24},{8,0},{16,8},{24,16},{1,25},{9,1},{17,9},{25,17},{2,26},{10... | collective-permute-start | bytes 786440 | tf_op jit(solution)/shard_map/ppermute | solution.py:24
  52.7 10.1 %collective-permute-start.10 = (bf16[128,1024]{1,0:T(8,128)(2,1)S(1)}, bf16[128,1024]{1,0:T(8,128)(2,1)S(1)}, u32[]{:S(2)}, u32[]{:S(2)}) collective-permute-start(bf16[128,1024]{1,0:T(8,128)(2,1)S(1)} %collective-permute-done.9.refs_0_), channel_id=1, source_target_pairs={{0,8},{8,16},{16,24},{24,0},{1,9},{9,17},{17,25},{25,1},{2,10},{10... | collective-permute-start | bytes 786440 | tf_op jit(solution)/shard_map/ppermute | solution.py:24
  56.1 7.6 %collective-permute-start.12 = (bf16[128,1024]{1,0:T(8,128)(2,1)S(1)}, bf16[128,1024]{1,0:T(8,128)(2,1)S(1)}, u32[]{:S(2)}, u32[]{:S(2)}) collective-permute-start(bf16[128,1024]{1,0:T(8,128)(2,1)S(1)} %collective-permute-done.11.refs_3_), channel_id=1, source_target_pairs={{0,24},{8,0},{16,8},{24,16},{1,25},{9,1},{17,9},{25,17},{2,26},{10... | collective-permute-start | bytes 786440 | tf_op jit(solution)/shard_map/ppermute | solution.py:24
  62.7 3.5 %collective-permute-start.24 = (bf16[4,256,512]{2,1,0:T(8,128)(2,1)S(1)}, bf16[4,256,512]{2,1,0:T(8,128)(2,1)S(1)}, u32[]{:S(2)}, u32[]{:S(2)}) collective-permute-start(bf16[4,256,512]{2,1,0:T(8,128)(2,1)S(1)} %get-tuple-element.50), channel_id=1, source_target_pairs={{0,1},{1,0},{2,3},{3,2},{4,5},{5,4},{6,7},{7,6},{8,9},{9,8},{10,11... | collective-permute-start | bytes 3145736 | tf_op jit(solution)/shard_map/ppermute | solution.py:28
  66.1 2.7 %collective-permute-start.17 = (bf16[4,256,512]{2,1,0:T(8,128)(2,1)S(1)}, bf16[4,256,512]{2,1,0:T(8,128)(2,1)S(1)}, u32[]{:S(2)}, u32[]{:S(2)}) collective-permute-start(bf16[4,256,512]{2,1,0:T(8,128)(2,1)S(1)} %get-tuple-element.44), channel_id=1, source_target_pairs={{0,1},{1,0},{2,3},{3,2},{4,5},{5,4},{6,7},{7,6},{8,9},{9,8},{10,11... | collective-permute-start | bytes 3145736 | tf_op jit(solution)/shard_map/ppermute | solution.py:28
  66.7 7.7 %collective-permute-start.26 = (bf16[256,512]{1,0:T(8,128)(2,1)S(1)}, bf16[256,512]{1,0:T(8,128)(2,1)S(1)}, u32[]{:S(2)}, u32[]{:S(2)}) collective-permute-start(bf16[256,512]{1,0:T(8,128)(2,1)S(1)} %get-tuple-element.54), channel_id=1, source_target_pairs={{0,2},{1,7},{2,4},{3,1},{4,6},{5,3},{6,0},{7,5},{8,10},{9,15},{10,... | collective-permute-start | bytes 786440 | tf_op jit(solution)/shard_map/ppermute | solution.py:258
  69.4 7.8 %collective-permute-start.19 = (bf16[256,512]{1,0:T(8,128)(2,1)S(1)}, bf16[256,512]{1,0:T(8,128)(2,1)S(1)}, u32[]{:S(2)}, u32[]{:S(2)}) collective-permute-start(bf16[256,512]{1,0:T(8,128)(2,1)S(1)} %get-tuple-element.48), channel_id=1, source_target_pairs={{0,2},{1,7},{2,4},{3,1},{4,6},{5,3},{6,0},{7,5},{8,10},{9,15},{10,... | collective-permute-start | bytes 786440 | tf_op jit(solution)/shard_map/ppermute | solution.py:258
  74.4 7.7 %collective-permute-start.27 = (bf16[256,512]{1,0:T(8,128)(2,1)S(1)}, bf16[256,512]{1,0:T(8,128)(2,1)S(1)}, u32[]{:S(2)}, u32[]{:S(2)}) collective-permute-start(bf16[256,512]{1,0:T(8,128)(2,1)S(1)} %add_convert_fusion.2), channel_id=1, source_target_pairs={{0,2},{1,7},{2,4},{3,1},{4,6},{5,3},{6,0},{7,5},{8,10},{9,15},{10,... | collective-permute-start | bytes 786440 | tf_op jit(solution)/shard_map/ppermute | solution.py:258
  77.3 7.7 %collective-permute-start.20 = (bf16[256,512]{1,0:T(8,128)(2,1)S(1)}, bf16[256,512]{1,0:T(8,128)(2,1)S(1)}, u32[]{:S(2)}, u32[]{:S(2)}) collective-permute-start(bf16[256,512]{1,0:T(8,128)(2,1)S(1)} %add_convert_fusion.5), channel_id=1, source_target_pairs={{0,2},{1,7},{2,4},{3,1},{4,6},{5,3},{6,0},{7,5},{8,10},{9,15},{10,... | collective-permute-start | bytes 786440 | tf_op jit(solution)/shard_map/ppermute | solution.py:258
  77.7 8.9 %collective-permute-start.25 = (bf16[256,512]{1,0:T(8,128)(2,1)S(1)}, bf16[256,512]{1,0:T(8,128)(2,1)S(1)}, u32[]{:S(2)}, u32[]{:S(2)}) collective-permute-start(bf16[256,512]{1,0:T(8,128)(2,1)S(1)} %get-tuple-element.51), channel_id=1, source_target_pairs={{0,24},{1,8},{2,26},{3,10},{4,28},{5,12},{6,30},{7,14},{8,0},{9,16... | collective-permute-start | bytes 786440 | tf_op jit(solution)/shard_map/ppermute | solution.py:268
  78.5 17.6 %collective-permute-start.18 = (bf16[256,512]{1,0:T(8,128)(2,1)S(1)}, bf16[256,512]{1,0:T(8,128)(2,1)S(1)}, u32[]{:S(2)}, u32[]{:S(2)}) collective-permute-start(bf16[256,512]{1,0:T(8,128)(2,1)S(1)} %get-tuple-element.45), channel_id=1, source_target_pairs={{0,0},{1,16},{2,2},{3,18},{4,4},{5,20},{6,6},{7,22},{8,8},{9,24},{... | collective-permute-start | bytes 786440 | tf_op jit(solution)/shard_map/ppermute | solution.py:268
  82.2 13.8 %collective-permute-start.28 = (bf16[256,512]{1,0:T(8,128)(2,1)S(1)}, bf16[256,512]{1,0:T(8,128)(2,1)S(1)}, u32[]{:S(2)}, u32[]{:S(2)}) collective-permute-start(bf16[256,512]{1,0:T(8,128)(2,1)S(1)} %add_convert_fusion.1), channel_id=1, source_target_pairs={{0,26},{1,14},{2,28},{3,8},{4,30},{5,10},{6,24},{7,12},{8,2},{9,22... | collective-permute-start | bytes 786440 | tf_op jit(solution)/shard_map/ppermute | solution.py:268
  85.0 11.1 %collective-permute-start.21 = (bf16[256,512]{1,0:T(8,128)(2,1)S(1)}, bf16[256,512]{1,0:T(8,128)(2,1)S(1)}, u32[]{:S(2)}, u32[]{:S(2)}) collective-permute-start(bf16[256,512]{1,0:T(8,128)(2,1)S(1)} %add_convert_fusion.4), channel_id=1, source_target_pairs={{0,2},{1,22},{2,4},{3,16},{4,6},{5,18},{6,0},{7,20},{8,10},{9,30},... | collective-permute-start | bytes 786440 | tf_op jit(solution)/shard_map/ppermute | solution.py:268

commit v4 on v3

--- a/solution.py
+++ b/solution.py
@@ -66,7 +66,7 @@
     )(positions, *blocks, *old)
 
 
-def attend_kernel(first_row, pos, lengths, spans, q, ks, vs, out):
+def attend_kernel(pos, lengths, spans, q, ks, vs, out):
     z, x = z_index(), lax.axis_index("x")
     heads, slots = out.shape[1] // DH, ks.shape[0]
     runs = out.shape[0] // RUN
@@ -91,7 +91,7 @@
         return low, high
 
     scale = math.log2(math.e) / math.sqrt(DH)
-    first_run = (z * 4 + x) * (q.shape[0] // RUN) + first_row // RUN
+    first_run = (z * 4 + x) * runs
 
     def block(i, _):
         p0 = pos[first_run + i]
@@ -114,7 +114,7 @@
             for g in range(groups):
                 columns = [(g * per + h) * DH for h in range(per)]
                 queries = jnp.concatenate(
-                    [q[pl.ds(first_row + row, RUN), c : c + DH] for c in columns], axis=0
+                    [q[pl.ds(row, RUN), c : c + DH] for c in columns], axis=0
                 )
                 s = lax.dot_general(
                     queries,
@@ -150,10 +150,10 @@
     lax.fori_loop(0, runs, block, 0)
 
 
-def attend(first_row, rows, positions, lengths, spans, q, ordered):
-    width = q.shape[1]
-    return pl.pallas_call(
-        functools.partial(attend_kernel, first_row),
+def attend(positions, lengths, spans, q, ordered):
+    rows, width = q.shape
+    return pl.pallas_call(
+        attend_kernel,
         out_shape=jax.ShapeDtypeStruct((rows, width), jnp.bfloat16),
         in_specs=[SMEM] * 3 + [VMEM] * 3,
         out_specs=VMEM,
@@ -185,40 +185,73 @@
     )(*pieces)
 
 
-def project_kernel(core_zero, core_one, *refs):
-    pieces = refs[: len(core_zero) + len(core_one)]
-    weights = refs[len(pieces) : -3]
-    keep, send, rows = refs[-3:]
+BLOCKS = ((0,), (1,), (2,), (3, 4))
+
+
+def product(rows, weights, parts):
+    total, at = None, 0
+    for part in parts:
+        depth = weights[part].shape[0]
+        share = jnp.dot(rows[:, at : at + depth], weights[part][...], preferred_element_type=jnp.float32)
+        total = share if total is None else total + share
+        at += depth
+    return total.astype(jnp.bfloat16)
+
+
+def near_kernel(left, right, *refs):
+    weights, (keep, send, rows) = refs[:-3], refs[-3:]
     core = lax.axis_index("c")
-    for mine, names in ((core, core_zero), (1 - core, core_one)):
-        at = 0
-        for n in names:
-            rows[mine, at : at + pieces[n].shape[0], :] = pieces[n][...]
-            at += pieces[n].shape[0]
+    for at in range(0, left.shape[0], 2 * RUN):
+        rows[core, at : at + 2 * RUN, :] = left[at : at + 2 * RUN, :]
+        rows[1 - core, at : at + 2 * RUN, :] = right[at : at + 2 * RUN, :]
     for target, which in ((send, 1), (keep, 0)):
         for n, parts in enumerate(BLOCKS):
-            total, at = None, 0
-            for part in parts:
-                depth = weights[part].shape[0]
-                share = jnp.dot(rows[which, :, at : at + depth], weights[part][...], preferred_element_type=jnp.float32)
-                total = share if total is None else total + share
-                at += depth
-            target[n] = total.astype(jnp.bfloat16)
-
-
-BLOCKS = ((0,), (1,), (2,), (3, 4))
-
-
-def project(pieces, core_zero, core_one, weights):
-    count, depth = sum(pieces[n].shape[0] for n in core_zero), pieces[0].shape[1]
-    width = weights[0].shape[1]
+            target[n] = product(rows.at[which], weights, parts)
+
+
+def own_kernel(rows, *refs):
+    weights, out = refs[:-1], refs[-1]
+    for n, parts in enumerate(BLOCKS):
+        out[n] = product(rows, weights, parts)
+
+
+def far_kernel(upper, lower, own, *refs):
+    weights, (keep, send, rows) = refs[:-3], refs[-3:]
+    core = lax.axis_index("c")
+    half = upper.shape[0]
+    rows[:half, :] = upper[...]
+    rows[half:, :] = lower[...]
+
+    def fill(target, other):
+        other[...] = own[...]
+        for n, parts in enumerate(BLOCKS):
+            target[n] = product(rows, weights, parts)
+
+    @pl.when(core == 0)
+    def _():
+        fill(send, keep)
+
+    @pl.when(core == 1)
+    def _():
+        fill(keep, send)
+
+
+def project(kernel, pieces, weights):
+    depth, width = weights[0].shape
+    count = 2 * pieces[0].shape[0] if kernel is far_kernel else pieces[0].shape[0]
     result = jax.ShapeDtypeStruct((len(BLOCKS), count, width), jnp.bfloat16)
-    return pl.pallas_call(
-        functools.partial(project_kernel, core_zero, core_one),
-        out_shape=[result, result],
+    results = 1 if kernel is own_kernel else 2
+    scratch = {
+        own_kernel: [],
+        near_kernel: [pltpu.VMEM((2, count, depth), jnp.bfloat16)],
+        far_kernel: [pltpu.VMEM((count, depth), jnp.bfloat16)],
+    }
+    return pl.pallas_call(
+        kernel,
+        out_shape=[result] * results,
         in_specs=[VMEM] * (len(pieces) + len(weights)),
-        out_specs=[VMEM, VMEM],
-        scratch_shapes=[pltpu.VMEM((2, count, depth), jnp.bfloat16)],
+        out_specs=[VMEM] * results,
+        scratch_shapes=scratch[kernel],
         compiler_params=pltpu.CompilerParams(vmem_limit_bytes=16 * 2**20),
         cost_estimate=pl.CostEstimate(
             flops=4 * count * depth * width * len(BLOCKS), bytes_accessed=4 * 2**20, transcendentals=0
@@ -277,6 +310,14 @@
 
 def after(value, *others):
     return lax.optimization_barrier((value, *others))[0]
+
+
+def halves(left, right, axis):
+    half = left.shape[0] // 2
+    return (
+        shift(join((left,), ((0, half),)), axis, 1),
+        shift(join((right,), ((half, 2 * half),)), axis, -1),
+    )
 
 
 def shards(queries, keys, values, positions, lengths, spans, weight):
@@ -296,35 +337,29 @@
     def at_x(dx, blocks=line_blocks):
         return [(dz, dx, which) for dz, which in blocks]
 
-    own = [(0, 0), (0, 1)]
-    ordered = place(runs, (at_x(0, own), at_x(0), at_x(3, own), at_x(1, own)), (kv, line, left, right))
+    here = [(0, 0), (0, 1)]
+    ordered = place(runs, (at_x(0, here), at_x(0), at_x(3, here), at_x(1, here)), (kv, line, left, right))
     left2 = shift(join((line_left, left), ((0, 3 * count), (0, count))), "x", 1)
     right2 = shift(join((line_right, right), ((3 * count, 6 * count), (count, 2 * count))), "x", -1)
     ordered = place(runs, (at_x(3), at_x(1)), (line_left, line_right), ordered)
     ordered = place(
         runs,
-        (at_x(2, line_blocks[:3] + own[:1]), at_x(2, line_blocks[3:] + own[1:])),
+        (at_x(2, line_blocks[:3] + here[:1]), at_x(2, line_blocks[3:] + here[1:])),
         (left2, right2),
         ordered,
     )
 
-    half = count // 2
-    upper = attend(0, half, runs, lengths, spans, queries, ordered)
-    lower = attend(half, half, runs, lengths, spans, after(queries, upper), ordered)
-    upper_left, upper_right = shift(upper, "x", 1), shift(upper, "x", -1)
-    lower_left, lower_right = shift(lower, "x", 1), shift(lower, "x", -1)
-
-    middle = weight.shape[0] // 2
-    weight_left_far = shift(join((after(weight_left, lower),), ((0, middle),)), Z, 1)
-    weight_right_far = shift(join((after(weight_right, lower),), ((middle, 2 * middle),)), Z, -1)
-    upper_far, lower_far = shift(upper_left, "x", 1), shift(lower_right, "x", -1)
-
-    weights = (weight, weight_left, weight_right, weight_left_far, weight_right_far)
-    rows = (upper_left, lower_left, upper_right, lower_right)
-    keep, send = project(rows, (0, 1), (2, 3), weights)
+    own = attend(runs, lengths, spans, queries, ordered)
+    rows_left, rows_right = shift(own, "x", 1), shift(own, "x", -1)
+    rows_far = halves(rows_left, rows_right, "x")
+    weight_far = halves(after(weight_left, own), after(weight_right, own), Z)
+
+    weights = (weight, weight_left, weight_right, *weight_far)
+    (own,) = project(own_kernel, (own,), weights)
+    rows = (after(rows_left, own), rows_right)
+    keep, send = project(near_kernel, rows, weights)
     near = combine(keep, swap_cores(send))
-    rows = (upper, lower, upper_far, lower_far)
-    keep, send = project(rows, (0, 1), (2, 3), weights)
+    keep, send = project(far_kernel, (*rows_far, own), weights)
     mixed = combine(keep, swap_cores(send))
 
     near = plus(*sum_shares(near, (-1, 1)))

time: 97.2 us -> 92.9 us (0.956)
  waiting for transfers between devices: 41.9 us -> 39.3 us
  starting transfers between devices: 34.4 us -> 32.6 us
    ppermute x19 -> x17, waiting for transfers between devices: 23.1 us -> 19.9 us  [shift(): return lax.ppermute(value, axis, [(i, (i + step) % 4) for i in range(4)])]
    ppermute x19 -> x17, starting transfers between devices: 24.5 us -> 23.4 us  [shift(): return lax.ppermute(value, axis, [(i, (i + step) % 4) for i in range(4)])]
  transfers between devices with their start and end apart: 29 -> 27, of which waited for: 16 -> 14; matrix products, arithmetic and copies ran while one was open for 2% -> 2% of each run, Pallas kernels for 16% -> 16%
where the time goes in v4:
time: 92.9 us; the launch traced here: 92.1 us
  waiting for transfers between devices  39.3 us (42%)
  starting transfers between devices  32.6 us (35%)
  Pallas kernels  14.5 us (16%)
  local copies, waits for them, and re-layouts  4 us (4%)
  other arithmetic  1.36 us (1%)
    ppermute x17, starting transfers between devices, shift(): return lax.ppermute(value, axis, [(i, (i + step) % 4) for i in range(4)])  23.4 us
    ppermute x17, waiting for transfers between devices, shift(): return lax.ppermute(value, axis, [(i, (i + step) % 4) for i in range(4)])  19.9 us
    ppermute x4, waiting for transfers between devices, home(): return lax.ppermute(value, ('x', 'y', 'c'), pairs)  10.4 us
    ppermute x4, waiting for transfers between devices, relay(): return lax.ppermute(value, (axis, 'c'), pairs)  8.51 us
    pallas_call x3, Pallas kernels, project(): pl.pallas_call(kernel, out_shape=[result] * results, in_specs=[VMEM] * (l...  4.97 us
    ppermute x4, starting transfers between devices, home(): return lax.ppermute(value, ('x', 'y', 'c'), pairs)  4.91 us
    pallas_call x1, Pallas kernels, attend(): pl.pallas_call(attend_kernel, out_shape=jax.ShapeDtypeStruct((rows, width...  4.44 us
    ppermute x4, starting transfers between devices, relay(): return lax.ppermute(value, (axis, 'c'), pairs)  4.16 us
  transfers between devices with their start and end apart: 27, of which 14 were waited for; matrix products, arithmetic and copies ran while one was open for 2% of the time, Pallas kernels for 16%

profile of v4, /device:TPU:6, one launch (start us, length us, event | category | flops | bytes accessed | tf_op | source)
XLA Modules:
  0.0 92.1 jit_solution(4944948362773650818)
XLA Ops:
  0.0 0.9 constant_dynamic-update-slice_fusion.1
  0.9 4.0 %collective-permute-start.2 = (bf16[512,128]{1,0:T(8,128)(2,1)S(1)}, bf16[512,128]{1,0:T(8,128)(2,1)S(1)}, u32[]{:S(2)}, u32[]{:S(2)}) collective-permute-start(bf16[512,128]{1,0:T(8,128)(2,1)S(1)} %constant_dynamic-update-slice_fusion.refs_0_), channel_id=1, source_target_pairs={{0,64},{32,96},{64,0},{96,32},{1,65},{33,97},{65,1},{97,33},{2,66}... | collective-permute-start | bytes 393224 | tf_op jit(solution)/shard_map/ppermute | solution.py:24
  4.9 0.7 collective-permute-start.1
  5.6 1.3 %collective-permute-start = (bf16[512,128]{1,0:T(8,128)(2,1)S(1)}, bf16[512,128]{1,0:T(8,128)(2,1)S(1)}, u32[]{:S(2)}, u32[]{:S(2)}) collective-permute-start(bf16[512,128]{1,0:T(8,128)(2,1)S(1)} %constant_dynamic-update-slice_fusion.refs_0_), channel_id=1, source_target_pairs={{0,32},{32,64},{64,96},{96,0},{1,33},{33,65},{65,97},{97,1},{2,34}... | collective-permute-start | bytes 393224 | tf_op jit(solution)/shard_map/ppermute | solution.py:24
  6.9 0.5 collective-permute-start.3
  7.4 1.5 %collective-permute-start.4 = (bf16[512,128]{1,0:T(8,128)(2,1)S(1)}, bf16[512,128]{1,0:T(8,128)(2,1)S(1)}, u32[]{:S(2)}, u32[]{:S(2)}) collective-permute-start(bf16[512,128]{1,0:T(8,128)(2,1)S(1)} %constant_dynamic-update-slice_fusion.refs_0_), channel_id=1, source_target_pairs={{0,24},{8,0},{16,8},{24,16},{1,25},{9,1},{17,9},{25,17},{2,26},{10... | collective-permute-start | bytes 393224 | tf_op jit(solution)/shard_map/ppermute | solution.py:24
  8.9 3.0 %collective-permute-done.1 = bf16[512,128]{1,0:T(8,128)(2,1)S(1)} collective-permute-done((bf16[512,128]{1,0:T(8,128)(2,1)S(1)}, bf16[512,128]{1,0:T(8,128)(2,1)S(1)}, u32[]{:S(2)}, u32[]{:S(2)}) %collective-permute-start.1) | collective-permute-done | bytes 131104 | tf_op jit(solution)/shard_map/ppermute | solution.py:24
  12.0 1.5 %collective-permute-done.4.refs_1_.refs_3_ = bf16[512,128]{1,0:T(8,128)(2,1)S(1)} collective-permute-done((bf16[512,128]{1,0:T(8,128)(2,1)S(1)}, bf16[512,128]{1,0:T(8,128)(2,1)S(1)}, u32[]{:S(2)}, u32[]{:S(2)}) %collective-permute-start.4) | collective-permute-done | bytes 131104 | tf_op jit(solution)/shard_map/ppermute | solution.py:24
  13.8 1.7 %collective-permute-start.7 = (bf16[1536,128]{1,0:T(8,128)(2,1)S(1)}, bf16[1536,128]{1,0:T(8,128)(2,1)S(1)}, u32[]{:S(2)}, u32[]{:S(2)}) collective-permute-start(bf16[1536,128]{1,0:T(8,128)(2,1)S(1)} %pad_maximum_fusion.refs_1_), channel_id=1, source_target_pairs={{0,24},{8,0},{16,8},{24,16},{1,25},{9,1},{17,9},{25,17},{2,26},{10... | collective-permute-start | bytes 1179656 | tf_op jit(solution)/shard_map/ppermute | solution.py:24
  15.6 1.0 %collective-permute-start.13 = (bf16[1024,512]{1,0:T(8,128)(2,1)}, bf16[1024,512]{1,0:T(8,128)(2,1)S(1)}, u32[]{:S(2)}, u32[]{:S(2)}) collective-permute-start(bf16[1024,512]{1,0:T(8,128)(2,1)} %refs_0_.2), channel_id=1, source_target_pairs={{0,32},{32,64},{64,96},{96,0},{1,33},{33,65},{65,97},{97,1},{2,34}... | collective-permute-start | bytes 3145736 | tf_op jit(solution)/shard_map/ppermute | solution.py:24
  16.6 2.2 %collective-permute-start.14 = (bf16[1024,512]{1,0:T(8,128)(2,1)}, bf16[1024,512]{1,0:T(8,128)(2,1)S(1)}, u32[]{:S(2)}, u32[]{:S(2)}) collective-permute-start(bf16[1024,512]{1,0:T(8,128)(2,1)} %refs_0_.2), channel_id=1, source_target_pairs={{0,96},{32,0},{64,32},{96,64},{1,97},{33,1},{65,33},{97,65},{2,98}... | collective-permute-start | bytes 3145736 | tf_op jit(solution)/shard_map/ppermute | solution.py:24
  18.8 3.6 %collective-permute-done.5.refs_0_ = bf16[1536,128]{1,0:T(8,128)(2,1)S(1)} collective-permute-done((bf16[1536,128]{1,0:T(8,128)(2,1)S(1)}, bf16[1536,128]{1,0:T(8,128)(2,1)S(1)}, u32[]{:S(2)}, u32[]{:S(2)}) %collective-permute-start.5) | collective-permute-done | bytes 393248 | tf_op jit(solution)/shard_map/ppermute | solution.py:24
  22.4 0.7 join.6
  23.1 1.5 %collective-permute-start.6 = (bf16[1024,128]{1,0:T(8,128)(2,1)}, bf16[1024,128]{1,0:T(8,128)(2,1)}, u32[]{:S(2)}, u32[]{:S(2)}) collective-permute-start(bf16[1024,128]{1,0:T(8,128)(2,1)} %join.6), channel_id=1, source_target_pairs={{0,8},{8,16},{16,24},{24,0},{1,9},{9,17},{17,25},{25,1},{2,10},{10... | collective-permute-start | bytes 786440 | tf_op jit(solution)/shard_map/ppermute | solution.py:24
  24.6 0.7 join.7
  25.4 0.5 collective-permute-start.8
  25.9 0.7 reshape.3
  26.6 0.9 slice_reduce_fusion.pos
  27.4 0.9 copy-done.1
  28.3 0.7 place.3
  29.0 0.7 place.4
  29.8 3.4 %collective-permute-done.8.refs_1_ = bf16[1024,128]{1,0:T(8,128)(2,1)} collective-permute-done((bf16[1024,128]{1,0:T(8,128)(2,1)}, bf16[1024,128]{1,0:T(8,128)(2,1)}, u32[]{:S(2)}, u32[]{:S(2)}) %collective-permute-start.8) | collective-permute-done | bytes 262176 | tf_op jit(solution)/shard_map/ppermute | solution.py:24
  33.3 1.2 %place.5 = (bf16[4096,128]{1,0:T(8,128)(2,1)S(1)}, bf16[4096,128]{1,0:T(8,128)(2,1)S(1)}) custom-call(s32[64]{0:T(128)S(1)} %slice_reduce_fusion.pos, bf16[1024,128]{1,0:T(8,128)(2,1)} %collective-permute-done.6.refs_0_, bf16[1024,128]{1,0:T(8,128)(2,1)} %collective-permute-done.8.refs_1_, ...), custom_call_target="tpu_custom_call", output_to_operand_aliasing={{0}: (3, {}), {1}: (4, {})} | custom-call | bytes 2097152 | tf_op jit(solution)/shard_map/place/pallas_call | solution.py:57
  34.5 0.6 copy-done.4
  35.1 4.4 %attend.1.rows = bf16[256,1024]{1,0:T(8,128)(2,1)S(1)} custom-call(s32[64]{0:T(128)S(1)} %slice_reduce_fusion.pos, s32[8]{0:T(128)S(1)} %copy-done.5, s32[2,4]{1,0:T(2,128)S(1)} %copy-done.4, bf16[256,1024]{1,0:T(8,128)(2,1)S(1)} %copy-done.3, bf16[4096,128]{1,0:T(8,128)(2,1)S(1)} %get-tuple-element.37.ks, bf16[4096,128]{1,0:T(8,128)(2,1)S(1)} %get-tuple-element.38.vs), custom_call_target="tpu_custom_call" | custom-call | flops 6442450944 | bytes 4194304 | tf_op jit(solution)/shard_map/attend/pallas_call | solution.py:155
  39.7 2.0 %collective-permute-start.11 = (bf16[256,1024]{1,0:T(8,128)(2,1)S(1)}, bf16[256,1024]{1,0:T(8,128)(2,1)S(1)}, u32[]{:S(2)}, u32[]{:S(2)}) collective-permute-start(bf16[256,1024]{1,0:T(8,128)(2,1)S(1)} %attend.1.rows), channel_id=1, source_target_pairs={{0,24},{8,0},{16,8},{24,16},{1,25},{9,1},{17,9},{25,17},{2,26},{10... | collective-permute-start | bytes 1572872 | tf_op jit(solution)/shard_map/ppermute | solution.py:24
  41.7 1.6 %collective-permute-start.15 = (bf16[512,512]{1,0:T(8,128)(2,1)S(1)}, bf16[512,512]{1,0:T(8,128)(2,1)S(1)}, u32[]{:S(2)}, u32[]{:S(2)}) collective-permute-start(bf16[512,512]{1,0:T(8,128)(2,1)S(1)} %join.10), channel_id=1, source_target_pairs={{0,32},{32,64},{64,96},{96,0},{1,33},{33,65},{65,97},{97,1},{2,34}... | collective-permute-start | bytes 1572872 | tf_op jit(solution)/shard_map/ppermute | solution.py:24
  43.4 2.0 %collective-permute-start.16 = (bf16[512,512]{1,0:T(8,128)(2,1)S(1)}, bf16[512,512]{1,0:T(8,128)(2,1)S(1)}, u32[]{:S(2)}, u32[]{:S(2)}) collective-permute-start(bf16[512,512]{1,0:T(8,128)(2,1)S(1)} %join.11), channel_id=1, source_target_pairs={{0,96},{32,0},{64,32},{96,64},{1,97},{33,1},{65,33},{97,65},{2,98}... | collective-permute-start | bytes 1572872 | tf_op jit(solution)/shard_map/ppermute | solution.py:24
  45.4 6.3 %collective-permute-done.9.refs_0_.left = bf16[256,1024]{1,0:T(8,128)(2,1)S(1)} collective-permute-done((bf16[256,1024]{1,0:T(8,128)(2,1)S(1)}, bf16[256,1024]{1,0:T(8,128)(2,1)S(1)}, u32[]{:S(2)}, u32[]{:S(2)}) %collective-permute-start.9) | collective-permute-done | bytes 524320 | tf_op jit(solution)/shard_map/ppermute | solution.py:24
  51.8 2.3 %collective-permute-start.12 = (bf16[128,1024]{1,0:T(8,128)(2,1)S(1)}, bf16[128,1024]{1,0:T(8,128)(2,1)S(1)}, u32[]{:S(2)}, u32[]{:S(2)}) collective-permute-start(bf16[128,1024]{1,0:T(8,128)(2,1)S(1)} %join.9), channel_id=1, source_target_pairs={{0,24},{8,0},{16,8},{24,16},{1,25},{9,1},{17,9},{25,17},{2,26},{10... | collective-permute-start | bytes 786440 | tf_op jit(solution)/shard_map/ppermute | solution.py:24
  54.1 1.2 %project.3.own = bf16[4,256,512]{2,1,0:T(8,128)(2,1)S(1)} custom-call(bf16[256,1024]{1,0:T(8,128)(2,1)S(1)} %attend.1.rows, bf16[1024,512]{1,0:T(8,128)(2,1)S(1)} %copy-done.2, bf16[1024,512]{1,0:T(8,128)(2,1)S(1)} %collective-permute-done.13.refs_0_.refs_1_, bf16[1024,512]{1,0:T(8,128)(2,1)S(1)} %collective-permute-done.14.refs_0_.refs_2_, ...), custom_call_target="tpu_custom_call" | custom-call | flops 2147483648 | bytes 4194304 | tf_op jit(solution)/shard_map/project/pallas_call | solution.py:249
  55.4 2.4 %project.5 = (bf16[4,256,512]{2,1,0:T(8,128)(2,1)S(1)}, bf16[4,256,512]{2,1,0:T(8,128)(2,1)S(1)}) custom-call(bf16[256,1024]{1,0:T(8,128)(2,1)S(1)} %collective-permute-done.9.refs_0_.left, bf16[256,1024]{1,0:T(8,128)(2,1)S(1)} %collective-permute-done.11.refs_0_.right, bf16[1024,512]{1,0:T(8,128)(2,1)S(1)} %copy-done.2, ...), custom_call_target="tpu_custom_call" | custom-call | flops 2147483648 | bytes 4194304 | tf_op jit(solution)/shard_map/project/pallas_call | solution.py:249
  58.1 1.6 %collective-permute-done.12.lower = bf16[128,1024]{1,0:T(8,128)(2,1)S(1)} collective-permute-done((bf16[128,1024]{1,0:T(8,128)(2,1)S(1)}, bf16[128,1024]{1,0:T(8,128)(2,1)S(1)}, u32[]{:S(2)}, u32[]{:S(2)}) %collective-permute-start.12) | collective-permute-done | bytes 262176 | tf_op jit(solution)/shard_map/ppermute | solution.py:24
  59.7 1.3 %project.4 = (bf16[4,256,512]{2,1,0:T(8,128)(2,1)S(1)}, bf16[4,256,512]{2,1,0:T(8,128)(2,1)S(1)}) custom-call(bf16[128,1024]{1,0:T(8,128)(2,1)S(1)} %collective-permute-done.10.upper, bf16[128,1024]{1,0:T(8,128)(2,1)S(1)} %collective-permute-done.12.lower, bf16[4,256,512]{2,1,0:T(8,128)(2,1)S(1)} %project.3.own, bf16[1024,512]{1,0:T(8,128)(2,1)S(1)} %copy-done.2, ...), custom_call_target="tpu_custom_call" | custom-call | flops 2147483648 | bytes 4194304 | tf_op jit(solution)/shard_map/project/pallas_call | solution.py:249
  61.1 0.5 combine.3
  61.7 1.6 %collective-permute-start.24 = (bf16[256,512]{1,0:T(8,128)(2,1)S(1)}, bf16[256,512]{1,0:T(8,128)(2,1)S(1)}, u32[]{:S(2)}, u32[]{:S(2)}) collective-permute-start(bf16[256,512]{1,0:T(8,128)(2,1)S(1)} %get-tuple-element.54), channel_id=1, source_target_pairs={{0,2},{1,7},{2,4},{3,1},{4,6},{5,3},{6,0},{7,5},{8,10},{9,15},{10,... | collective-permute-start | bytes 786440 | tf_op jit(solution)/shard_map/ppermute | solution.py:291
  63.3 0.5 collective-permute-done.17.got
  63.8 0.5 combine.2
  64.3 1.6 %collective-permute-start.19 = (bf16[256,512]{1,0:T(8,128)(2,1)S(1)}, bf16[256,512]{1,0:T(8,128)(2,1)S(1)}, u32[]{:S(2)}, u32[]{:S(2)}) collective-permute-start(bf16[256,512]{1,0:T(8,128)(2,1)S(1)} %get-tuple-element.47), channel_id=1, source_target_pairs={{0,2},{1,7},{2,4},{3,1},{4,6},{5,3},{6,0},{7,5},{8,10},{9,15},{10,... | collective-permute-start | bytes 786440 | tf_op jit(solution)/shard_map/ppermute | solution.py:291
  66.0 3.4 %collective-permute-done.24 = bf16[256,512]{1,0:T(8,128)(2,1)S(1)} collective-permute-done((bf16[256,512]{1,0:T(8,128)(2,1)S(1)}, bf16[256,512]{1,0:T(8,128)(2,1)S(1)}, u32[]{:S(2)}, u32[]{:S(2)}) %collective-permute-start.24) | collective-permute-done | bytes 262176 | tf_op jit(solution)/shard_map/ppermute | solution.py:291
  69.4 0.4 collective-permute-start.25
  69.8 2.3 %collective-permute-done.19 = bf16[256,512]{1,0:T(8,128)(2,1)S(1)} collective-permute-done((bf16[256,512]{1,0:T(8,128)(2,1)S(1)}, bf16[256,512]{1,0:T(8,128)(2,1)S(1)}, u32[]{:S(2)}, u32[]{:S(2)}) %collective-permute-start.19) | collective-permute-done | bytes 262176 | tf_op jit(solution)/shard_map/ppermute | solution.py:291
  72.6 2.1 %collective-permute-start.23 = (bf16[256,512]{1,0:T(8,128)(2,1)S(1)}, bf16[256,512]{1,0:T(8,128)(2,1)S(1)}, u32[]{:S(2)}, u32[]{:S(2)}) collective-permute-start(bf16[256,512]{1,0:T(8,128)(2,1)S(1)} %get-tuple-element.51), channel_id=1, source_target_pairs={{0,24},{1,8},{2,26},{3,10},{4,28},{5,12},{6,30},{7,14},{8,0},{9,16... | collective-permute-start | bytes 786440 | tf_op jit(solution)/shard_map/ppermute | solution.py:301
  74.7 1.9 %collective-permute-start.18 = (bf16[256,512]{1,0:T(8,128)(2,1)S(1)}, bf16[256,512]{1,0:T(8,128)(2,1)S(1)}, u32[]{:S(2)}, u32[]{:S(2)}) collective-permute-start(bf16[256,512]{1,0:T(8,128)(2,1)S(1)} %get-tuple-element.44), channel_id=1, source_target_pairs={{0,0},{1,16},{2,2},{3,18},{4,4},{5,20},{6,6},{7,22},{8,8},{9,24},{... | collective-permute-start | bytes 786440 | tf_op jit(solution)/shard_map/ppermute | solution.py:301
  77.4 2.4 %collective-permute-done.20 = bf16[256,512]{1,0:T(8,128)(2,1)S(1)} collective-permute-done((bf16[256,512]{1,0:T(8,128)(2,1)S(1)}, bf16[256,512]{1,0:T(8,128)(2,1)S(1)}, u32[]{:S(2)}, u32[]{:S(2)}) %collective-permute-start.20) | collective-permute-done | bytes 262176 | tf_op jit(solution)/shard_map/ppermute | solution.py:291
  79.9 0.6 collective-permute-start.21
  80.5 10.4 %collective-permute-done.26 = bf16[256,512]{1,0:T(8,128)(2,1)S(1)} collective-permute-done((bf16[256,512]{1,0:T(8,128)(2,1)S(1)}, bf16[256,512]{1,0:T(8,128)(2,1)S(1)}, u32[]{:S(2)}, u32[]{:S(2)}) %collective-permute-start.26) | collective-permute-done | bytes 262176 | tf_op jit(solution)/shard_map/ppermute | solution.py:301
  91.1 0.9 %maximum_select_fusion = bf16[256,1024]{1,0:T(8,128)(2,1)} fusion(bf16[256,512]{1,0:T(8,128)(2,1)S(1)} %add_convert_fusion, bf16[256,512]{1,0:T(8,128)(2,1)S(1)} %add_convert_fusion.3, pred[]{:T(512)S(6)} %eq.3), kind=kLoop, calls=%fused_computation | loop fusion | flops 2359296 | bytes 1048577 | tf_op jit(solution)/shard_map/jit(_where)/select_n | solution.py:367
  (49 shorter events, 2.8 us)
Async XLA Ops:
  0.0 0.9 copy-start.6
  0.9 11.1 %copy-start = (bf16[512,128]{1,0:T(8,128)(2,1)}, bf16[512,128]{1,0:T(8,128)(2,1)S(1)}, u32[]{:S(2)}) copy-start(bf16[512,128]{1,0:T(8,128)(2,1)S(1)} %constant_dynamic-update-slice_fusion.refs_0_) | copy-start | bytes 393220
  0.9 8.0 %collective-permute-start.2 = (bf16[512,128]{1,0:T(8,128)(2,1)S(1)}, bf16[512,128]{1,0:T(8,128)(2,1)S(1)}, u32[]{:S(2)}, u32[]{:S(2)}) collective-permute-start(bf16[512,128]{1,0:T(8,128)(2,1)S(1)} %constant_dynamic-update-slice_fusion.refs_0_), channel_id=1, source_target_pairs={{0,64},{32,96},{64,0},{96,32},{1,65},{33,97},{65,1},{97,33},{2,66}... | collective-permute-start | bytes 393224 | tf_op jit(solution)/shard_map/ppermute | solution.py:24
  4.9 7.1 %collective-permute-start.1 = (bf16[512,128]{1,0:T(8,128)(2,1)S(1)}, bf16[512,128]{1,0:T(8,128)(2,1)S(1)}, u32[]{:S(2)}, u32[]{:S(2)}) collective-permute-start(bf16[512,128]{1,0:T(8,128)(2,1)S(1)} %constant_dynamic-update-slice_fusion.refs_0_), channel_id=1, source_target_pairs={{0,96},{32,0},{64,32},{96,64},{1,97},{33,1},{65,33},{97,65},{2,98}... | collective-permute-start | bytes 393224 | tf_op jit(solution)/shard_map/ppermute | solution.py:24
  5.6 6.4 %collective-permute-start = (bf16[512,128]{1,0:T(8,128)(2,1)S(1)}, bf16[512,128]{1,0:T(8,128)(2,1)S(1)}, u32[]{:S(2)}, u32[]{:S(2)}) collective-permute-start(bf16[512,128]{1,0:T(8,128)(2,1)S(1)} %constant_dynamic-update-slice_fusion.refs_0_), channel_id=1, source_target_pairs={{0,32},{32,64},{64,96},{96,0},{1,33},{33,65},{65,97},{97,1},{2,34}... | collective-permute-start | bytes 393224 | tf_op jit(solution)/shard_map/ppermute | solution.py:24
  6.9 5.1 %collective-permute-start.3 = (bf16[512,128]{1,0:T(8,128)(2,1)S(1)}, bf16[512,128]{1,0:T(8,128)(2,1)S(1)}, u32[]{:S(2)}, u32[]{:S(2)}) collective-permute-start(bf16[512,128]{1,0:T(8,128)(2,1)S(1)} %constant_dynamic-update-slice_fusion.refs_0_), channel_id=1, source_target_pairs={{0,8},{8,16},{16,24},{24,0},{1,9},{9,17},{17,25},{25,1},{2,10},{10... | collective-permute-start | bytes 393224 | tf_op jit(solution)/shard_map/ppermute | solution.py:24
  7.4 6.2 %collective-permute-start.4 = (bf16[512,128]{1,0:T(8,128)(2,1)S(1)}, bf16[512,128]{1,0:T(8,128)(2,1)S(1)}, u32[]{:S(2)}, u32[]{:S(2)}) collective-permute-start(bf16[512,128]{1,0:T(8,128)(2,1)S(1)} %constant_dynamic-update-slice_fusion.refs_0_), channel_id=1, source_target_pairs={{0,24},{8,0},{16,8},{24,16},{1,25},{9,1},{17,9},{25,17},{2,26},{10... | collective-permute-start | bytes 393224 | tf_op jit(solution)/shard_map/ppermute | solution.py:24
  13.5 8.9 %collective-permute-start.5 = (bf16[1536,128]{1,0:T(8,128)(2,1)S(1)}, bf16[1536,128]{1,0:T(8,128)(2,1)S(1)}, u32[]{:S(2)}, u32[]{:S(2)}) collective-permute-start(bf16[1536,128]{1,0:T(8,128)(2,1)S(1)} %pad_maximum_fusion.refs_1_), channel_id=1, source_target_pairs={{0,8},{8,16},{16,24},{24,0},{1,9},{9,17},{17,25},{25,1},{2,10},{10... | collective-permute-start | bytes 1179656 | tf_op jit(solution)/shard_map/ppermute | solution.py:24
  13.8 10.8 %collective-permute-start.7 = (bf16[1536,128]{1,0:T(8,128)(2,1)S(1)}, bf16[1536,128]{1,0:T(8,128)(2,1)S(1)}, u32[]{:S(2)}, u32[]{:S(2)}) collective-permute-start(bf16[1536,128]{1,0:T(8,128)(2,1)S(1)} %pad_maximum_fusion.refs_1_), channel_id=1, source_target_pairs={{0,24},{8,0},{16,8},{24,16},{1,25},{9,1},{17,9},{25,17},{2,26},{10... | collective-permute-start | bytes 1179656 | tf_op jit(solution)/shard_map/ppermute | solution.py:24
  15.6 26.1 %collective-permute-start.13 = (bf16[1024,512]{1,0:T(8,128)(2,1)}, bf16[1024,512]{1,0:T(8,128)(2,1)S(1)}, u32[]{:S(2)}, u32[]{:S(2)}) collective-permute-start(bf16[1024,512]{1,0:T(8,128)(2,1)} %refs_0_.2), channel_id=1, source_target_pairs={{0,32},{32,64},{64,96},{96,0},{1,33},{33,65},{65,97},{97,1},{2,34}... | collective-permute-start | bytes 3145736 | tf_op jit(solution)/shard_map/ppermute | solution.py:24
  16.6 26.7 %collective-permute-start.14 = (bf16[1024,512]{1,0:T(8,128)(2,1)}, bf16[1024,512]{1,0:T(8,128)(2,1)S(1)}, u32[]{:S(2)}, u32[]{:S(2)}) collective-permute-start(bf16[1024,512]{1,0:T(8,128)(2,1)} %refs_0_.2), channel_id=1, source_target_pairs={{0,96},{32,0},{64,32},{96,64},{1,97},{33,1},{65,33},{97,65},{2,98}... | collective-permute-start | bytes 3145736 | tf_op jit(solution)/shard_map/ppermute | solution.py:24
  23.1 2.8 %copy-start.7 = (s32[4096]{0:T(1024)S(1)}, s32[4096]{0:T(1024)}, u32[]{:S(2)}) copy-start(s32[4096]{0:T(1024)} %param.10) | copy-start | bytes 49156
  23.1 6.7 %collective-permute-start.6 = (bf16[1024,128]{1,0:T(8,128)(2,1)}, bf16[1024,128]{1,0:T(8,128)(2,1)}, u32[]{:S(2)}, u32[]{:S(2)}) collective-permute-start(bf16[1024,128]{1,0:T(8,128)(2,1)} %join.6), channel_id=1, source_target_pairs={{0,8},{8,16},{16,24},{24,0},{1,9},{9,17},{17,25},{25,1},{2,10},{10... | collective-permute-start | bytes 786440 | tf_op jit(solution)/shard_map/ppermute | solution.py:24
  25.4 7.9 %collective-permute-start.8 = (bf16[1024,128]{1,0:T(8,128)(2,1)}, bf16[1024,128]{1,0:T(8,128)(2,1)}, u32[]{:S(2)}, u32[]{:S(2)}) collective-permute-start(bf16[1024,128]{1,0:T(8,128)(2,1)} %join.7), channel_id=1, source_target_pairs={{0,24},{8,0},{16,8},{24,16},{1,25},{9,1},{17,9},{25,17},{2,26},{10... | collective-permute-start | bytes 786440 | tf_op jit(solution)/shard_map/ppermute | solution.py:24
  27.4 0.9 copy-start.1
  33.3 1.2 %copy-start.3 = (bf16[256,1024]{1,0:T(8,128)(2,1)S(1)}, bf16[256,1024]{1,0:T(8,128)(2,1)}, u32[]{:S(2)}) copy-start(bf16[256,1024]{1,0:T(8,128)(2,1)} %q.1) | copy-start | bytes 1572868
  34.5 0.7 copy-start.4
  34.5 0.7 copy-start.5
  39.6 12.1 %collective-permute-start.9 = (bf16[256,1024]{1,0:T(8,128)(2,1)S(1)}, bf16[256,1024]{1,0:T(8,128)(2,1)S(1)}, u32[]{:S(2)}, u32[]{:S(2)}) collective-permute-start(bf16[256,1024]{1,0:T(8,128)(2,1)S(1)} %attend.1.rows), channel_id=1, source_target_pairs={{0,8},{8,16},{16,24},{24,0},{1,9},{9,17},{17,25},{25,1},{2,10},{10... | collective-permute-start | bytes 1572872 | tf_op jit(solution)/shard_map/ppermute | solution.py:24
  39.7 12.1 %collective-permute-start.11 = (bf16[256,1024]{1,0:T(8,128)(2,1)S(1)}, bf16[256,1024]{1,0:T(8,128)(2,1)S(1)}, u32[]{:S(2)}, u32[]{:S(2)}) collective-permute-start(bf16[256,1024]{1,0:T(8,128)(2,1)S(1)} %attend.1.rows), channel_id=1, source_target_pairs={{0,24},{8,0},{16,8},{24,16},{1,25},{9,1},{17,9},{25,17},{2,26},{10... | collective-permute-start | bytes 1572872 | tf_op jit(solution)/shard_map/ppermute | solution.py:24
  41.7 12.4 %collective-permute-start.15 = (bf16[512,512]{1,0:T(8,128)(2,1)S(1)}, bf16[512,512]{1,0:T(8,128)(2,1)S(1)}, u32[]{:S(2)}, u32[]{:S(2)}) collective-permute-start(bf16[512,512]{1,0:T(8,128)(2,1)S(1)} %join.10), channel_id=1, source_target_pairs={{0,32},{32,64},{64,96},{96,0},{1,33},{33,65},{65,97},{97,1},{2,34}... | collective-permute-start | bytes 1572872 | tf_op jit(solution)/shard_map/ppermute | solution.py:24
  43.4 10.7 %copy-start.2 = (bf16[1024,512]{1,0:T(8,128)(2,1)S(1)}, bf16[1024,512]{1,0:T(8,128)(2,1)}, u32[]{:S(2)}) copy-start(bf16[1024,512]{1,0:T(8,128)(2,1)} %refs_0_.2) | copy-start | bytes 3145732
  43.4 10.7 %collective-permute-start.16 = (bf16[512,512]{1,0:T(8,128)(2,1)S(1)}, bf16[512,512]{1,0:T(8,128)(2,1)S(1)}, u32[]{:S(2)}, u32[]{:S(2)}) collective-permute-start(bf16[512,512]{1,0:T(8,128)(2,1)S(1)} %join.11), channel_id=1, source_target_pairs={{0,96},{32,0},{64,32},{96,64},{1,97},{33,1},{65,33},{97,65},{2,98}... | collective-permute-start | bytes 1572872 | tf_op jit(solution)/shard_map/ppermute | solution.py:24
  51.7 6.4 %collective-permute-start.10 = (bf16[128,1024]{1,0:T(8,128)(2,1)S(1)}, bf16[128,1024]{1,0:T(8,128)(2,1)S(1)}, u32[]{:S(2)}, u32[]{:S(2)}) collective-permute-start(bf16[128,1024]{1,0:T(8,128)(2,1)S(1)} %join.8), channel_id=1, source_target_pairs={{0,8},{8,16},{16,24},{24,0},{1,9},{9,17},{17,25},{25,1},{2,10},{10... | collective-permute-start | bytes 786440 | tf_op jit(solution)/shard_map/ppermute | solution.py:24
  51.8 7.9 %collective-permute-start.12 = (bf16[128,1024]{1,0:T(8,128)(2,1)S(1)}, bf16[128,1024]{1,0:T(8,128)(2,1)S(1)}, u32[]{:S(2)}, u32[]{:S(2)}) collective-permute-start(bf16[128,1024]{1,0:T(8,128)(2,1)S(1)} %join.9), channel_id=1, source_target_pairs={{0,24},{8,0},{16,8},{24,16},{1,25},{9,1},{17,9},{25,17},{2,26},{10... | collective-permute-start | bytes 786440 | tf_op jit(solution)/shard_map/ppermute | solution.py:24
  57.7 3.4 %collective-permute-start.22 = (bf16[4,256,512]{2,1,0:T(8,128)(2,1)S(1)}, bf16[4,256,512]{2,1,0:T(8,128)(2,1)S(1)}, u32[]{:S(2)}, u32[]{:S(2)}) collective-permute-start(bf16[4,256,512]{2,1,0:T(8,128)(2,1)S(1)} %get-tuple-element.50), channel_id=1, source_target_pairs={{0,1},{1,0},{2,3},{3,2},{4,5},{5,4},{6,7},{7,6},{8,9},{9,8},{10,11... | collective-permute-start | bytes 3145736 | tf_op jit(solution)/shard_map/ppermute | solution.py:28
  61.0 2.7 %collective-permute-start.17 = (bf16[4,256,512]{2,1,0:T(8,128)(2,1)S(1)}, bf16[4,256,512]{2,1,0:T(8,128)(2,1)S(1)}, u32[]{:S(2)}, u32[]{:S(2)}) collective-permute-start(bf16[4,256,512]{2,1,0:T(8,128)(2,1)S(1)} %get-tuple-element.43), channel_id=1, source_target_pairs={{0,1},{1,0},{2,3},{3,2},{4,5},{5,4},{6,7},{7,6},{8,9},{9,8},{10,11... | collective-permute-start | bytes 3145736 | tf_op jit(solution)/shard_map/ppermute | solution.py:28
  61.7 7.7 %collective-permute-start.24 = (bf16[256,512]{1,0:T(8,128)(2,1)S(1)}, bf16[256,512]{1,0:T(8,128)(2,1)S(1)}, u32[]{:S(2)}, u32[]{:S(2)}) collective-permute-start(bf16[256,512]{1,0:T(8,128)(2,1)S(1)} %get-tuple-element.54), channel_id=1, source_target_pairs={{0,2},{1,7},{2,4},{3,1},{4,6},{5,3},{6,0},{7,5},{8,10},{9,15},{10,... | collective-permute-start | bytes 786440 | tf_op jit(solution)/shard_map/ppermute | solution.py:291
  64.3 7.8 %collective-permute-start.19 = (bf16[256,512]{1,0:T(8,128)(2,1)S(1)}, bf16[256,512]{1,0:T(8,128)(2,1)S(1)}, u32[]{:S(2)}, u32[]{:S(2)}) collective-permute-start(bf16[256,512]{1,0:T(8,128)(2,1)S(1)} %get-tuple-element.47), channel_id=1, source_target_pairs={{0,2},{1,7},{2,4},{3,1},{4,6},{5,3},{6,0},{7,5},{8,10},{9,15},{10,... | collective-permute-start | bytes 786440 | tf_op jit(solution)/shard_map/ppermute | solution.py:291
  69.4 7.7 %collective-permute-start.25 = (bf16[256,512]{1,0:T(8,128)(2,1)S(1)}, bf16[256,512]{1,0:T(8,128)(2,1)S(1)}, u32[]{:S(2)}, u32[]{:S(2)}) collective-permute-start(bf16[256,512]{1,0:T(8,128)(2,1)S(1)} %add_convert_fusion.2), channel_id=1, source_target_pairs={{0,2},{1,7},{2,4},{3,1},{4,6},{5,3},{6,0},{7,5},{8,10},{9,15},{10,... | collective-permute-start | bytes 786440 | tf_op jit(solution)/shard_map/ppermute | solution.py:291
  72.2 7.7 %collective-permute-start.20 = (bf16[256,512]{1,0:T(8,128)(2,1)S(1)}, bf16[256,512]{1,0:T(8,128)(2,1)S(1)}, u32[]{:S(2)}, u32[]{:S(2)}) collective-permute-start(bf16[256,512]{1,0:T(8,128)(2,1)S(1)} %add_convert_fusion.5), channel_id=1, source_target_pairs={{0,2},{1,7},{2,4},{3,1},{4,6},{5,3},{6,0},{7,5},{8,10},{9,15},{10,... | collective-permute-start | bytes 786440 | tf_op jit(solution)/shard_map/ppermute | solution.py:291
  72.6 7.9 %collective-permute-start.23 = (bf16[256,512]{1,0:T(8,128)(2,1)S(1)}, bf16[256,512]{1,0:T(8,128)(2,1)S(1)}, u32[]{:S(2)}, u32[]{:S(2)}) collective-permute-start(bf16[256,512]{1,0:T(8,128)(2,1)S(1)} %get-tuple-element.51), channel_id=1, source_target_pairs={{0,24},{1,8},{2,26},{3,10},{4,28},{5,12},{6,30},{7,14},{8,0},{9,16... | collective-permute-start | bytes 786440 | tf_op jit(solution)/shard_map/ppermute | solution.py:301
  74.7 16.3 %collective-permute-start.18 = (bf16[256,512]{1,0:T(8,128)(2,1)S(1)}, bf16[256,512]{1,0:T(8,128)(2,1)S(1)}, u32[]{:S(2)}, u32[]{:S(2)}) collective-permute-start(bf16[256,512]{1,0:T(8,128)(2,1)S(1)} %get-tuple-element.44), channel_id=1, source_target_pairs={{0,0},{1,16},{2,2},{3,18},{4,4},{5,20},{6,6},{7,22},{8,8},{9,24},{... | collective-permute-start | bytes 786440 | tf_op jit(solution)/shard_map/ppermute | solution.py:301
  77.1 13.8 %collective-permute-start.26 = (bf16[256,512]{1,0:T(8,128)(2,1)S(1)}, bf16[256,512]{1,0:T(8,128)(2,1)S(1)}, u32[]{:S(2)}, u32[]{:S(2)}) collective-permute-start(bf16[256,512]{1,0:T(8,128)(2,1)S(1)} %add_convert_fusion.1), channel_id=1, source_target_pairs={{0,26},{1,14},{2,28},{3,8},{4,30},{5,10},{6,24},{7,12},{8,2},{9,22... | collective-permute-start | bytes 786440 | tf_op jit(solution)/shard_map/ppermute | solution.py:301
  79.9 11.1 %collective-permute-start.21 = (bf16[256,512]{1,0:T(8,128)(2,1)S(1)}, bf16[256,512]{1,0:T(8,128)(2,1)S(1)}, u32[]{:S(2)}, u32[]{:S(2)}) collective-permute-start(bf16[256,512]{1,0:T(8,128)(2,1)S(1)} %add_convert_fusion.4), channel_id=1, source_target_pairs={{0,2},{1,22},{2,4},{3,16},{4,6},{5,18},{6,0},{7,20},{8,10},{9,30},... | collective-permute-start | bytes 786440 | tf_op jit(solution)/shard_map/ppermute | solution.py:301

commit v5 on v4

--- a/solution.py
+++ b/solution.py
@@ -11,6 +11,7 @@
 
 DH = 128
 RUN = 64
+DOCS = 8
 SIZES = (256, 512, 768, 1024, 1152, 1536, 2304)
 NEGATIVE = -1e30
 Z = ("zh", "zl")
@@ -50,8 +51,8 @@
                 outs[which][pl.ds(at, RUN), :] = ref[row : row + RUN, :]
 
 
-def place(positions, held, blocks, ordered=None):
-    shape = jax.ShapeDtypeStruct((positions.shape[0] * RUN, DH), jnp.bfloat16)
+def place(runs, slots, held, blocks, ordered=None):
+    shape = jax.ShapeDtypeStruct((slots, DH), jnp.bfloat16)
     old = list(ordered or ())
     at = 1 + len(blocks)
     return pl.pallas_call(
@@ -60,22 +61,24 @@
         in_specs=[SMEM] + [VMEM] * (len(blocks) + len(old)),
         out_specs=[VMEM, VMEM],
         input_output_aliases={at: 0, at + 1: 1} if old else {},
-        compiler_params=pltpu.CompilerParams(vmem_limit_bytes=8 * 2**20),
+        compiler_params=pltpu.CompilerParams(vmem_limit_bytes=6 * 2**20),
         cost_estimate=pl.CostEstimate(flops=0, bytes_accessed=2 * 2**20, transcendentals=0),
         name="place",
-    )(positions, *blocks, *old)
-
-
-def attend_kernel(pos, lengths, spans, q, ks, vs, out):
+    )(runs, *blocks, *old)
+
+
+def attend_kernel(pos, q, ks, vs, out):
     z, x = z_index(), lax.axis_index("x")
     heads, slots = out.shape[1] // DH, ks.shape[0]
     runs = out.shape[0] // RUN
 
+    first_length, first_span = slots // RUN, slots // RUN + DOCS
     ends = []
-    for d in range(lengths.shape[0]):
-        ends.append(lengths[d] + (ends[-1] if ends else 0))
+    for d in range(DOCS):
+        ends.append(pos[first_length + d] + (ends[-1] if ends else 0))
     starts = [0] + ends[:-1]
-    span_list = [(spans[0, k], spans[1, k]) for k in range(spans.shape[1])]
+    count = (pos.shape[0] - first_span) // 2
+    span_list = [(pos[first_span + k], pos[first_span + count + k]) for k in range(count)]
 
     def interval(at):
         low = jnp.zeros_like(at)
@@ -111,31 +114,34 @@
                 t = lanes + (start + n * DH)
                 allowed.append((t >= 0) & (t < width))
             per = heads // groups
-            for g in range(groups):
-                columns = [(g * per + h) * DH for h in range(per)]
-                queries = jnp.concatenate(
-                    [q[pl.ds(row, RUN), c : c + DH] for c in columns], axis=0
-                )
+            columns = [[(g * per + h) * DH for h in range(per)] for g in range(groups)]
+            scores, mixed = [], []
+            for group in columns:
+                queries = jnp.concatenate([q[pl.ds(row, RUN), c : c + DH] for c in group], axis=0)
                 s = lax.dot_general(
                     queries,
                     ks[pl.ds(start, size), :],
                     (((1,), (1,)), ((), ())),
                     preferred_element_type=jnp.float32,
                 )
-                parts = [
-                    jnp.where(
-                        allowed[n][None], s[:, n * DH : (n + 1) * DH].reshape(per, RUN, DH), NEGATIVE
-                    ).reshape(per * RUN, DH)
-                    for n in range(size // DH)
-                ]
-                top = jnp.max(functools.reduce(jnp.maximum, parts), axis=1, keepdims=True)
-                expo = [jnp.exp2((part - top) * scale) for part in parts]
+                scores.append(
+                    [
+                        jnp.where(
+                            allowed[n][None], s[:, n * DH : (n + 1) * DH].reshape(per, RUN, DH), NEGATIVE
+                        ).reshape(per * RUN, DH)
+                        for n in range(size // DH)
+                    ]
+                )
+            for parts in scores:
+                top = jnp.max(functools.reduce(jnp.maximum, parts), axis=1, keepdims=True) * scale
+                expo = [jnp.exp2(part * scale - top) for part in parts]
                 total = jnp.sum(functools.reduce(jnp.add, expo), axis=1, keepdims=True)
                 weights = jnp.concatenate([e.astype(jnp.bfloat16) for e in expo], axis=1)
-                mixed = jnp.dot(weights, vs[pl.ds(start, size), :], preferred_element_type=jnp.float32)
-                mixed = (mixed / total).astype(jnp.bfloat16)
-                for h, c in enumerate(columns):
-                    out[pl.ds(row, RUN), c : c + DH] = mixed[h * RUN : (h + 1) * RUN]
+                mixed.append((jnp.dot(weights, vs[pl.ds(start, size), :], preferred_element_type=jnp.float32), total))
+            for group, (value, total) in zip(columns, mixed):
+                value = (value / total).astype(jnp.bfloat16)
+                for h, c in enumerate(group):
+                    out[pl.ds(row, RUN), c : c + DH] = value[h * RUN : (h + 1) * RUN]
 
         below = 0
         for size in SIZES:
@@ -150,19 +156,19 @@
     lax.fori_loop(0, runs, block, 0)
 
 
-def attend(positions, lengths, spans, q, ordered):
+def attend(runs, q, ordered):
     rows, width = q.shape
     return pl.pallas_call(
         attend_kernel,
         out_shape=jax.ShapeDtypeStruct((rows, width), jnp.bfloat16),
-        in_specs=[SMEM] * 3 + [VMEM] * 3,
+        in_specs=[SMEM] + [VMEM] * 3,
         out_specs=VMEM,
-        compiler_params=pltpu.CompilerParams(vmem_limit_bytes=16 * 2**20),
+        compiler_params=pltpu.CompilerParams(vmem_limit_bytes=10 * 2**20),
         cost_estimate=pl.CostEstimate(
             flops=24 * rows * 1024 * width, bytes_accessed=4 * 2**20, transcendentals=rows * 8 * width
         ),
         name="attend",
-    )(positions, lengths, spans, q, *ordered)
+    )(runs, q, *ordered)
 
 
 def join_kernel(ranges, *refs):
@@ -252,7 +258,7 @@
         in_specs=[VMEM] * (len(pieces) + len(weights)),
         out_specs=[VMEM] * results,
         scratch_shapes=scratch[kernel],
-        compiler_params=pltpu.CompilerParams(vmem_limit_bytes=16 * 2**20),
+        compiler_params=pltpu.CompilerParams(vmem_limit_bytes=10 * 2**20),
         cost_estimate=pl.CostEstimate(
             flops=4 * count * depth * width * len(BLOCKS), bytes_accessed=4 * 2**20, transcendentals=0
         ),
@@ -280,7 +286,7 @@
         in_specs=[VMEM] * 2,
         out_specs=[VMEM] * 4,
         scratch_shapes=[pltpu.VMEM(keep.shape, jnp.bfloat16)],
-        compiler_params=pltpu.CompilerParams(vmem_limit_bytes=8 * 2**20),
+        compiler_params=pltpu.CompilerParams(vmem_limit_bytes=6 * 2**20),
         cost_estimate=pl.CostEstimate(flops=0, bytes_accessed=3 * 2**20, transcendentals=0),
         name="combine",
     )(keep, got)
@@ -322,7 +328,7 @@
 
 def shards(queries, keys, values, positions, lengths, spans, weight):
     x = lax.axis_index("x")
-    count = keys.shape[0]
+    count, slots = keys.shape[0], positions.shape[0]
     kv = jnp.concatenate([keys, values], axis=0)
     line = [shift(kv, Z, 1), shift(kv, Z, -1), shift(kv, Z, 2)]
     left, right = shift(kv, "x", 1), shift(kv, "x", -1)
@@ -332,24 +338,26 @@
     weight_left, weight_right = shift(weight, Z, 1), shift(weight, Z, -1)
 
     runs = positions.reshape(-1, RUN)[:, 0]
+    runs = jnp.concatenate([runs, lengths, spans[0], spans[1]])
     line_blocks = [(dz, which) for dz in (3, 1, 2) for which in (0, 1)]
 
     def at_x(dx, blocks=line_blocks):
         return [(dz, dx, which) for dz, which in blocks]
 
     here = [(0, 0), (0, 1)]
-    ordered = place(runs, (at_x(0, here), at_x(0), at_x(3, here), at_x(1, here)), (kv, line, left, right))
+    ordered = place(runs, slots, (at_x(0, here), at_x(0), at_x(3, here), at_x(1, here)), (kv, line, left, right))
     left2 = shift(join((line_left, left), ((0, 3 * count), (0, count))), "x", 1)
     right2 = shift(join((line_right, right), ((3 * count, 6 * count), (count, 2 * count))), "x", -1)
-    ordered = place(runs, (at_x(3), at_x(1)), (line_left, line_right), ordered)
+    ordered = place(runs, slots, (at_x(3), at_x(1)), (line_left, line_right), ordered)
     ordered = place(
         runs,
+        slots,
         (at_x(2, line_blocks[:3] + here[:1]), at_x(2, line_blocks[3:] + here[1:])),
         (left2, right2),
         ordered,
     )
 
-    own = attend(runs, lengths, spans, queries, ordered)
+    own = attend(runs, queries, ordered)
     rows_left, rows_right = shift(own, "x", 1), shift(own, "x", -1)
     rows_far = halves(rows_left, rows_right, "x")
     weight_far = halves(after(weight_left, own), after(weight_right, own), Z)

time: 92.9 us -> 92.4 us (level)
  waiting for transfers between devices: 39.3 us -> 38.3 us
    unnamed x17 -> x21, local copies, waits for them, and re-layouts: 2.46 us -> 2.48 us
  transfers between devices with their start and end apart: 27 -> 27, of which waited for: 14 -> 13; matrix products, arithmetic and copies ran while one was open for 2% -> 3% of each run, Pallas kernels for 16% -> 15%
where the time goes in v5:
time: 92.4 us; the launch traced here: 91.3 us
  waiting for transfers between devices  38.3 us (41%)
  starting transfers between devices  32.7 us (35%)
  Pallas kernels  14 us (15%)
  local copies, waits for them, and re-layouts  4.62 us (5%)
  other arithmetic  1.44 us (2%)
    ppermute x17, starting transfers between devices, shift(): return lax.ppermute(value, axis, [(i, (i + step) % 4) for i in range(4)])  23.1 us
    ppermute x17, waiting for transfers between devices, shift(): return lax.ppermute(value, axis, [(i, (i + step) % 4) for i in range(4)])  19 us
    ppermute x4, waiting for transfers between devices, home(): return lax.ppermute(value, ('x', 'y', 'c'), pairs)  10.8 us
    ppermute x4, waiting for transfers between devices, relay(): return lax.ppermute(value, (axis, 'c'), pairs)  7.96 us
    ppermute x4, starting transfers between devices, home(): return lax.ppermute(value, ('x', 'y', 'c'), pairs)  5.18 us
    pallas_call x3, Pallas kernels, project(): pl.pallas_call(kernel, out_shape=[result] * results, in_specs=[VMEM] * (l...  4.96 us
    ppermute x4, starting transfers between devices, relay(): return lax.ppermute(value, (axis, 'c'), pairs)  4.16 us
    pallas_call x1, Pallas kernels, attend(): pl.pallas_call(attend_kernel, out_shape=jax.ShapeDtypeStruct((rows, width...  3.96 us
  transfers between devices with their start and end apart: 27, of which 13 were waited for; matrix products, arithmetic and copies ran while one was open for 3% of the time, Pallas kernels for 15%

profile of v5, /device:TPU:6, one launch (start us, length us, event | category | flops | bytes accessed | tf_op | source)
XLA Modules:
  0.0 91.3 jit_solution(9682034579750453284)
XLA Ops:
  0.0 0.9 constant_dynamic-update-slice_fusion.1
  0.9 4.0 %collective-permute-start.2 = (bf16[512,128]{1,0:T(8,128)(2,1)S(1)}, bf16[512,128]{1,0:T(8,128)(2,1)S(1)}, u32[]{:S(2)}, u32[]{:S(2)}) collective-permute-start(bf16[512,128]{1,0:T(8,128)(2,1)S(1)} %constant_dynamic-update-slice_fusion.refs_0_), channel_id=1, source_target_pairs={{0,64},{32,96},{64,0},{96,32},{1,65},{33,97},{65,1},{97,33},{2,66}... | collective-permute-start | bytes 393224 | tf_op jit(solution)/shard_map/ppermute | solution.py:25
  4.9 0.7 collective-permute-start.1
  5.6 1.3 %collective-permute-start = (bf16[512,128]{1,0:T(8,128)(2,1)S(1)}, bf16[512,128]{1,0:T(8,128)(2,1)S(1)}, u32[]{:S(2)}, u32[]{:S(2)}) collective-permute-start(bf16[512,128]{1,0:T(8,128)(2,1)S(1)} %constant_dynamic-update-slice_fusion.refs_0_), channel_id=1, source_target_pairs={{0,32},{32,64},{64,96},{96,0},{1,33},{33,65},{65,97},{97,1},{2,34}... | collective-permute-start | bytes 393224 | tf_op jit(solution)/shard_map/ppermute | solution.py:25
  6.9 0.5 collective-permute-start.3
  7.4 1.5 %collective-permute-start.4 = (bf16[512,128]{1,0:T(8,128)(2,1)S(1)}, bf16[512,128]{1,0:T(8,128)(2,1)S(1)}, u32[]{:S(2)}, u32[]{:S(2)}) collective-permute-start(bf16[512,128]{1,0:T(8,128)(2,1)S(1)} %constant_dynamic-update-slice_fusion.refs_0_), channel_id=1, source_target_pairs={{0,24},{8,0},{16,8},{24,16},{1,25},{9,1},{17,9},{25,17},{2,26},{10... | collective-permute-start | bytes 393224 | tf_op jit(solution)/shard_map/ppermute | solution.py:25
  8.9 3.0 %collective-permute-done.1 = bf16[512,128]{1,0:T(8,128)(2,1)S(1)} collective-permute-done((bf16[512,128]{1,0:T(8,128)(2,1)S(1)}, bf16[512,128]{1,0:T(8,128)(2,1)S(1)}, u32[]{:S(2)}, u32[]{:S(2)}) %collective-permute-start.1) | collective-permute-done | bytes 131104 | tf_op jit(solution)/shard_map/ppermute | solution.py:25
  12.0 1.5 %collective-permute-done.4.refs_1_.refs_3_ = bf16[512,128]{1,0:T(8,128)(2,1)S(1)} collective-permute-done((bf16[512,128]{1,0:T(8,128)(2,1)S(1)}, bf16[512,128]{1,0:T(8,128)(2,1)S(1)}, u32[]{:S(2)}, u32[]{:S(2)}) %collective-permute-start.4) | collective-permute-done | bytes 131104 | tf_op jit(solution)/shard_map/ppermute | solution.py:25
  13.8 1.7 %collective-permute-start.7 = (bf16[1536,128]{1,0:T(8,128)(2,1)S(1)}, bf16[1536,128]{1,0:T(8,128)(2,1)S(1)}, u32[]{:S(2)}, u32[]{:S(2)}) collective-permute-start(bf16[1536,128]{1,0:T(8,128)(2,1)S(1)} %pad_maximum_fusion.refs_1_), channel_id=1, source_target_pairs={{0,24},{8,0},{16,8},{24,16},{1,25},{9,1},{17,9},{25,17},{2,26},{10... | collective-permute-start | bytes 1179656 | tf_op jit(solution)/shard_map/ppermute | solution.py:25
  15.6 1.0 %collective-permute-start.13 = (bf16[1024,512]{1,0:T(8,128)(2,1)}, bf16[1024,512]{1,0:T(8,128)(2,1)S(1)}, u32[]{:S(2)}, u32[]{:S(2)}) collective-permute-start(bf16[1024,512]{1,0:T(8,128)(2,1)} %refs_0_.2), channel_id=1, source_target_pairs={{0,32},{32,64},{64,96},{96,0},{1,33},{33,65},{65,97},{97,1},{2,34}... | collective-permute-start | bytes 3145736 | tf_op jit(solution)/shard_map/ppermute | solution.py:25
  16.6 2.2 %collective-permute-start.14 = (bf16[1024,512]{1,0:T(8,128)(2,1)}, bf16[1024,512]{1,0:T(8,128)(2,1)S(1)}, u32[]{:S(2)}, u32[]{:S(2)}) collective-permute-start(bf16[1024,512]{1,0:T(8,128)(2,1)} %refs_0_.2), channel_id=1, source_target_pairs={{0,96},{32,0},{64,32},{96,64},{1,97},{33,1},{65,33},{97,65},{2,98}... | collective-permute-start | bytes 3145736 | tf_op jit(solution)/shard_map/ppermute | solution.py:25
  18.8 3.6 %collective-permute-done.5.refs_0_ = bf16[1536,128]{1,0:T(8,128)(2,1)S(1)} collective-permute-done((bf16[1536,128]{1,0:T(8,128)(2,1)S(1)}, bf16[1536,128]{1,0:T(8,128)(2,1)S(1)}, u32[]{:S(2)}, u32[]{:S(2)}) %collective-permute-start.5) | collective-permute-done | bytes 393248 | tf_op jit(solution)/shard_map/ppermute | solution.py:25
  22.4 0.7 join.6
  23.2 1.5 %collective-permute-start.6 = (bf16[1024,128]{1,0:T(8,128)(2,1)}, bf16[1024,128]{1,0:T(8,128)(2,1)}, u32[]{:S(2)}, u32[]{:S(2)}) collective-permute-start(bf16[1024,128]{1,0:T(8,128)(2,1)} %join.6), channel_id=1, source_target_pairs={{0,8},{8,16},{16,24},{24,0},{1,9},{9,17},{17,25},{25,1},{2,10},{10... | collective-permute-start | bytes 786440 | tf_op jit(solution)/shard_map/ppermute | solution.py:25
  24.6 0.7 join.7
  25.4 0.5 collective-permute-start.8
  25.9 0.6 slice_bitcast_fusion.1
  26.5 0.7 reshape.3
  27.2 0.9 slice_reduce_fusion
  28.1 0.7 copy-done.6
  28.8 0.9 copy-done.1
  29.7 0.7 place.3
  30.4 0.7 place.4
  31.1 2.2 %collective-permute-done.8.refs_1_ = bf16[1024,128]{1,0:T(8,128)(2,1)} collective-permute-done((bf16[1024,128]{1,0:T(8,128)(2,1)}, bf16[1024,128]{1,0:T(8,128)(2,1)}, u32[]{:S(2)}, u32[]{:S(2)}) %collective-permute-start.8) | collective-permute-done | bytes 262176 | tf_op jit(solution)/shard_map/ppermute | solution.py:25
  33.3 1.2 %place.5 = (bf16[4096,128]{1,0:T(8,128)(2,1)S(1)}, bf16[4096,128]{1,0:T(8,128)(2,1)S(1)}) custom-call(s32[80]{0:T(128)S(1)} %pad_add_fusion.pos, bf16[1024,128]{1,0:T(8,128)(2,1)} %collective-permute-done.6.refs_0_, bf16[1024,128]{1,0:T(8,128)(2,1)} %collective-permute-done.8.refs_1_, ...), custom_call_target="tpu_custom_call", output_to_operand_aliasing={{0}: (3, {}), {1}: (4, {})} | custom-call | bytes 2097152 | tf_op jit(solution)/shard_map/place/pallas_call | solution.py:58
  34.5 4.0 %attend.1.rows = bf16[256,1024]{1,0:T(8,128)(2,1)S(1)} custom-call(s32[80]{0:T(128)S(1)} %pad_add_fusion.pos, bf16[256,1024]{1,0:T(8,128)(2,1)S(1)} %copy-done.3, bf16[4096,128]{1,0:T(8,128)(2,1)S(1)} %get-tuple-element.37.ks, bf16[4096,128]{1,0:T(8,128)(2,1)S(1)} %get-tuple-element.38.vs), custom_call_target="tpu_custom_call" | custom-call | flops 6442450944 | bytes 4194304 | tf_op jit(solution)/shard_map/attend/pallas_call | solution.py:161
  38.8 1.7 %collective-permute-start.11 = (bf16[256,1024]{1,0:T(8,128)(2,1)S(1)}, bf16[256,1024]{1,0:T(8,128)(2,1)S(1)}, u32[]{:S(2)}, u32[]{:S(2)}) collective-permute-start(bf16[256,1024]{1,0:T(8,128)(2,1)S(1)} %attend.1.rows), channel_id=1, source_target_pairs={{0,24},{8,0},{16,8},{24,16},{1,25},{9,1},{17,9},{25,17},{2,26},{10... | collective-permute-start | bytes 1572872 | tf_op jit(solution)/shard_map/ppermute | solution.py:25
  40.6 0.5 collective-permute-start.15
  41.1 2.9 %collective-permute-start.16 = (bf16[512,512]{1,0:T(8,128)(2,1)S(1)}, bf16[512,512]{1,0:T(8,128)(2,1)S(1)}, u32[]{:S(2)}, u32[]{:S(2)}) collective-permute-start(bf16[512,512]{1,0:T(8,128)(2,1)S(1)} %join.11), channel_id=1, source_target_pairs={{0,96},{32,0},{64,32},{96,64},{1,97},{33,1},{65,33},{97,65},{2,98}... | collective-permute-start | bytes 1572872 | tf_op jit(solution)/shard_map/ppermute | solution.py:25
  44.0 6.5 %collective-permute-done.9.refs_0_.left = bf16[256,1024]{1,0:T(8,128)(2,1)S(1)} collective-permute-done((bf16[256,1024]{1,0:T(8,128)(2,1)S(1)}, bf16[256,1024]{1,0:T(8,128)(2,1)S(1)}, u32[]{:S(2)}, u32[]{:S(2)}) %collective-permute-start.9) | collective-permute-done | bytes 524320 | tf_op jit(solution)/shard_map/ppermute | solution.py:25
  50.9 2.0 %collective-permute-start.12 = (bf16[128,1024]{1,0:T(8,128)(2,1)S(1)}, bf16[128,1024]{1,0:T(8,128)(2,1)S(1)}, u32[]{:S(2)}, u32[]{:S(2)}) collective-permute-start(bf16[128,1024]{1,0:T(8,128)(2,1)S(1)} %join.9), channel_id=1, source_target_pairs={{0,24},{8,0},{16,8},{24,16},{1,25},{9,1},{17,9},{25,17},{2,26},{10... | collective-permute-start | bytes 786440 | tf_op jit(solution)/shard_map/ppermute | solution.py:25
  53.2 1.2 %project.3.own = bf16[4,256,512]{2,1,0:T(8,128)(2,1)S(1)} custom-call(bf16[256,1024]{1,0:T(8,128)(2,1)S(1)} %attend.1.rows, bf16[1024,512]{1,0:T(8,128)(2,1)S(1)} %copy-done.2, bf16[1024,512]{1,0:T(8,128)(2,1)S(1)} %collective-permute-done.13.refs_0_.refs_1_, bf16[1024,512]{1,0:T(8,128)(2,1)S(1)} %collective-permute-done.14.refs_0_.refs_2_, ...), custom_call_target="tpu_custom_call" | custom-call | flops 2147483648 | bytes 4194304 | tf_op jit(solution)/shard_map/project/pallas_call | solution.py:255
  54.4 2.4 %project.5 = (bf16[4,256,512]{2,1,0:T(8,128)(2,1)S(1)}, bf16[4,256,512]{2,1,0:T(8,128)(2,1)S(1)}) custom-call(bf16[256,1024]{1,0:T(8,128)(2,1)S(1)} %collective-permute-done.9.refs_0_.left, bf16[256,1024]{1,0:T(8,128)(2,1)S(1)} %collective-permute-done.11.refs_0_.right, bf16[1024,512]{1,0:T(8,128)(2,1)S(1)} %copy-done.2, ...), custom_call_target="tpu_custom_call" | custom-call | flops 2147483648 | bytes 4194304 | tf_op jit(solution)/shard_map/project/pallas_call | solution.py:255
  57.0 1.8 %collective-permute-done.12.lower = bf16[128,1024]{1,0:T(8,128)(2,1)S(1)} collective-permute-done((bf16[128,1024]{1,0:T(8,128)(2,1)S(1)}, bf16[128,1024]{1,0:T(8,128)(2,1)S(1)}, u32[]{:S(2)}, u32[]{:S(2)}) %collective-permute-start.12) | collective-permute-done | bytes 262176 | tf_op jit(solution)/shard_map/ppermute | solution.py:25
  58.8 1.3 %project.4 = (bf16[4,256,512]{2,1,0:T(8,128)(2,1)S(1)}, bf16[4,256,512]{2,1,0:T(8,128)(2,1)S(1)}) custom-call(bf16[128,1024]{1,0:T(8,128)(2,1)S(1)} %collective-permute-done.10.upper, bf16[128,1024]{1,0:T(8,128)(2,1)S(1)} %collective-permute-done.12.lower, bf16[4,256,512]{2,1,0:T(8,128)(2,1)S(1)} %project.3.own, bf16[1024,512]{1,0:T(8,128)(2,1)S(1)} %copy-done.2, ...), custom_call_target="tpu_custom_call" | custom-call | flops 2147483648 | bytes 4194304 | tf_op jit(solution)/shard_map/project/pallas_call | solution.py:255
  60.3 0.5 combine.3
  60.8 1.6 %collective-permute-start.24 = (bf16[256,512]{1,0:T(8,128)(2,1)S(1)}, bf16[256,512]{1,0:T(8,128)(2,1)S(1)}, u32[]{:S(2)}, u32[]{:S(2)}) collective-permute-start(bf16[256,512]{1,0:T(8,128)(2,1)S(1)} %get-tuple-element.54), channel_id=1, source_target_pairs={{0,2},{1,7},{2,4},{3,1},{4,6},{5,3},{6,0},{7,5},{8,10},{9,15},{10,... | collective-permute-start | bytes 786440 | tf_op jit(solution)/shard_map/ppermute | solution.py:297
  62.4 0.5 collective-permute-done.17.got
  62.9 0.5 combine.2
  63.4 1.6 %collective-permute-start.19 = (bf16[256,512]{1,0:T(8,128)(2,1)S(1)}, bf16[256,512]{1,0:T(8,128)(2,1)S(1)}, u32[]{:S(2)}, u32[]{:S(2)}) collective-permute-start(bf16[256,512]{1,0:T(8,128)(2,1)S(1)} %get-tuple-element.47), channel_id=1, source_target_pairs={{0,2},{1,7},{2,4},{3,1},{4,6},{5,3},{6,0},{7,5},{8,10},{9,15},{10,... | collective-permute-start | bytes 786440 | tf_op jit(solution)/shard_map/ppermute | solution.py:297
  65.1 3.4 %collective-permute-done.24 = bf16[256,512]{1,0:T(8,128)(2,1)S(1)} collective-permute-done((bf16[256,512]{1,0:T(8,128)(2,1)S(1)}, bf16[256,512]{1,0:T(8,128)(2,1)S(1)}, u32[]{:S(2)}, u32[]{:S(2)}) %collective-permute-start.24) | collective-permute-done | bytes 262176 | tf_op jit(solution)/shard_map/ppermute | solution.py:297
  68.5 0.4 collective-permute-start.25
  68.9 2.3 %collective-permute-done.19 = bf16[256,512]{1,0:T(8,128)(2,1)S(1)} collective-permute-done((bf16[256,512]{1,0:T(8,128)(2,1)S(1)}, bf16[256,512]{1,0:T(8,128)(2,1)S(1)}, u32[]{:S(2)}, u32[]{:S(2)}) %collective-permute-start.19) | collective-permute-done | bytes 262176 | tf_op jit(solution)/shard_map/ppermute | solution.py:297
  71.8 1.8 %collective-permute-start.23 = (bf16[256,512]{1,0:T(8,128)(2,1)S(1)}, bf16[256,512]{1,0:T(8,128)(2,1)S(1)}, u32[]{:S(2)}, u32[]{:S(2)}) collective-permute-start(bf16[256,512]{1,0:T(8,128)(2,1)S(1)} %get-tuple-element.51), channel_id=1, source_target_pairs={{0,24},{1,8},{2,26},{3,10},{4,28},{5,12},{6,30},{7,14},{8,0},{9,16... | collective-permute-start | bytes 786440 | tf_op jit(solution)/shard_map/ppermute | solution.py:307
  73.6 2.9 %collective-permute-start.18 = (bf16[256,512]{1,0:T(8,128)(2,1)S(1)}, bf16[256,512]{1,0:T(8,128)(2,1)S(1)}, u32[]{:S(2)}, u32[]{:S(2)}) collective-permute-start(bf16[256,512]{1,0:T(8,128)(2,1)S(1)} %get-tuple-element.44), channel_id=1, source_target_pairs={{0,0},{1,16},{2,2},{3,18},{4,4},{5,20},{6,6},{7,22},{8,8},{9,24},{... | collective-permute-start | bytes 786440 | tf_op jit(solution)/shard_map/ppermute | solution.py:307
  76.7 2.3 %collective-permute-done.20 = bf16[256,512]{1,0:T(8,128)(2,1)S(1)} collective-permute-done((bf16[256,512]{1,0:T(8,128)(2,1)S(1)}, bf16[256,512]{1,0:T(8,128)(2,1)S(1)}, u32[]{:S(2)}, u32[]{:S(2)}) %collective-permute-start.20) | collective-permute-done | bytes 262176 | tf_op jit(solution)/shard_map/ppermute | solution.py:297
  79.4 10.8 %collective-permute-done.26 = bf16[256,512]{1,0:T(8,128)(2,1)S(1)} collective-permute-done((bf16[256,512]{1,0:T(8,128)(2,1)S(1)}, bf16[256,512]{1,0:T(8,128)(2,1)S(1)}, u32[]{:S(2)}, u32[]{:S(2)}) %collective-permute-start.26) | collective-permute-done | bytes 262176 | tf_op jit(solution)/shard_map/ppermute | solution.py:307
  90.4 0.9 %maximum_select_fusion = bf16[256,1024]{1,0:T(8,128)(2,1)} fusion(bf16[256,512]{1,0:T(8,128)(2,1)S(1)} %add_convert_fusion, bf16[256,512]{1,0:T(8,128)(2,1)S(1)} %add_convert_fusion.3, pred[]{:T(512)S(6)} %eq.3), kind=kLoop, calls=%fused_computation | loop fusion | flops 2359296 | bytes 1048577 | tf_op jit(solution)/shard_map/jit(_where)/select_n | solution.py:375
  (55 shorter events, 3.0 us)
Async XLA Ops:
  0.0 0.9 copy-start.4
  0.9 11.1 %copy-start = (bf16[512,128]{1,0:T(8,128)(2,1)}, bf16[512,128]{1,0:T(8,128)(2,1)S(1)}, u32[]{:S(2)}) copy-start(bf16[512,128]{1,0:T(8,128)(2,1)S(1)} %constant_dynamic-update-slice_fusion.refs_0_) | copy-start | bytes 393220
  0.9 8.0 %collective-permute-start.2 = (bf16[512,128]{1,0:T(8,128)(2,1)S(1)}, bf16[512,128]{1,0:T(8,128)(2,1)S(1)}, u32[]{:S(2)}, u32[]{:S(2)}) collective-permute-start(bf16[512,128]{1,0:T(8,128)(2,1)S(1)} %constant_dynamic-update-slice_fusion.refs_0_), channel_id=1, source_target_pairs={{0,64},{32,96},{64,0},{96,32},{1,65},{33,97},{65,1},{97,33},{2,66}... | collective-permute-start | bytes 393224 | tf_op jit(solution)/shard_map/ppermute | solution.py:25
  4.9 7.1 %collective-permute-start.1 = (bf16[512,128]{1,0:T(8,128)(2,1)S(1)}, bf16[512,128]{1,0:T(8,128)(2,1)S(1)}, u32[]{:S(2)}, u32[]{:S(2)}) collective-permute-start(bf16[512,128]{1,0:T(8,128)(2,1)S(1)} %constant_dynamic-update-slice_fusion.refs_0_), channel_id=1, source_target_pairs={{0,96},{32,0},{64,32},{96,64},{1,97},{33,1},{65,33},{97,65},{2,98}... | collective-permute-start | bytes 393224 | tf_op jit(solution)/shard_map/ppermute | solution.py:25
  5.6 6.4 %collective-permute-start = (bf16[512,128]{1,0:T(8,128)(2,1)S(1)}, bf16[512,128]{1,0:T(8,128)(2,1)S(1)}, u32[]{:S(2)}, u32[]{:S(2)}) collective-permute-start(bf16[512,128]{1,0:T(8,128)(2,1)S(1)} %constant_dynamic-update-slice_fusion.refs_0_), channel_id=1, source_target_pairs={{0,32},{32,64},{64,96},{96,0},{1,33},{33,65},{65,97},{97,1},{2,34}... | collective-permute-start | bytes 393224 | tf_op jit(solution)/shard_map/ppermute | solution.py:25
  6.9 5.1 %collective-permute-start.3 = (bf16[512,128]{1,0:T(8,128)(2,1)S(1)}, bf16[512,128]{1,0:T(8,128)(2,1)S(1)}, u32[]{:S(2)}, u32[]{:S(2)}) collective-permute-start(bf16[512,128]{1,0:T(8,128)(2,1)S(1)} %constant_dynamic-update-slice_fusion.refs_0_), channel_id=1, source_target_pairs={{0,8},{8,16},{16,24},{24,0},{1,9},{9,17},{17,25},{25,1},{2,10},{10... | collective-permute-start | bytes 393224 | tf_op jit(solution)/shard_map/ppermute | solution.py:25
  7.4 6.2 %collective-permute-start.4 = (bf16[512,128]{1,0:T(8,128)(2,1)S(1)}, bf16[512,128]{1,0:T(8,128)(2,1)S(1)}, u32[]{:S(2)}, u32[]{:S(2)}) collective-permute-start(bf16[512,128]{1,0:T(8,128)(2,1)S(1)} %constant_dynamic-update-slice_fusion.refs_0_), channel_id=1, source_target_pairs={{0,24},{8,0},{16,8},{24,16},{1,25},{9,1},{17,9},{25,17},{2,26},{10... | collective-permute-start | bytes 393224 | tf_op jit(solution)/shard_map/ppermute | solution.py:25
  13.5 8.9 %collective-permute-start.5 = (bf16[1536,128]{1,0:T(8,128)(2,1)S(1)}, bf16[1536,128]{1,0:T(8,128)(2,1)S(1)}, u32[]{:S(2)}, u32[]{:S(2)}) collective-permute-start(bf16[1536,128]{1,0:T(8,128)(2,1)S(1)} %pad_maximum_fusion.refs_1_), channel_id=1, source_target_pairs={{0,8},{8,16},{16,24},{24,0},{1,9},{9,17},{17,25},{25,1},{2,10},{10... | collective-permute-start | bytes 1179656 | tf_op jit(solution)/shard_map/ppermute | solution.py:25
  13.8 10.8 %collective-permute-start.7 = (bf16[1536,128]{1,0:T(8,128)(2,1)S(1)}, bf16[1536,128]{1,0:T(8,128)(2,1)S(1)}, u32[]{:S(2)}, u32[]{:S(2)}) collective-permute-start(bf16[1536,128]{1,0:T(8,128)(2,1)S(1)} %pad_maximum_fusion.refs_1_), channel_id=1, source_target_pairs={{0,24},{8,0},{16,8},{24,16},{1,25},{9,1},{17,9},{25,17},{2,26},{10... | collective-permute-start | bytes 1179656 | tf_op jit(solution)/shard_map/ppermute | solution.py:25
  15.6 25.0 %collective-permute-start.13 = (bf16[1024,512]{1,0:T(8,128)(2,1)}, bf16[1024,512]{1,0:T(8,128)(2,1)S(1)}, u32[]{:S(2)}, u32[]{:S(2)}) collective-permute-start(bf16[1024,512]{1,0:T(8,128)(2,1)} %refs_0_.2), channel_id=1, source_target_pairs={{0,32},{32,64},{64,96},{96,0},{1,33},{33,65},{65,97},{97,1},{2,34}... | collective-permute-start | bytes 3145736 | tf_op jit(solution)/shard_map/ppermute | solution.py:25
  16.6 24.5 %collective-permute-start.14 = (bf16[1024,512]{1,0:T(8,128)(2,1)}, bf16[1024,512]{1,0:T(8,128)(2,1)S(1)}, u32[]{:S(2)}, u32[]{:S(2)}) collective-permute-start(bf16[1024,512]{1,0:T(8,128)(2,1)} %refs_0_.2), channel_id=1, source_target_pairs={{0,96},{32,0},{64,32},{96,64},{1,97},{33,1},{65,33},{97,65},{2,98}... | collective-permute-start | bytes 3145736 | tf_op jit(solution)/shard_map/ppermute | solution.py:25
  23.1 2.8 %copy-start.8 = (s32[2,4]{1,0:T(2,128)S(1)}, s32[2,4]{1,0:T(2,128)}, u32[]{:S(2)}) copy-start(s32[2,4]{1,0:T(2,128)} %param.12) | copy-start | bytes 100
  23.1 3.4 %copy-start.5 = (s32[4096]{0:T(1024)S(1)}, s32[4096]{0:T(1024)}, u32[]{:S(2)}) copy-start(s32[4096]{0:T(1024)} %param.10) | copy-start | bytes 49156
  23.2 7.9 %collective-permute-start.6 = (bf16[1024,128]{1,0:T(8,128)(2,1)}, bf16[1024,128]{1,0:T(8,128)(2,1)}, u32[]{:S(2)}, u32[]{:S(2)}) collective-permute-start(bf16[1024,128]{1,0:T(8,128)(2,1)} %join.6), channel_id=1, source_target_pairs={{0,8},{8,16},{16,24},{24,0},{1,9},{9,17},{17,25},{25,1},{2,10},{10... | collective-permute-start | bytes 786440 | tf_op jit(solution)/shard_map/ppermute | solution.py:25
  25.4 7.9 %collective-permute-start.8 = (bf16[1024,128]{1,0:T(8,128)(2,1)}, bf16[1024,128]{1,0:T(8,128)(2,1)}, u32[]{:S(2)}, u32[]{:S(2)}) collective-permute-start(bf16[1024,128]{1,0:T(8,128)(2,1)} %join.7), channel_id=1, source_target_pairs={{0,24},{8,0},{16,8},{24,16},{1,25},{9,1},{17,9},{25,17},{2,26},{10... | collective-permute-start | bytes 786440 | tf_op jit(solution)/shard_map/ppermute | solution.py:25
  28.0 0.7 copy-start.6
  28.1 0.7 copy-start.7
  28.1 0.7 copy-start.9
  28.8 0.9 copy-start.1
  33.3 1.2 %copy-start.3 = (bf16[256,1024]{1,0:T(8,128)(2,1)S(1)}, bf16[256,1024]{1,0:T(8,128)(2,1)}, u32[]{:S(2)}) copy-start(bf16[256,1024]{1,0:T(8,128)(2,1)} %q.1) | copy-start | bytes 1572868
  38.4 12.1 %collective-permute-start.9 = (bf16[256,1024]{1,0:T(8,128)(2,1)S(1)}, bf16[256,1024]{1,0:T(8,128)(2,1)S(1)}, u32[]{:S(2)}, u32[]{:S(2)}) collective-permute-start(bf16[256,1024]{1,0:T(8,128)(2,1)S(1)} %attend.1.rows), channel_id=1, source_target_pairs={{0,8},{8,16},{16,24},{24,0},{1,9},{9,17},{17,25},{25,1},{2,10},{10... | collective-permute-start | bytes 1572872 | tf_op jit(solution)/shard_map/ppermute | solution.py:25
  38.8 12.1 %collective-permute-start.11 = (bf16[256,1024]{1,0:T(8,128)(2,1)S(1)}, bf16[256,1024]{1,0:T(8,128)(2,1)S(1)}, u32[]{:S(2)}, u32[]{:S(2)}) collective-permute-start(bf16[256,1024]{1,0:T(8,128)(2,1)S(1)} %attend.1.rows), channel_id=1, source_target_pairs={{0,24},{8,0},{16,8},{24,16},{1,25},{9,1},{17,9},{25,17},{2,26},{10... | collective-permute-start | bytes 1572872 | tf_op jit(solution)/shard_map/ppermute | solution.py:25
  40.6 12.4 %collective-permute-start.15 = (bf16[512,512]{1,0:T(8,128)(2,1)S(1)}, bf16[512,512]{1,0:T(8,128)(2,1)S(1)}, u32[]{:S(2)}, u32[]{:S(2)}) collective-permute-start(bf16[512,512]{1,0:T(8,128)(2,1)S(1)} %join.10), channel_id=1, source_target_pairs={{0,32},{32,64},{64,96},{96,0},{1,33},{33,65},{65,97},{97,1},{2,34}... | collective-permute-start | bytes 1572872 | tf_op jit(solution)/shard_map/ppermute | solution.py:25
  41.1 12.1 %copy-start.2 = (bf16[1024,512]{1,0:T(8,128)(2,1)S(1)}, bf16[1024,512]{1,0:T(8,128)(2,1)}, u32[]{:S(2)}) copy-start(bf16[1024,512]{1,0:T(8,128)(2,1)} %refs_0_.2) | copy-start | bytes 3145732
  41.1 12.0 %collective-permute-start.16 = (bf16[512,512]{1,0:T(8,128)(2,1)S(1)}, bf16[512,512]{1,0:T(8,128)(2,1)S(1)}, u32[]{:S(2)}, u32[]{:S(2)}) collective-permute-start(bf16[512,512]{1,0:T(8,128)(2,1)S(1)} %join.11), channel_id=1, source_target_pairs={{0,96},{32,0},{64,32},{96,64},{1,97},{33,1},{65,33},{97,65},{2,98}... | collective-permute-start | bytes 1572872 | tf_op jit(solution)/shard_map/ppermute | solution.py:25
  50.5 6.4 %collective-permute-start.10 = (bf16[128,1024]{1,0:T(8,128)(2,1)S(1)}, bf16[128,1024]{1,0:T(8,128)(2,1)S(1)}, u32[]{:S(2)}, u32[]{:S(2)}) collective-permute-start(bf16[128,1024]{1,0:T(8,128)(2,1)S(1)} %join.8), channel_id=1, source_target_pairs={{0,8},{8,16},{16,24},{24,0},{1,9},{9,17},{17,25},{25,1},{2,10},{10... | collective-permute-start | bytes 786440 | tf_op jit(solution)/shard_map/ppermute | solution.py:25
  50.9 7.9 %collective-permute-start.12 = (bf16[128,1024]{1,0:T(8,128)(2,1)S(1)}, bf16[128,1024]{1,0:T(8,128)(2,1)S(1)}, u32[]{:S(2)}, u32[]{:S(2)}) collective-permute-start(bf16[128,1024]{1,0:T(8,128)(2,1)S(1)} %join.9), channel_id=1, source_target_pairs={{0,24},{8,0},{16,8},{24,16},{1,25},{9,1},{17,9},{25,17},{2,26},{10... | collective-permute-start | bytes 786440 | tf_op jit(solution)/shard_map/ppermute | solution.py:25
  56.8 3.4 %collective-permute-start.22 = (bf16[4,256,512]{2,1,0:T(8,128)(2,1)S(1)}, bf16[4,256,512]{2,1,0:T(8,128)(2,1)S(1)}, u32[]{:S(2)}, u32[]{:S(2)}) collective-permute-start(bf16[4,256,512]{2,1,0:T(8,128)(2,1)S(1)} %get-tuple-element.50), channel_id=1, source_target_pairs={{0,1},{1,0},{2,3},{3,2},{4,5},{5,4},{6,7},{7,6},{8,9},{9,8},{10,11... | collective-permute-start | bytes 3145736 | tf_op jit(solution)/shard_map/ppermute | solution.py:29
  60.2 2.7 %collective-permute-start.17 = (bf16[4,256,512]{2,1,0:T(8,128)(2,1)S(1)}, bf16[4,256,512]{2,1,0:T(8,128)(2,1)S(1)}, u32[]{:S(2)}, u32[]{:S(2)}) collective-permute-start(bf16[4,256,512]{2,1,0:T(8,128)(2,1)S(1)} %get-tuple-element.43), channel_id=1, source_target_pairs={{0,1},{1,0},{2,3},{3,2},{4,5},{5,4},{6,7},{7,6},{8,9},{9,8},{10,11... | collective-permute-start | bytes 3145736 | tf_op jit(solution)/shard_map/ppermute | solution.py:29
  60.8 7.7 %collective-permute-start.24 = (bf16[256,512]{1,0:T(8,128)(2,1)S(1)}, bf16[256,512]{1,0:T(8,128)(2,1)S(1)}, u32[]{:S(2)}, u32[]{:S(2)}) collective-permute-start(bf16[256,512]{1,0:T(8,128)(2,1)S(1)} %get-tuple-element.54), channel_id=1, source_target_pairs={{0,2},{1,7},{2,4},{3,1},{4,6},{5,3},{6,0},{7,5},{8,10},{9,15},{10,... | collective-permute-start | bytes 786440 | tf_op jit(solution)/shard_map/ppermute | solution.py:297
  63.4 7.8 %collective-permute-start.19 = (bf16[256,512]{1,0:T(8,128)(2,1)S(1)}, bf16[256,512]{1,0:T(8,128)(2,1)S(1)}, u32[]{:S(2)}, u32[]{:S(2)}) collective-permute-start(bf16[256,512]{1,0:T(8,128)(2,1)S(1)} %get-tuple-element.47), channel_id=1, source_target_pairs={{0,2},{1,7},{2,4},{3,1},{4,6},{5,3},{6,0},{7,5},{8,10},{9,15},{10,... | collective-permute-start | bytes 786440 | tf_op jit(solution)/shard_map/ppermute | solution.py:297
  68.5 8.0 %collective-permute-start.25 = (bf16[256,512]{1,0:T(8,128)(2,1)S(1)}, bf16[256,512]{1,0:T(8,128)(2,1)S(1)}, u32[]{:S(2)}, u32[]{:S(2)}) collective-permute-start(bf16[256,512]{1,0:T(8,128)(2,1)S(1)} %add_convert_fusion.2), channel_id=1, source_target_pairs={{0,2},{1,7},{2,4},{3,1},{4,6},{5,3},{6,0},{7,5},{8,10},{9,15},{10,... | collective-permute-start | bytes 786440 | tf_op jit(solution)/shard_map/ppermute | solution.py:297
  71.3 7.7 %collective-permute-start.20 = (bf16[256,512]{1,0:T(8,128)(2,1)S(1)}, bf16[256,512]{1,0:T(8,128)(2,1)S(1)}, u32[]{:S(2)}, u32[]{:S(2)}) collective-permute-start(bf16[256,512]{1,0:T(8,128)(2,1)S(1)} %add_convert_fusion.5), channel_id=1, source_target_pairs={{0,2},{1,7},{2,4},{3,1},{4,6},{5,3},{6,0},{7,5},{8,10},{9,15},{10,... | collective-permute-start | bytes 786440 | tf_op jit(solution)/shard_map/ppermute | solution.py:297
  71.8 7.6 %collective-permute-start.23 = (bf16[256,512]{1,0:T(8,128)(2,1)S(1)}, bf16[256,512]{1,0:T(8,128)(2,1)S(1)}, u32[]{:S(2)}, u32[]{:S(2)}) collective-permute-start(bf16[256,512]{1,0:T(8,128)(2,1)S(1)} %get-tuple-element.51), channel_id=1, source_target_pairs={{0,24},{1,8},{2,26},{3,10},{4,28},{5,12},{6,30},{7,14},{8,0},{9,16... | collective-permute-start | bytes 786440 | tf_op jit(solution)/shard_map/ppermute | solution.py:307
  73.6 16.7 %collective-permute-start.18 = (bf16[256,512]{1,0:T(8,128)(2,1)S(1)}, bf16[256,512]{1,0:T(8,128)(2,1)S(1)}, u32[]{:S(2)}, u32[]{:S(2)}) collective-permute-start(bf16[256,512]{1,0:T(8,128)(2,1)S(1)} %get-tuple-element.44), channel_id=1, source_target_pairs={{0,0},{1,16},{2,2},{3,18},{4,4},{5,20},{6,6},{7,22},{8,8},{9,24},{... | collective-permute-start | bytes 786440 | tf_op jit(solution)/shard_map/ppermute | solution.py:307
  76.6 13.6 %collective-permute-start.26 = (bf16[256,512]{1,0:T(8,128)(2,1)S(1)}, bf16[256,512]{1,0:T(8,128)(2,1)S(1)}, u32[]{:S(2)}, u32[]{:S(2)}) collective-permute-start(bf16[256,512]{1,0:T(8,128)(2,1)S(1)} %add_convert_fusion.1), channel_id=1, source_target_pairs={{0,26},{1,14},{2,28},{3,8},{4,30},{5,10},{6,24},{7,12},{8,2},{9,22... | collective-permute-start | bytes 786440 | tf_op jit(solution)/shard_map/ppermute | solution.py:307
  79.0 11.3 %collective-permute-start.21 = (bf16[256,512]{1,0:T(8,128)(2,1)S(1)}, bf16[256,512]{1,0:T(8,128)(2,1)S(1)}, u32[]{:S(2)}, u32[]{:S(2)}) collective-permute-start(bf16[256,512]{1,0:T(8,128)(2,1)S(1)} %add_convert_fusion.4), channel_id=1, source_target_pairs={{0,2},{1,22},{2,4},{3,16},{4,6},{5,18},{6,0},{7,20},{8,10},{9,30},... | collective-permute-start | bytes 786440 | tf_op jit(solution)/shard_map/ppermute | solution.py:307

commit v6 on v5

--- a/solution.py
+++ b/solution.py
@@ -12,7 +12,7 @@
 DH = 128
 RUN = 64
 DOCS = 8
-SIZES = (256, 512, 768, 1024, 1152, 1536, 2304)
+SIZES = (256, 384, 512, 640, 768, 896, 1024, 1152, 1536, 2304)
 NEGATIVE = -1e30
 Z = ("zh", "zl")
 
@@ -171,6 +171,28 @@
     )(runs, q, *ordered)
 
 
+def far_parts_kernel(cut, line_left, left, line_right, right, upper, lower):
+    count = left.shape[0] // 2
+    upper[:cut, :] = line_left[:cut, :]
+    upper[cut:, :] = left[:count, :]
+    lower[:cut, :] = line_right[cut:, :]
+    lower[cut:, :] = right[count:, :]
+
+
+def far_parts(line_left, left, line_right, right):
+    cut, count = line_left.shape[0] // 2, left.shape[0] // 2
+    half = jax.ShapeDtypeStruct((cut + count, left.shape[1]), left.dtype)
+    return pl.pallas_call(
+        functools.partial(far_parts_kernel, cut),
+        out_shape=[half, half],
+        in_specs=[VMEM] * 4,
+        out_specs=[VMEM] * 2,
+        compiler_params=pltpu.CompilerParams(vmem_limit_bytes=4 * 2**20),
+        cost_estimate=pl.CostEstimate(flops=0, bytes_accessed=2**20, transcendentals=0),
+        name="far_parts",
+    )(line_left, left, line_right, right)
+
+
 def join_kernel(ranges, *refs):
     row = 0
     for ref, (first, last) in zip(refs, ranges):
@@ -346,8 +368,8 @@
 
     here = [(0, 0), (0, 1)]
     ordered = place(runs, slots, (at_x(0, here), at_x(0), at_x(3, here), at_x(1, here)), (kv, line, left, right))
-    left2 = shift(join((line_left, left), ((0, 3 * count), (0, count))), "x", 1)
-    right2 = shift(join((line_right, right), ((3 * count, 6 * count), (count, 2 * count))), "x", -1)
+    left2, right2 = far_parts(line_left, left, line_right, right)
+    left2, right2 = shift(left2, "x", 1), shift(right2, "x", -1)
     ordered = place(runs, slots, (at_x(3), at_x(1)), (line_left, line_right), ordered)
     ordered = place(
         runs,

time: 92.4 us -> 91.3 us (0.988)
    pallas_call x6 -> x4, Pallas kernels: 1.55 us -> 0.11 us  [join(): pl.pallas_call(functools.partial(join_kernel, ranges), out_shape=jax.Shap...]
  transfers between devices with their start and end apart: 27 -> 27, of which waited for: 13 -> 14; matrix products, arithmetic and copies ran while one was open for 3% -> 3% of each run, Pallas kernels for 15% -> 15%
where the time goes in v6:
time: 91.3 us; the launch traced here: 90.5 us
  waiting for transfers between devices  37.9 us (42%)
  starting transfers between devices  32.6 us (36%)
  Pallas kernels  13.6 us (15%)
  local copies, waits for them, and re-layouts  4.59 us (5%)
  other arithmetic  1.44 us (2%)
    ppermute x17, starting transfers between devices, shift(): return lax.ppermute(value, axis, [(i, (i + step) % 4) for i in range(4)])  23.3 us
    ppermute x17, waiting for transfers between devices, shift(): return lax.ppermute(value, axis, [(i, (i + step) % 4) for i in range(4)])  18.6 us
    ppermute x4, waiting for transfers between devices, home(): return lax.ppermute(value, ('x', 'y', 'c'), pairs)  10.4 us
    ppermute x4, waiting for transfers between devices, relay(): return lax.ppermute(value, (axis, 'c'), pairs)  8.43 us
    ppermute x4, starting transfers between devices, home(): return lax.ppermute(value, ('x', 'y', 'c'), pairs)  5 us
    pallas_call x3, Pallas kernels, project(): pl.pallas_call(kernel, out_shape=[result] * results, in_specs=[VMEM] * (l...  4.97 us
    pallas_call x1, Pallas kernels, attend(): pl.pallas_call(attend_kernel, out_shape=jax.ShapeDtypeStruct((rows, width...  4.17 us
    ppermute x4, starting transfers between devices, relay(): return lax.ppermute(value, (axis, 'c'), pairs)  4.16 us
  transfers between devices with their start and end apart: 27, of which 14 were waited for; matrix products, arithmetic and copies ran while one was open for 3% of the time, Pallas kernels for 15%

profile of v6, /device:TPU:6, one launch (start us, length us, event | category | flops | bytes accessed | tf_op | source)
XLA Modules:
  0.0 90.5 jit_solution(3491593574547791105)
XLA Ops:
  0.0 0.9 constant_dynamic-update-slice_fusion.1
  0.9 4.0 %collective-permute-start.2 = (bf16[512,128]{1,0:T(8,128)(2,1)S(1)}, bf16[512,128]{1,0:T(8,128)(2,1)S(1)}, u32[]{:S(2)}, u32[]{:S(2)}) collective-permute-start(bf16[512,128]{1,0:T(8,128)(2,1)S(1)} %constant_dynamic-update-slice_fusion.refs_0_), channel_id=1, source_target_pairs={{0,64},{32,96},{64,0},{96,32},{1,65},{33,97},{65,1},{97,33},{2,66}... | collective-permute-start | bytes 393224 | tf_op jit(solution)/shard_map/ppermute | solution.py:25
  4.9 0.7 collective-permute-start.1
  5.6 1.3 %collective-permute-start = (bf16[512,128]{1,0:T(8,128)(2,1)S(1)}, bf16[512,128]{1,0:T(8,128)(2,1)S(1)}, u32[]{:S(2)}, u32[]{:S(2)}) collective-permute-start(bf16[512,128]{1,0:T(8,128)(2,1)S(1)} %constant_dynamic-update-slice_fusion.refs_0_), channel_id=1, source_target_pairs={{0,32},{32,64},{64,96},{96,0},{1,33},{33,65},{65,97},{97,1},{2,34}... | collective-permute-start | bytes 393224 | tf_op jit(solution)/shard_map/ppermute | solution.py:25
  6.9 0.5 collective-permute-start.3
  7.4 1.5 %collective-permute-start.4 = (bf16[512,128]{1,0:T(8,128)(2,1)S(1)}, bf16[512,128]{1,0:T(8,128)(2,1)S(1)}, u32[]{:S(2)}, u32[]{:S(2)}) collective-permute-start(bf16[512,128]{1,0:T(8,128)(2,1)S(1)} %constant_dynamic-update-slice_fusion.refs_0_), channel_id=1, source_target_pairs={{0,24},{8,0},{16,8},{24,16},{1,25},{9,1},{17,9},{25,17},{2,26},{10... | collective-permute-start | bytes 393224 | tf_op jit(solution)/shard_map/ppermute | solution.py:25
  8.9 3.0 %collective-permute-done.1 = bf16[512,128]{1,0:T(8,128)(2,1)S(1)} collective-permute-done((bf16[512,128]{1,0:T(8,128)(2,1)S(1)}, bf16[512,128]{1,0:T(8,128)(2,1)S(1)}, u32[]{:S(2)}, u32[]{:S(2)}) %collective-permute-start.1) | collective-permute-done | bytes 131104 | tf_op jit(solution)/shard_map/ppermute | solution.py:25
  12.0 1.5 %collective-permute-done.4.right.refs_3_ = bf16[512,128]{1,0:T(8,128)(2,1)S(1)} collective-permute-done((bf16[512,128]{1,0:T(8,128)(2,1)S(1)}, bf16[512,128]{1,0:T(8,128)(2,1)S(1)}, u32[]{:S(2)}, u32[]{:S(2)}) %collective-permute-start.4) | collective-permute-done | bytes 131104 | tf_op jit(solution)/shard_map/ppermute | solution.py:25
  13.8 1.7 %collective-permute-start.6 = (bf16[1536,128]{1,0:T(8,128)(2,1)S(1)}, bf16[1536,128]{1,0:T(8,128)(2,1)S(1)}, u32[]{:S(2)}, u32[]{:S(2)}) collective-permute-start(bf16[1536,128]{1,0:T(8,128)(2,1)S(1)} %pad_maximum_fusion.refs_1_), channel_id=1, source_target_pairs={{0,24},{8,0},{16,8},{24,16},{1,25},{9,1},{17,9},{25,17},{2,26},{10... | collective-permute-start | bytes 1179656 | tf_op jit(solution)/shard_map/ppermute | solution.py:25
  15.6 1.0 %collective-permute-start.13 = (bf16[1024,512]{1,0:T(8,128)(2,1)}, bf16[1024,512]{1,0:T(8,128)(2,1)S(1)}, u32[]{:S(2)}, u32[]{:S(2)}) collective-permute-start(bf16[1024,512]{1,0:T(8,128)(2,1)} %refs_0_.2), channel_id=1, source_target_pairs={{0,32},{32,64},{64,96},{96,0},{1,33},{33,65},{65,97},{97,1},{2,34}... | collective-permute-start | bytes 3145736 | tf_op jit(solution)/shard_map/ppermute | solution.py:25
  16.6 2.2 %collective-permute-start.14 = (bf16[1024,512]{1,0:T(8,128)(2,1)}, bf16[1024,512]{1,0:T(8,128)(2,1)S(1)}, u32[]{:S(2)}, u32[]{:S(2)}) collective-permute-start(bf16[1024,512]{1,0:T(8,128)(2,1)} %refs_0_.2), channel_id=1, source_target_pairs={{0,96},{32,0},{64,32},{96,64},{1,97},{33,1},{65,33},{97,65},{2,98}... | collective-permute-start | bytes 3145736 | tf_op jit(solution)/shard_map/ppermute | solution.py:25
  18.8 3.6 %collective-permute-done.5.line_left.refs_0_ = bf16[1536,128]{1,0:T(8,128)(2,1)S(1)} collective-permute-done((bf16[1536,128]{1,0:T(8,128)(2,1)S(1)}, bf16[1536,128]{1,0:T(8,128)(2,1)S(1)}, u32[]{:S(2)}, u32[]{:S(2)}) %collective-permute-start.5) | collective-permute-done | bytes 393248 | tf_op jit(solution)/shard_map/ppermute | solution.py:25
  22.4 1.2 %collective-permute-done.6.line_right.refs_1_ = bf16[1536,128]{1,0:T(8,128)(2,1)S(1)} collective-permute-done((bf16[1536,128]{1,0:T(8,128)(2,1)S(1)}, bf16[1536,128]{1,0:T(8,128)(2,1)S(1)}, u32[]{:S(2)}, u32[]{:S(2)}) %collective-permute-start.6) | collective-permute-done | bytes 393248 | tf_op jit(solution)/shard_map/ppermute | solution.py:25
  23.6 0.8 far_parts.1
  24.8 1.7 %collective-permute-start.8 = (bf16[1024,128]{1,0:T(8,128)(2,1)}, bf16[1024,128]{1,0:T(8,128)(2,1)}, u32[]{:S(2)}, u32[]{:S(2)}) collective-permute-start(bf16[1024,128]{1,0:T(8,128)(2,1)} %get-tuple-element.36), channel_id=1, source_target_pairs={{0,24},{8,0},{16,8},{24,16},{1,25},{9,1},{17,9},{25,17},{2,26},{10... | collective-permute-start | bytes 786440 | tf_op jit(solution)/shard_map/ppermute | solution.py:25
  26.5 0.6 slice_bitcast_fusion.1
  27.1 0.7 reshape.3
  27.8 0.9 slice_reduce_fusion
  28.6 0.6 copy-done.6
  29.4 0.9 copy-done.1
  30.3 0.7 place.3
  31.0 0.7 place.4
  31.7 1.0 %collective-permute-done.8.refs_1_ = bf16[1024,128]{1,0:T(8,128)(2,1)} collective-permute-done((bf16[1024,128]{1,0:T(8,128)(2,1)}, bf16[1024,128]{1,0:T(8,128)(2,1)}, u32[]{:S(2)}, u32[]{:S(2)}) %collective-permute-start.8) | collective-permute-done | bytes 262176 | tf_op jit(solution)/shard_map/ppermute | solution.py:25
  32.7 1.2 %place.5 = (bf16[4096,128]{1,0:T(8,128)(2,1)S(1)}, bf16[4096,128]{1,0:T(8,128)(2,1)S(1)}) custom-call(s32[80]{0:T(128)S(1)} %pad_add_fusion.pos, bf16[1024,128]{1,0:T(8,128)(2,1)} %collective-permute-done.7.refs_0_, bf16[1024,128]{1,0:T(8,128)(2,1)} %collective-permute-done.8.refs_1_, ...), custom_call_target="tpu_custom_call", output_to_operand_aliasing={{0}: (3, {}), {1}: (4, {})} | custom-call | bytes 2097152 | tf_op jit(solution)/shard_map/place/pallas_call | solution.py:58
  33.9 4.2 %attend.1.rows = bf16[256,1024]{1,0:T(8,128)(2,1)S(1)} custom-call(s32[80]{0:T(128)S(1)} %pad_add_fusion.pos, bf16[256,1024]{1,0:T(8,128)(2,1)S(1)} %copy-done.3, bf16[4096,128]{1,0:T(8,128)(2,1)S(1)} %get-tuple-element.41.ks, bf16[4096,128]{1,0:T(8,128)(2,1)S(1)} %get-tuple-element.42.vs), custom_call_target="tpu_custom_call" | custom-call | flops 6442450944 | bytes 4194304 | tf_op jit(solution)/shard_map/attend/pallas_call | solution.py:161
  38.1 2.0 %collective-permute-start.11 = (bf16[256,1024]{1,0:T(8,128)(2,1)S(1)}, bf16[256,1024]{1,0:T(8,128)(2,1)S(1)}, u32[]{:S(2)}, u32[]{:S(2)}) collective-permute-start(bf16[256,1024]{1,0:T(8,128)(2,1)S(1)} %attend.1.rows), channel_id=1, source_target_pairs={{0,24},{8,0},{16,8},{24,16},{1,25},{9,1},{17,9},{25,17},{2,26},{10... | collective-permute-start | bytes 1572872 | tf_op jit(solution)/shard_map/ppermute | solution.py:25
  40.3 3.4 %collective-permute-start.16 = (bf16[512,512]{1,0:T(8,128)(2,1)S(1)}, bf16[512,512]{1,0:T(8,128)(2,1)S(1)}, u32[]{:S(2)}, u32[]{:S(2)}) collective-permute-start(bf16[512,512]{1,0:T(8,128)(2,1)S(1)} %join.7), channel_id=1, source_target_pairs={{0,96},{32,0},{64,32},{96,64},{1,97},{33,1},{65,33},{97,65},{2,98}... | collective-permute-start | bytes 1572872 | tf_op jit(solution)/shard_map/ppermute | solution.py:25
  43.8 6.3 %collective-permute-done.9.refs_0_.left = bf16[256,1024]{1,0:T(8,128)(2,1)S(1)} collective-permute-done((bf16[256,1024]{1,0:T(8,128)(2,1)S(1)}, bf16[256,1024]{1,0:T(8,128)(2,1)S(1)}, u32[]{:S(2)}, u32[]{:S(2)}) %collective-permute-start.9) | collective-permute-done | bytes 524320 | tf_op jit(solution)/shard_map/ppermute | solution.py:25
  50.2 2.3 %collective-permute-start.12 = (bf16[128,1024]{1,0:T(8,128)(2,1)S(1)}, bf16[128,1024]{1,0:T(8,128)(2,1)S(1)}, u32[]{:S(2)}, u32[]{:S(2)}) collective-permute-start(bf16[128,1024]{1,0:T(8,128)(2,1)S(1)} %join.5), channel_id=1, source_target_pairs={{0,24},{8,0},{16,8},{24,16},{1,25},{9,1},{17,9},{25,17},{2,26},{10... | collective-permute-start | bytes 786440 | tf_op jit(solution)/shard_map/ppermute | solution.py:25
  52.5 1.2 %project.3.own = bf16[4,256,512]{2,1,0:T(8,128)(2,1)S(1)} custom-call(bf16[256,1024]{1,0:T(8,128)(2,1)S(1)} %attend.1.rows, bf16[1024,512]{1,0:T(8,128)(2,1)S(1)} %copy-done.2, bf16[1024,512]{1,0:T(8,128)(2,1)S(1)} %collective-permute-done.13.refs_0_.refs_1_, bf16[1024,512]{1,0:T(8,128)(2,1)S(1)} %collective-permute-done.14.refs_0_.refs_2_, ...), custom_call_target="tpu_custom_call" | custom-call | flops 2147483648 | bytes 4194304 | tf_op jit(solution)/shard_map/project/pallas_call | solution.py:277
  53.8 2.4 %project.5 = (bf16[4,256,512]{2,1,0:T(8,128)(2,1)S(1)}, bf16[4,256,512]{2,1,0:T(8,128)(2,1)S(1)}) custom-call(bf16[256,1024]{1,0:T(8,128)(2,1)S(1)} %collective-permute-done.9.refs_0_.left, bf16[256,1024]{1,0:T(8,128)(2,1)S(1)} %collective-permute-done.11.refs_0_.right, bf16[1024,512]{1,0:T(8,128)(2,1)S(1)} %copy-done.2, ...), custom_call_target="tpu_custom_call" | custom-call | flops 2147483648 | bytes 4194304 | tf_op jit(solution)/shard_map/project/pallas_call | solution.py:277
  56.6 1.6 %collective-permute-done.12.lower = bf16[128,1024]{1,0:T(8,128)(2,1)S(1)} collective-permute-done((bf16[128,1024]{1,0:T(8,128)(2,1)S(1)}, bf16[128,1024]{1,0:T(8,128)(2,1)S(1)}, u32[]{:S(2)}, u32[]{:S(2)}) %collective-permute-start.12) | collective-permute-done | bytes 262176 | tf_op jit(solution)/shard_map/ppermute | solution.py:25
  58.1 1.3 %project.4 = (bf16[4,256,512]{2,1,0:T(8,128)(2,1)S(1)}, bf16[4,256,512]{2,1,0:T(8,128)(2,1)S(1)}) custom-call(bf16[128,1024]{1,0:T(8,128)(2,1)S(1)} %collective-permute-done.10.upper, bf16[128,1024]{1,0:T(8,128)(2,1)S(1)} %collective-permute-done.12.lower, bf16[4,256,512]{2,1,0:T(8,128)(2,1)S(1)} %project.3.own, bf16[1024,512]{1,0:T(8,128)(2,1)S(1)} %copy-done.2, ...), custom_call_target="tpu_custom_call" | custom-call | flops 2147483648 | bytes 4194304 | tf_op jit(solution)/shard_map/project/pallas_call | solution.py:277
  59.6 0.5 combine.3
  60.1 1.6 %collective-permute-start.24 = (bf16[256,512]{1,0:T(8,128)(2,1)S(1)}, bf16[256,512]{1,0:T(8,128)(2,1)S(1)}, u32[]{:S(2)}, u32[]{:S(2)}) collective-permute-start(bf16[256,512]{1,0:T(8,128)(2,1)S(1)} %get-tuple-element.58), channel_id=1, source_target_pairs={{0,2},{1,7},{2,4},{3,1},{4,6},{5,3},{6,0},{7,5},{8,10},{9,15},{10,... | collective-permute-start | bytes 786440 | tf_op jit(solution)/shard_map/ppermute | solution.py:319
  61.8 0.5 collective-permute-done.17.got
  62.2 0.5 combine.2
  62.7 1.6 %collective-permute-start.19 = (bf16[256,512]{1,0:T(8,128)(2,1)S(1)}, bf16[256,512]{1,0:T(8,128)(2,1)S(1)}, u32[]{:S(2)}, u32[]{:S(2)}) collective-permute-start(bf16[256,512]{1,0:T(8,128)(2,1)S(1)} %get-tuple-element.51), channel_id=1, source_target_pairs={{0,2},{1,7},{2,4},{3,1},{4,6},{5,3},{6,0},{7,5},{8,10},{9,15},{10,... | collective-permute-start | bytes 786440 | tf_op jit(solution)/shard_map/ppermute | solution.py:319
  64.4 3.4 %collective-permute-done.24 = bf16[256,512]{1,0:T(8,128)(2,1)S(1)} collective-permute-done((bf16[256,512]{1,0:T(8,128)(2,1)S(1)}, bf16[256,512]{1,0:T(8,128)(2,1)S(1)}, u32[]{:S(2)}, u32[]{:S(2)}) %collective-permute-start.24) | collective-permute-done | bytes 262176 | tf_op jit(solution)/shard_map/ppermute | solution.py:319
  67.8 0.4 collective-permute-start.25
  68.3 2.3 %collective-permute-done.19 = bf16[256,512]{1,0:T(8,128)(2,1)S(1)} collective-permute-done((bf16[256,512]{1,0:T(8,128)(2,1)S(1)}, bf16[256,512]{1,0:T(8,128)(2,1)S(1)}, u32[]{:S(2)}, u32[]{:S(2)}) %collective-permute-start.19) | collective-permute-done | bytes 262176 | tf_op jit(solution)/shard_map/ppermute | solution.py:319
  70.6 0.4 collective-permute-start.20
  71.1 2.1 %collective-permute-start.23 = (bf16[256,512]{1,0:T(8,128)(2,1)S(1)}, bf16[256,512]{1,0:T(8,128)(2,1)S(1)}, u32[]{:S(2)}, u32[]{:S(2)}) collective-permute-start(bf16[256,512]{1,0:T(8,128)(2,1)S(1)} %get-tuple-element.55), channel_id=1, source_target_pairs={{0,24},{1,8},{2,26},{3,10},{4,28},{5,12},{6,30},{7,14},{8,0},{9,16... | collective-permute-start | bytes 786440 | tf_op jit(solution)/shard_map/ppermute | solution.py:329
  73.2 2.0 %collective-permute-start.18 = (bf16[256,512]{1,0:T(8,128)(2,1)S(1)}, bf16[256,512]{1,0:T(8,128)(2,1)S(1)}, u32[]{:S(2)}, u32[]{:S(2)}) collective-permute-start(bf16[256,512]{1,0:T(8,128)(2,1)S(1)} %get-tuple-element.48), channel_id=1, source_target_pairs={{0,0},{1,16},{2,2},{3,18},{4,4},{5,20},{6,6},{7,22},{8,8},{9,24},{... | collective-permute-start | bytes 786440 | tf_op jit(solution)/shard_map/ppermute | solution.py:329
  75.8 2.4 %collective-permute-done.20 = bf16[256,512]{1,0:T(8,128)(2,1)S(1)} collective-permute-done((bf16[256,512]{1,0:T(8,128)(2,1)S(1)}, bf16[256,512]{1,0:T(8,128)(2,1)S(1)}, u32[]{:S(2)}, u32[]{:S(2)}) %collective-permute-start.20) | collective-permute-done | bytes 262176 | tf_op jit(solution)/shard_map/ppermute | solution.py:319
  78.4 0.6 collective-permute-start.21
  79.0 10.4 %collective-permute-done.26 = bf16[256,512]{1,0:T(8,128)(2,1)S(1)} collective-permute-done((bf16[256,512]{1,0:T(8,128)(2,1)S(1)}, bf16[256,512]{1,0:T(8,128)(2,1)S(1)}, u32[]{:S(2)}, u32[]{:S(2)}) %collective-permute-start.26) | collective-permute-done | bytes 262176 | tf_op jit(solution)/shard_map/ppermute | solution.py:329
  89.6 0.9 %maximum_select_fusion = bf16[256,1024]{1,0:T(8,128)(2,1)} fusion(bf16[256,512]{1,0:T(8,128)(2,1)S(1)} %add_convert_fusion, bf16[256,512]{1,0:T(8,128)(2,1)S(1)} %add_convert_fusion.3, pred[]{:T(512)S(6)} %eq.3), kind=kLoop, calls=%fused_computation | loop fusion | flops 2359296 | bytes 1048577 | tf_op jit(solution)/shard_map/jit(_where)/select_n | solution.py:397
  (54 shorter events, 2.6 us)
Async XLA Ops:
  0.0 0.9 copy-start.4
  0.9 11.1 %copy-start = (bf16[512,128]{1,0:T(8,128)(2,1)}, bf16[512,128]{1,0:T(8,128)(2,1)S(1)}, u32[]{:S(2)}) copy-start(bf16[512,128]{1,0:T(8,128)(2,1)S(1)} %constant_dynamic-update-slice_fusion.refs_0_) | copy-start | bytes 393220
  0.9 8.0 %collective-permute-start.2 = (bf16[512,128]{1,0:T(8,128)(2,1)S(1)}, bf16[512,128]{1,0:T(8,128)(2,1)S(1)}, u32[]{:S(2)}, u32[]{:S(2)}) collective-permute-start(bf16[512,128]{1,0:T(8,128)(2,1)S(1)} %constant_dynamic-update-slice_fusion.refs_0_), channel_id=1, source_target_pairs={{0,64},{32,96},{64,0},{96,32},{1,65},{33,97},{65,1},{97,33},{2,66}... | collective-permute-start | bytes 393224 | tf_op jit(solution)/shard_map/ppermute | solution.py:25
  4.9 7.1 %collective-permute-start.1 = (bf16[512,128]{1,0:T(8,128)(2,1)S(1)}, bf16[512,128]{1,0:T(8,128)(2,1)S(1)}, u32[]{:S(2)}, u32[]{:S(2)}) collective-permute-start(bf16[512,128]{1,0:T(8,128)(2,1)S(1)} %constant_dynamic-update-slice_fusion.refs_0_), channel_id=1, source_target_pairs={{0,96},{32,0},{64,32},{96,64},{1,97},{33,1},{65,33},{97,65},{2,98}... | collective-permute-start | bytes 393224 | tf_op jit(solution)/shard_map/ppermute | solution.py:25
  5.6 6.4 %collective-permute-start = (bf16[512,128]{1,0:T(8,128)(2,1)S(1)}, bf16[512,128]{1,0:T(8,128)(2,1)S(1)}, u32[]{:S(2)}, u32[]{:S(2)}) collective-permute-start(bf16[512,128]{1,0:T(8,128)(2,1)S(1)} %constant_dynamic-update-slice_fusion.refs_0_), channel_id=1, source_target_pairs={{0,32},{32,64},{64,96},{96,0},{1,33},{33,65},{65,97},{97,1},{2,34}... | collective-permute-start | bytes 393224 | tf_op jit(solution)/shard_map/ppermute | solution.py:25
  6.9 5.1 %collective-permute-start.3 = (bf16[512,128]{1,0:T(8,128)(2,1)S(1)}, bf16[512,128]{1,0:T(8,128)(2,1)S(1)}, u32[]{:S(2)}, u32[]{:S(2)}) collective-permute-start(bf16[512,128]{1,0:T(8,128)(2,1)S(1)} %constant_dynamic-update-slice_fusion.refs_0_), channel_id=1, source_target_pairs={{0,8},{8,16},{16,24},{24,0},{1,9},{9,17},{17,25},{25,1},{2,10},{10... | collective-permute-start | bytes 393224 | tf_op jit(solution)/shard_map/ppermute | solution.py:25
  7.4 6.2 %collective-permute-start.4 = (bf16[512,128]{1,0:T(8,128)(2,1)S(1)}, bf16[512,128]{1,0:T(8,128)(2,1)S(1)}, u32[]{:S(2)}, u32[]{:S(2)}) collective-permute-start(bf16[512,128]{1,0:T(8,128)(2,1)S(1)} %constant_dynamic-update-slice_fusion.refs_0_), channel_id=1, source_target_pairs={{0,24},{8,0},{16,8},{24,16},{1,25},{9,1},{17,9},{25,17},{2,26},{10... | collective-permute-start | bytes 393224 | tf_op jit(solution)/shard_map/ppermute | solution.py:25
  13.5 8.9 %collective-permute-start.5 = (bf16[1536,128]{1,0:T(8,128)(2,1)S(1)}, bf16[1536,128]{1,0:T(8,128)(2,1)S(1)}, u32[]{:S(2)}, u32[]{:S(2)}) collective-permute-start(bf16[1536,128]{1,0:T(8,128)(2,1)S(1)} %pad_maximum_fusion.refs_1_), channel_id=1, source_target_pairs={{0,8},{8,16},{16,24},{24,0},{1,9},{9,17},{17,25},{25,1},{2,10},{10... | collective-permute-start | bytes 1179656 | tf_op jit(solution)/shard_map/ppermute | solution.py:25
  13.8 9.8 %collective-permute-start.6 = (bf16[1536,128]{1,0:T(8,128)(2,1)S(1)}, bf16[1536,128]{1,0:T(8,128)(2,1)S(1)}, u32[]{:S(2)}, u32[]{:S(2)}) collective-permute-start(bf16[1536,128]{1,0:T(8,128)(2,1)S(1)} %pad_maximum_fusion.refs_1_), channel_id=1, source_target_pairs={{0,24},{8,0},{16,8},{24,16},{1,25},{9,1},{17,9},{25,17},{2,26},{10... | collective-permute-start | bytes 1179656 | tf_op jit(solution)/shard_map/ppermute | solution.py:25
  15.6 24.6 %collective-permute-start.13 = (bf16[1024,512]{1,0:T(8,128)(2,1)}, bf16[1024,512]{1,0:T(8,128)(2,1)S(1)}, u32[]{:S(2)}, u32[]{:S(2)}) collective-permute-start(bf16[1024,512]{1,0:T(8,128)(2,1)} %refs_0_.2), channel_id=1, source_target_pairs={{0,32},{32,64},{64,96},{96,0},{1,33},{33,65},{65,97},{97,1},{2,34}... | collective-permute-start | bytes 3145736 | tf_op jit(solution)/shard_map/ppermute | solution.py:25
  16.6 23.7 %collective-permute-start.14 = (bf16[1024,512]{1,0:T(8,128)(2,1)}, bf16[1024,512]{1,0:T(8,128)(2,1)S(1)}, u32[]{:S(2)}, u32[]{:S(2)}) collective-permute-start(bf16[1024,512]{1,0:T(8,128)(2,1)} %refs_0_.2), channel_id=1, source_target_pairs={{0,96},{32,0},{64,32},{96,64},{1,97},{33,1},{65,33},{97,65},{2,98}... | collective-permute-start | bytes 3145736 | tf_op jit(solution)/shard_map/ppermute | solution.py:25
  23.6 3.4 %copy-start.5 = (s32[4096]{0:T(1024)S(1)}, s32[4096]{0:T(1024)}, u32[]{:S(2)}) copy-start(s32[4096]{0:T(1024)} %param.10) | copy-start | bytes 49156
  24.5 2.0 %copy-start.8 = (s32[2,4]{1,0:T(2,128)S(1)}, s32[2,4]{1,0:T(2,128)}, u32[]{:S(2)}) copy-start(s32[2,4]{1,0:T(2,128)} %param.12) | copy-start | bytes 100
  24.5 7.2 %collective-permute-start.7 = (bf16[1024,128]{1,0:T(8,128)(2,1)}, bf16[1024,128]{1,0:T(8,128)(2,1)}, u32[]{:S(2)}, u32[]{:S(2)}) collective-permute-start(bf16[1024,128]{1,0:T(8,128)(2,1)} %get-tuple-element.35), channel_id=1, source_target_pairs={{0,8},{8,16},{16,24},{24,0},{1,9},{9,17},{17,25},{25,1},{2,10},{10... | collective-permute-start | bytes 786440 | tf_op jit(solution)/shard_map/ppermute | solution.py:25
  24.8 7.9 %collective-permute-start.8 = (bf16[1024,128]{1,0:T(8,128)(2,1)}, bf16[1024,128]{1,0:T(8,128)(2,1)}, u32[]{:S(2)}, u32[]{:S(2)}) collective-permute-start(bf16[1024,128]{1,0:T(8,128)(2,1)} %get-tuple-element.36), channel_id=1, source_target_pairs={{0,24},{8,0},{16,8},{24,16},{1,25},{9,1},{17,9},{25,17},{2,26},{10... | collective-permute-start | bytes 786440 | tf_op jit(solution)/shard_map/ppermute | solution.py:25
  28.6 0.6 copy-start.6
  28.6 0.7 copy-start.7
  28.6 0.7 copy-start.9
  29.4 0.9 %copy-start.1 = (bf16[512,128]{1,0:T(8,128)(2,1)S(1)}, bf16[512,128]{1,0:T(8,128)(2,1)}, u32[]{:S(2)}) copy-start(bf16[512,128]{1,0:T(8,128)(2,1)} %copy-done) | copy-start | bytes 393220
  32.7 1.2 %copy-start.3 = (bf16[256,1024]{1,0:T(8,128)(2,1)S(1)}, bf16[256,1024]{1,0:T(8,128)(2,1)}, u32[]{:S(2)}) copy-start(bf16[256,1024]{1,0:T(8,128)(2,1)} %q.1) | copy-start | bytes 1572868
  38.0 12.1 %collective-permute-start.9 = (bf16[256,1024]{1,0:T(8,128)(2,1)S(1)}, bf16[256,1024]{1,0:T(8,128)(2,1)S(1)}, u32[]{:S(2)}, u32[]{:S(2)}) collective-permute-start(bf16[256,1024]{1,0:T(8,128)(2,1)S(1)} %attend.1.rows), channel_id=1, source_target_pairs={{0,8},{8,16},{16,24},{24,0},{1,9},{9,17},{17,25},{25,1},{2,10},{10... | collective-permute-start | bytes 1572872 | tf_op jit(solution)/shard_map/ppermute | solution.py:25
  38.1 12.1 %collective-permute-start.11 = (bf16[256,1024]{1,0:T(8,128)(2,1)S(1)}, bf16[256,1024]{1,0:T(8,128)(2,1)S(1)}, u32[]{:S(2)}, u32[]{:S(2)}) collective-permute-start(bf16[256,1024]{1,0:T(8,128)(2,1)S(1)} %attend.1.rows), channel_id=1, source_target_pairs={{0,24},{8,0},{16,8},{24,16},{1,25},{9,1},{17,9},{25,17},{2,26},{10... | collective-permute-start | bytes 1572872 | tf_op jit(solution)/shard_map/ppermute | solution.py:25
  40.2 12.4 %collective-permute-start.15 = (bf16[512,512]{1,0:T(8,128)(2,1)S(1)}, bf16[512,512]{1,0:T(8,128)(2,1)S(1)}, u32[]{:S(2)}, u32[]{:S(2)}) collective-permute-start(bf16[512,512]{1,0:T(8,128)(2,1)S(1)} %join.6), channel_id=1, source_target_pairs={{0,32},{32,64},{64,96},{96,0},{1,33},{33,65},{65,97},{97,1},{2,34}... | collective-permute-start | bytes 1572872 | tf_op jit(solution)/shard_map/ppermute | solution.py:25
  40.3 12.2 %copy-start.2 = (bf16[1024,512]{1,0:T(8,128)(2,1)S(1)}, bf16[1024,512]{1,0:T(8,128)(2,1)}, u32[]{:S(2)}) copy-start(bf16[1024,512]{1,0:T(8,128)(2,1)} %refs_0_.2) | copy-start | bytes 3145732
  40.3 12.2 %collective-permute-start.16 = (bf16[512,512]{1,0:T(8,128)(2,1)S(1)}, bf16[512,512]{1,0:T(8,128)(2,1)S(1)}, u32[]{:S(2)}, u32[]{:S(2)}) collective-permute-start(bf16[512,512]{1,0:T(8,128)(2,1)S(1)} %join.7), channel_id=1, source_target_pairs={{0,96},{32,0},{64,32},{96,64},{1,97},{33,1},{65,33},{97,65},{2,98}... | collective-permute-start | bytes 1572872 | tf_op jit(solution)/shard_map/ppermute | solution.py:25
  50.1 6.4 %collective-permute-start.10 = (bf16[128,1024]{1,0:T(8,128)(2,1)S(1)}, bf16[128,1024]{1,0:T(8,128)(2,1)S(1)}, u32[]{:S(2)}, u32[]{:S(2)}) collective-permute-start(bf16[128,1024]{1,0:T(8,128)(2,1)S(1)} %join.4), channel_id=1, source_target_pairs={{0,8},{8,16},{16,24},{24,0},{1,9},{9,17},{17,25},{25,1},{2,10},{10... | collective-permute-start | bytes 786440 | tf_op jit(solution)/shard_map/ppermute | solution.py:25
  50.2 7.9 %collective-permute-start.12 = (bf16[128,1024]{1,0:T(8,128)(2,1)S(1)}, bf16[128,1024]{1,0:T(8,128)(2,1)S(1)}, u32[]{:S(2)}, u32[]{:S(2)}) collective-permute-start(bf16[128,1024]{1,0:T(8,128)(2,1)S(1)} %join.5), channel_id=1, source_target_pairs={{0,24},{8,0},{16,8},{24,16},{1,25},{9,1},{17,9},{25,17},{2,26},{10... | collective-permute-start | bytes 786440 | tf_op jit(solution)/shard_map/ppermute | solution.py:25
  56.2 3.4 %collective-permute-start.22 = (bf16[4,256,512]{2,1,0:T(8,128)(2,1)S(1)}, bf16[4,256,512]{2,1,0:T(8,128)(2,1)S(1)}, u32[]{:S(2)}, u32[]{:S(2)}) collective-permute-start(bf16[4,256,512]{2,1,0:T(8,128)(2,1)S(1)} %get-tuple-element.54), channel_id=1, source_target_pairs={{0,1},{1,0},{2,3},{3,2},{4,5},{5,4},{6,7},{7,6},{8,9},{9,8},{10,11... | collective-permute-start | bytes 3145736 | tf_op jit(solution)/shard_map/ppermute | solution.py:29
  59.5 2.7 %collective-permute-start.17 = (bf16[4,256,512]{2,1,0:T(8,128)(2,1)S(1)}, bf16[4,256,512]{2,1,0:T(8,128)(2,1)S(1)}, u32[]{:S(2)}, u32[]{:S(2)}) collective-permute-start(bf16[4,256,512]{2,1,0:T(8,128)(2,1)S(1)} %get-tuple-element.47), channel_id=1, source_target_pairs={{0,1},{1,0},{2,3},{3,2},{4,5},{5,4},{6,7},{7,6},{8,9},{9,8},{10,11... | collective-permute-start | bytes 3145736 | tf_op jit(solution)/shard_map/ppermute | solution.py:29
  60.1 7.7 %collective-permute-start.24 = (bf16[256,512]{1,0:T(8,128)(2,1)S(1)}, bf16[256,512]{1,0:T(8,128)(2,1)S(1)}, u32[]{:S(2)}, u32[]{:S(2)}) collective-permute-start(bf16[256,512]{1,0:T(8,128)(2,1)S(1)} %get-tuple-element.58), channel_id=1, source_target_pairs={{0,2},{1,7},{2,4},{3,1},{4,6},{5,3},{6,0},{7,5},{8,10},{9,15},{10,... | collective-permute-start | bytes 786440 | tf_op jit(solution)/shard_map/ppermute | solution.py:319
  62.7 7.8 %collective-permute-start.19 = (bf16[256,512]{1,0:T(8,128)(2,1)S(1)}, bf16[256,512]{1,0:T(8,128)(2,1)S(1)}, u32[]{:S(2)}, u32[]{:S(2)}) collective-permute-start(bf16[256,512]{1,0:T(8,128)(2,1)S(1)} %get-tuple-element.51), channel_id=1, source_target_pairs={{0,2},{1,7},{2,4},{3,1},{4,6},{5,3},{6,0},{7,5},{8,10},{9,15},{10,... | collective-permute-start | bytes 786440 | tf_op jit(solution)/shard_map/ppermute | solution.py:319
  67.8 7.7 %collective-permute-start.25 = (bf16[256,512]{1,0:T(8,128)(2,1)S(1)}, bf16[256,512]{1,0:T(8,128)(2,1)S(1)}, u32[]{:S(2)}, u32[]{:S(2)}) collective-permute-start(bf16[256,512]{1,0:T(8,128)(2,1)S(1)} %add_convert_fusion.2), channel_id=1, source_target_pairs={{0,2},{1,7},{2,4},{3,1},{4,6},{5,3},{6,0},{7,5},{8,10},{9,15},{10,... | collective-permute-start | bytes 786440 | tf_op jit(solution)/shard_map/ppermute | solution.py:319
  70.6 7.7 %collective-permute-start.20 = (bf16[256,512]{1,0:T(8,128)(2,1)S(1)}, bf16[256,512]{1,0:T(8,128)(2,1)S(1)}, u32[]{:S(2)}, u32[]{:S(2)}) collective-permute-start(bf16[256,512]{1,0:T(8,128)(2,1)S(1)} %add_convert_fusion.5), channel_id=1, source_target_pairs={{0,2},{1,7},{2,4},{3,1},{4,6},{5,3},{6,0},{7,5},{8,10},{9,15},{10,... | collective-permute-start | bytes 786440 | tf_op jit(solution)/shard_map/ppermute | solution.py:319
  71.1 7.9 %collective-permute-start.23 = (bf16[256,512]{1,0:T(8,128)(2,1)S(1)}, bf16[256,512]{1,0:T(8,128)(2,1)S(1)}, u32[]{:S(2)}, u32[]{:S(2)}) collective-permute-start(bf16[256,512]{1,0:T(8,128)(2,1)S(1)} %get-tuple-element.55), channel_id=1, source_target_pairs={{0,24},{1,8},{2,26},{3,10},{4,28},{5,12},{6,30},{7,14},{8,0},{9,16... | collective-permute-start | bytes 786440 | tf_op jit(solution)/shard_map/ppermute | solution.py:329
  73.2 16.3 %collective-permute-start.18 = (bf16[256,512]{1,0:T(8,128)(2,1)S(1)}, bf16[256,512]{1,0:T(8,128)(2,1)S(1)}, u32[]{:S(2)}, u32[]{:S(2)}) collective-permute-start(bf16[256,512]{1,0:T(8,128)(2,1)S(1)} %get-tuple-element.48), channel_id=1, source_target_pairs={{0,0},{1,16},{2,2},{3,18},{4,4},{5,20},{6,6},{7,22},{8,8},{9,24},{... | collective-permute-start | bytes 786440 | tf_op jit(solution)/shard_map/ppermute | solution.py:329
  75.6 13.8 %collective-permute-start.26 = (bf16[256,512]{1,0:T(8,128)(2,1)S(1)}, bf16[256,512]{1,0:T(8,128)(2,1)S(1)}, u32[]{:S(2)}, u32[]{:S(2)}) collective-permute-start(bf16[256,512]{1,0:T(8,128)(2,1)S(1)} %add_convert_fusion.1), channel_id=1, source_target_pairs={{0,26},{1,14},{2,28},{3,8},{4,30},{5,10},{6,24},{7,12},{8,2},{9,22... | collective-permute-start | bytes 786440 | tf_op jit(solution)/shard_map/ppermute | solution.py:329
  78.4 11.1 %collective-permute-start.21 = (bf16[256,512]{1,0:T(8,128)(2,1)S(1)}, bf16[256,512]{1,0:T(8,128)(2,1)S(1)}, u32[]{:S(2)}, u32[]{:S(2)}) collective-permute-start(bf16[256,512]{1,0:T(8,128)(2,1)S(1)} %add_convert_fusion.4), channel_id=1, source_target_pairs={{0,2},{1,22},{2,4},{3,16},{4,6},{5,18},{6,0},{7,20},{8,10},{9,30},... | collective-permute-start | bytes 786440 | tf_op jit(solution)/shard_map/ppermute | solution.py:329

commit v7 on v6

--- a/solution.py
+++ b/solution.py
@@ -314,6 +314,28 @@
     )(keep, got)
 
 
+def finish_kernel(near_stay, near_passed, mixed_stay, mixed_passed, out):
+    width = near_stay.shape[1]
+    odd = lax.rem(lax.axis_index("x"), 2)
+    near_at = pl.multiple_of((1 - odd) * width, width)
+    mixed_at = pl.multiple_of(odd * width, width)
+    out[:, pl.ds(near_at, width)] = plus(near_stay[...], near_passed[...])
+    out[:, pl.ds(mixed_at, width)] = plus(mixed_stay[...], mixed_passed[...])
+
+
+def finish(*shares):
+    rows, width = shares[0].shape
+    return pl.pallas_call(
+        finish_kernel,
+        out_shape=jax.ShapeDtypeStruct((rows, 2 * width), jnp.bfloat16),
+        in_specs=[VMEM] * 4,
+        out_specs=VMEM,
+        compiler_params=pltpu.CompilerParams(vmem_limit_bytes=6 * 2**20),
+        cost_estimate=pl.CostEstimate(flops=0, bytes_accessed=2 * 2**20, transcendentals=0),
+        name="finish",
+    )(*shares)
+
+
 def relay(value, axis):
     pairs = [(2 * i + c, 2 * ((i + 1 - 2 * c) % 4) + c) for i in range(4) for c in range(2)]
     return lax.ppermute(value, (axis, "c"), pairs)
@@ -349,7 +371,6 @@
 
 
 def shards(queries, keys, values, positions, lengths, spans, weight):
-    x = lax.axis_index("x")
     count, slots = keys.shape[0], positions.shape[0]
     kv = jnp.concatenate([keys, values], axis=0)
     line = [shift(kv, Z, 1), shift(kv, Z, -1), shift(kv, Z, 2)]
@@ -392,13 +413,7 @@
     keep, send = project(far_kernel, (*rows_far, own), weights)
     mixed = combine(keep, swap_cores(send))
 
-    near = plus(*sum_shares(near, (-1, 1)))
-    mixed = plus(*sum_shares(mixed, (0, 2)))
-    return jnp.where(
-        lax.rem(x, 2) == 0,
-        jnp.concatenate([mixed, near], axis=1),
-        jnp.concatenate([near, mixed], axis=1),
-    )
+    return finish(*sum_shares(near, (-1, 1)), *sum_shares(mixed, (0, 2)))
 
 
 def solution(mesh):

time: 91.3 us -> 91.1 us (level)
  starting transfers between devices: 32.6 us -> 35.6 us
  waiting for transfers between devices: 37.9 us -> 35.3 us
  other arithmetic: 1.44 us -> 0.37 us
    ppermute x4, starting transfers between devices: 5 us -> 7.56 us  [home(): return lax.ppermute(value, ('x', 'y', 'c'), pairs)]
    ppermute x4, waiting for transfers between devices: 8.43 us -> 7.04 us  [relay(): return lax.ppermute(value, (axis, 'c'), pairs)]
    ppermute x4, waiting for transfers between devices: 10.4 us -> 9.24 us  [home(): return lax.ppermute(value, ('x', 'y', 'c'), pairs)]
    select_n x1 -> x0, other arithmetic: 0.94 us -> none  [shards(): jnp.where(lax.rem(x, 2) == 0, jnp.concatenate([mixed, near], axis=1), jnp...]
    pallas_call x0 -> x1, Pallas kernels: none -> 0.91 us  [finish(): pl.pallas_call(finish_kernel, out_shape=jax.ShapeDtypeStruct((rows, 2 * w...]
  transfers between devices with their start and end apart: 27 -> 27, of which waited for: 14 -> 16; matrix products, arithmetic and copies ran while one was open for 3% -> 3% of each run, Pallas kernels for 15% -> 14%
where the time goes in v7:
time: 91.1 us; the launch traced here: 90 us
  starting transfers between devices  35.6 us (39%)
  waiting for transfers between devices  35.3 us (39%)
  Pallas kernels  13.9 us (15%)
  local copies, waits for them, and re-layouts  4.59 us (5%)
    ppermute x17, starting transfers between devices, shift(): return lax.ppermute(value, axis, [(i, (i + step) % 4) for i in range(4)])  23.7 us
    ppermute x17, waiting for transfers between devices, shift(): return lax.ppermute(value, axis, [(i, (i + step) % 4) for i in range(4)])  18.5 us
    ppermute x4, waiting for transfers between devices, home(): return lax.ppermute(value, ('x', 'y', 'c'), pairs)  9.24 us
    ppermute x4, starting transfers between devices, home(): return lax.ppermute(value, ('x', 'y', 'c'), pairs)  7.56 us
    ppermute x4, waiting for transfers between devices, relay(): return lax.ppermute(value, (axis, 'c'), pairs)  7.04 us
    pallas_call x3, Pallas kernels, project(): pl.pallas_call(kernel, out_shape=[result] * results, in_specs=[VMEM] * (l...  4.96 us
    ppermute x4, starting transfers between devices, relay(): return lax.ppermute(value, (axis, 'c'), pairs)  4.17 us
    pallas_call x1, Pallas kernels, attend(): pl.pallas_call(attend_kernel, out_shape=jax.ShapeDtypeStruct((rows, width...  3.51 us
  transfers between devices with their start and end apart: 27, of which 16 were waited for; matrix products, arithmetic and copies ran while one was open for 3% of the time, Pallas kernels for 14%

profile of v7, /device:TPU:6, one launch (start us, length us, event | category | flops | bytes accessed | tf_op | source)
XLA Modules:
  0.0 90.0 jit_solution(7666456201250593037)
XLA Ops:
  0.0 0.9 constant_dynamic-update-slice_fusion.1
  0.9 4.0 %collective-permute-start.2 = (bf16[512,128]{1,0:T(8,128)(2,1)S(1)}, bf16[512,128]{1,0:T(8,128)(2,1)S(1)}, u32[]{:S(2)}, u32[]{:S(2)}) collective-permute-start(bf16[512,128]{1,0:T(8,128)(2,1)S(1)} %constant_dynamic-update-slice_fusion.refs_0_), channel_id=1, source_target_pairs={{0,64},{32,96},{64,0},{96,32},{1,65},{33,97},{65,1},{97,33},{2,66}... | collective-permute-start | bytes 393224 | tf_op jit(solution)/shard_map/ppermute | solution.py:25
  4.9 0.7 collective-permute-start.1
  5.6 1.3 %collective-permute-start = (bf16[512,128]{1,0:T(8,128)(2,1)S(1)}, bf16[512,128]{1,0:T(8,128)(2,1)S(1)}, u32[]{:S(2)}, u32[]{:S(2)}) collective-permute-start(bf16[512,128]{1,0:T(8,128)(2,1)S(1)} %constant_dynamic-update-slice_fusion.refs_0_), channel_id=1, source_target_pairs={{0,32},{32,64},{64,96},{96,0},{1,33},{33,65},{65,97},{97,1},{2,34}... | collective-permute-start | bytes 393224 | tf_op jit(solution)/shard_map/ppermute | solution.py:25
  6.9 0.5 collective-permute-start.3
  7.4 1.5 %collective-permute-start.4 = (bf16[512,128]{1,0:T(8,128)(2,1)S(1)}, bf16[512,128]{1,0:T(8,128)(2,1)S(1)}, u32[]{:S(2)}, u32[]{:S(2)}) collective-permute-start(bf16[512,128]{1,0:T(8,128)(2,1)S(1)} %constant_dynamic-update-slice_fusion.refs_0_), channel_id=1, source_target_pairs={{0,24},{8,0},{16,8},{24,16},{1,25},{9,1},{17,9},{25,17},{2,26},{10... | collective-permute-start | bytes 393224 | tf_op jit(solution)/shard_map/ppermute | solution.py:25
  8.9 3.0 %collective-permute-done.1 = bf16[512,128]{1,0:T(8,128)(2,1)S(1)} collective-permute-done((bf16[512,128]{1,0:T(8,128)(2,1)S(1)}, bf16[512,128]{1,0:T(8,128)(2,1)S(1)}, u32[]{:S(2)}, u32[]{:S(2)}) %collective-permute-start.1) | collective-permute-done | bytes 131104 | tf_op jit(solution)/shard_map/ppermute | solution.py:25
  12.0 1.5 %collective-permute-done.4.right.refs_3_ = bf16[512,128]{1,0:T(8,128)(2,1)S(1)} collective-permute-done((bf16[512,128]{1,0:T(8,128)(2,1)S(1)}, bf16[512,128]{1,0:T(8,128)(2,1)S(1)}, u32[]{:S(2)}, u32[]{:S(2)}) %collective-permute-start.4) | collective-permute-done | bytes 131104 | tf_op jit(solution)/shard_map/ppermute | solution.py:25
  13.8 1.7 %collective-permute-start.6 = (bf16[1536,128]{1,0:T(8,128)(2,1)S(1)}, bf16[1536,128]{1,0:T(8,128)(2,1)S(1)}, u32[]{:S(2)}, u32[]{:S(2)}) collective-permute-start(bf16[1536,128]{1,0:T(8,128)(2,1)S(1)} %pad_maximum_fusion.refs_1_), channel_id=1, source_target_pairs={{0,24},{8,0},{16,8},{24,16},{1,25},{9,1},{17,9},{25,17},{2,26},{10... | collective-permute-start | bytes 1179656 | tf_op jit(solution)/shard_map/ppermute | solution.py:25
  15.6 1.0 %collective-permute-start.10 = (bf16[1024,512]{1,0:T(8,128)(2,1)}, bf16[1024,512]{1,0:T(8,128)(2,1)S(1)}, u32[]{:S(2)}, u32[]{:S(2)}) collective-permute-start(bf16[1024,512]{1,0:T(8,128)(2,1)} %refs_0_.2), channel_id=1, source_target_pairs={{0,32},{32,64},{64,96},{96,0},{1,33},{33,65},{65,97},{97,1},{2,34}... | collective-permute-start | bytes 3145736 | tf_op jit(solution)/shard_map/ppermute | solution.py:25
  16.6 2.2 %collective-permute-start.11 = (bf16[1024,512]{1,0:T(8,128)(2,1)}, bf16[1024,512]{1,0:T(8,128)(2,1)S(1)}, u32[]{:S(2)}, u32[]{:S(2)}) collective-permute-start(bf16[1024,512]{1,0:T(8,128)(2,1)} %refs_0_.2), channel_id=1, source_target_pairs={{0,96},{32,0},{64,32},{96,64},{1,97},{33,1},{65,33},{97,65},{2,98}... | collective-permute-start | bytes 3145736 | tf_op jit(solution)/shard_map/ppermute | solution.py:25
  18.8 3.6 %collective-permute-done.5.line_left.refs_0_ = bf16[1536,128]{1,0:T(8,128)(2,1)S(1)} collective-permute-done((bf16[1536,128]{1,0:T(8,128)(2,1)S(1)}, bf16[1536,128]{1,0:T(8,128)(2,1)S(1)}, u32[]{:S(2)}, u32[]{:S(2)}) %collective-permute-start.5) | collective-permute-done | bytes 393248 | tf_op jit(solution)/shard_map/ppermute | solution.py:25
  22.4 1.2 %collective-permute-done.6.line_right.refs_1_ = bf16[1536,128]{1,0:T(8,128)(2,1)S(1)} collective-permute-done((bf16[1536,128]{1,0:T(8,128)(2,1)S(1)}, bf16[1536,128]{1,0:T(8,128)(2,1)S(1)}, u32[]{:S(2)}, u32[]{:S(2)}) %collective-permute-start.6) | collective-permute-done | bytes 393248 | tf_op jit(solution)/shard_map/ppermute | solution.py:25
  23.6 0.8 far_parts.1
  24.8 1.7 %collective-permute-start.8 = (bf16[1024,128]{1,0:T(8,128)(2,1)}, bf16[1024,128]{1,0:T(8,128)(2,1)}, u32[]{:S(2)}, u32[]{:S(2)}) collective-permute-start(bf16[1024,128]{1,0:T(8,128)(2,1)} %get-tuple-element.36), channel_id=1, source_target_pairs={{0,24},{8,0},{16,8},{24,16},{1,25},{9,1},{17,9},{25,17},{2,26},{10... | collective-permute-start | bytes 786440 | tf_op jit(solution)/shard_map/ppermute | solution.py:25
  26.5 0.6 slice_bitcast_fusion.1
  27.1 0.7 reshape.3
  27.8 0.9 slice_reduce_fusion
  28.6 0.6 copy-done.6
  29.4 0.9 %copy-done.1 = bf16[512,128]{1,0:T(8,128)(2,1)S(1)} copy-done((bf16[512,128]{1,0:T(8,128)(2,1)S(1)}, bf16[512,128]{1,0:T(8,128)(2,1)}, u32[]{:S(2)}) %copy-start.1) | copy-done | bytes 131096
  30.3 0.7 place.3
  31.0 0.7 place.4
  31.7 1.0 %collective-permute-done.8.refs_1_ = bf16[1024,128]{1,0:T(8,128)(2,1)} collective-permute-done((bf16[1024,128]{1,0:T(8,128)(2,1)}, bf16[1024,128]{1,0:T(8,128)(2,1)}, u32[]{:S(2)}, u32[]{:S(2)}) %collective-permute-start.8) | collective-permute-done | bytes 262176 | tf_op jit(solution)/shard_map/ppermute | solution.py:25
  32.7 1.2 %place.5 = (bf16[4096,128]{1,0:T(8,128)(2,1)S(1)}, bf16[4096,128]{1,0:T(8,128)(2,1)S(1)}) custom-call(s32[80]{0:T(128)S(1)} %pad_add_fusion.pos, bf16[1024,128]{1,0:T(8,128)(2,1)} %collective-permute-done.7.refs_0_, bf16[1024,128]{1,0:T(8,128)(2,1)} %collective-permute-done.8.refs_1_, ...), custom_call_target="tpu_custom_call", output_to_operand_aliasing={{0}: (3, {}), {1}: (4, {})} | custom-call | bytes 2097152 | tf_op jit(solution)/shard_map/place/pallas_call | solution.py:58
  33.9 3.5 %attend.1.rows = bf16[256,1024]{1,0:T(8,128)(2,1)S(1)} custom-call(s32[80]{0:T(128)S(1)} %pad_add_fusion.pos, bf16[256,1024]{1,0:T(8,128)(2,1)S(1)} %copy-done.3, bf16[4096,128]{1,0:T(8,128)(2,1)S(1)} %get-tuple-element.41.ks, bf16[4096,128]{1,0:T(8,128)(2,1)S(1)} %get-tuple-element.42.vs), custom_call_target="tpu_custom_call" | custom-call | flops 6442450944 | bytes 4194304 | tf_op jit(solution)/shard_map/attend/pallas_call | solution.py:161
  37.8 1.7 %collective-permute-start.14 = (bf16[256,1024]{1,0:T(8,128)(2,1)S(1)}, bf16[256,1024]{1,0:T(8,128)(2,1)S(1)}, u32[]{:S(2)}, u32[]{:S(2)}) collective-permute-start(bf16[256,1024]{1,0:T(8,128)(2,1)S(1)} %attend.1.rows), channel_id=1, source_target_pairs={{0,24},{8,0},{16,8},{24,16},{1,25},{9,1},{17,9},{25,17},{2,26},{10... | collective-permute-start | bytes 1572872 | tf_op jit(solution)/shard_map/ppermute | solution.py:25
  39.7 1.3 %collective-permute-start.12 = (bf16[512,512]{1,0:T(8,128)(2,1)S(1)}, bf16[512,512]{1,0:T(8,128)(2,1)S(1)}, u32[]{:S(2)}, u32[]{:S(2)}) collective-permute-start(bf16[512,512]{1,0:T(8,128)(2,1)S(1)} %join.4), channel_id=1, source_target_pairs={{0,32},{32,64},{64,96},{96,0},{1,33},{33,65},{65,97},{97,1},{2,34}... | collective-permute-start | bytes 1572872 | tf_op jit(solution)/shard_map/ppermute | solution.py:25
  41.0 2.6 %collective-permute-start.13 = (bf16[512,512]{1,0:T(8,128)(2,1)S(1)}, bf16[512,512]{1,0:T(8,128)(2,1)S(1)}, u32[]{:S(2)}, u32[]{:S(2)}) collective-permute-start(bf16[512,512]{1,0:T(8,128)(2,1)S(1)} %join.5), channel_id=1, source_target_pairs={{0,96},{32,0},{64,32},{96,64},{1,97},{33,1},{65,33},{97,65},{2,98}... | collective-permute-start | bytes 1572872 | tf_op jit(solution)/shard_map/ppermute | solution.py:25
  43.7 5.8 %collective-permute-done.9.left.refs_0_ = bf16[256,1024]{1,0:T(8,128)(2,1)S(1)} collective-permute-done((bf16[256,1024]{1,0:T(8,128)(2,1)S(1)}, bf16[256,1024]{1,0:T(8,128)(2,1)S(1)}, u32[]{:S(2)}, u32[]{:S(2)}) %collective-permute-start.9) | collective-permute-done | bytes 524320 | tf_op jit(solution)/shard_map/ppermute | solution.py:25
  49.9 2.0 %collective-permute-start.21 = (bf16[128,1024]{1,0:T(8,128)(2,1)S(1)}, bf16[128,1024]{1,0:T(8,128)(2,1)S(1)}, u32[]{:S(2)}, u32[]{:S(2)}) collective-permute-start(bf16[128,1024]{1,0:T(8,128)(2,1)S(1)} %join.7), channel_id=1, source_target_pairs={{0,24},{8,0},{16,8},{24,16},{1,25},{9,1},{17,9},{25,17},{2,26},{10... | collective-permute-start | bytes 786440 | tf_op jit(solution)/shard_map/ppermute | solution.py:25
  52.3 1.2 %project.3.own = bf16[4,256,512]{2,1,0:T(8,128)(2,1)S(1)} custom-call(bf16[256,1024]{1,0:T(8,128)(2,1)S(1)} %attend.1.rows, bf16[1024,512]{1,0:T(8,128)(2,1)S(1)} %copy-done.2, bf16[1024,512]{1,0:T(8,128)(2,1)S(1)} %collective-permute-done.10.refs_0_.refs_1_, bf16[1024,512]{1,0:T(8,128)(2,1)S(1)} %collective-permute-done.11.refs_0_.refs_2_, ...), custom_call_target="tpu_custom_call" | custom-call | flops 2147483648 | bytes 4194304 | tf_op jit(solution)/shard_map/project/pallas_call | solution.py:277
  53.5 2.4 %project.4 = (bf16[4,256,512]{2,1,0:T(8,128)(2,1)S(1)}, bf16[4,256,512]{2,1,0:T(8,128)(2,1)S(1)}) custom-call(bf16[256,1024]{1,0:T(8,128)(2,1)S(1)} %collective-permute-done.9.left.refs_0_, bf16[256,1024]{1,0:T(8,128)(2,1)S(1)} %collective-permute-done.14.right.refs_0_, bf16[1024,512]{1,0:T(8,128)(2,1)S(1)} %copy-done.2, ...), custom_call_target="tpu_custom_call" | custom-call | flops 2147483648 | bytes 4194304 | tf_op jit(solution)/shard_map/project/pallas_call | solution.py:277
  56.0 1.8 %collective-permute-done.21.lower = bf16[128,1024]{1,0:T(8,128)(2,1)S(1)} collective-permute-done((bf16[128,1024]{1,0:T(8,128)(2,1)S(1)}, bf16[128,1024]{1,0:T(8,128)(2,1)S(1)}, u32[]{:S(2)}, u32[]{:S(2)}) %collective-permute-start.21) | collective-permute-done | bytes 262176 | tf_op jit(solution)/shard_map/ppermute | solution.py:25
  57.8 1.3 %project.5 = (bf16[4,256,512]{2,1,0:T(8,128)(2,1)S(1)}, bf16[4,256,512]{2,1,0:T(8,128)(2,1)S(1)}) custom-call(bf16[128,1024]{1,0:T(8,128)(2,1)S(1)} %collective-permute-done.20.upper, bf16[128,1024]{1,0:T(8,128)(2,1)S(1)} %collective-permute-done.21.lower, bf16[4,256,512]{2,1,0:T(8,128)(2,1)S(1)} %project.3.own, bf16[1024,512]{1,0:T(8,128)(2,1)S(1)} %copy-done.2, ...), custom_call_target="tpu_custom_call" | custom-call | flops 2147483648 | bytes 4194304 | tf_op jit(solution)/shard_map/project/pallas_call | solution.py:277
  59.2 0.5 combine.2
  59.8 1.6 %collective-permute-start.17 = (bf16[256,512]{1,0:T(8,128)(2,1)S(1)}, bf16[256,512]{1,0:T(8,128)(2,1)S(1)}, u32[]{:S(2)}, u32[]{:S(2)}) collective-permute-start(bf16[256,512]{1,0:T(8,128)(2,1)S(1)} %get-tuple-element.52), channel_id=1, source_target_pairs={{0,2},{1,7},{2,4},{3,1},{4,6},{5,3},{6,0},{7,5},{8,10},{9,15},{10,... | collective-permute-start | bytes 786440 | tf_op jit(solution)/shard_map/ppermute | solution.py:341
  61.9 0.5 combine.3
  62.4 1.6 %collective-permute-start.24 = (bf16[256,512]{1,0:T(8,128)(2,1)S(1)}, bf16[256,512]{1,0:T(8,128)(2,1)S(1)}, u32[]{:S(2)}, u32[]{:S(2)}) collective-permute-start(bf16[256,512]{1,0:T(8,128)(2,1)S(1)} %get-tuple-element.58), channel_id=1, source_target_pairs={{0,2},{1,7},{2,4},{3,1},{4,6},{5,3},{6,0},{7,5},{8,10},{9,15},{10,... | collective-permute-start | bytes 786440 | tf_op jit(solution)/shard_map/ppermute | solution.py:341
  64.0 3.4 %collective-permute-done.17 = bf16[256,512]{1,0:T(8,128)(2,1)S(1)} collective-permute-done((bf16[256,512]{1,0:T(8,128)(2,1)S(1)}, bf16[256,512]{1,0:T(8,128)(2,1)S(1)}, u32[]{:S(2)}, u32[]{:S(2)}) %collective-permute-start.17) | collective-permute-done | bytes 262176 | tf_op jit(solution)/shard_map/ppermute | solution.py:341
  67.9 2.3 %collective-permute-done.24 = bf16[256,512]{1,0:T(8,128)(2,1)S(1)} collective-permute-done((bf16[256,512]{1,0:T(8,128)(2,1)S(1)}, bf16[256,512]{1,0:T(8,128)(2,1)S(1)}, u32[]{:S(2)}, u32[]{:S(2)}) %collective-permute-start.24) | collective-permute-done | bytes 262176 | tf_op jit(solution)/shard_map/ppermute | solution.py:341
  70.7 1.8 %collective-permute-start.16 = (bf16[256,512]{1,0:T(8,128)(2,1)S(1)}, bf16[256,512]{1,0:T(8,128)(2,1)S(1)}, u32[]{:S(2)}, u32[]{:S(2)}) collective-permute-start(bf16[256,512]{1,0:T(8,128)(2,1)S(1)} %get-tuple-element.49), channel_id=1, source_target_pairs={{0,24},{1,8},{2,26},{3,10},{4,28},{5,12},{6,30},{7,14},{8,0},{9,16... | collective-permute-start | bytes 786440 | tf_op jit(solution)/shard_map/ppermute | solution.py:351
  72.5 2.5 %collective-permute-start.23 = (bf16[256,512]{1,0:T(8,128)(2,1)S(1)}, bf16[256,512]{1,0:T(8,128)(2,1)S(1)}, u32[]{:S(2)}, u32[]{:S(2)}) collective-permute-start(bf16[256,512]{1,0:T(8,128)(2,1)S(1)} %get-tuple-element.55), channel_id=1, source_target_pairs={{0,0},{1,16},{2,2},{3,18},{4,4},{5,20},{6,6},{7,22},{8,8},{9,24},{... | collective-permute-start | bytes 786440 | tf_op jit(solution)/shard_map/ppermute | solution.py:351
  75.2 1.5 %collective-permute-start.19 = (bf16[256,512]{1,0:T(8,128)(2,1)S(1)}, bf16[256,512]{1,0:T(8,128)(2,1)S(1)}, u32[]{:S(2)}, u32[]{:S(2)}) collective-permute-start(bf16[256,512]{1,0:T(8,128)(2,1)S(1)} %add_convert_fusion.2), channel_id=1, source_target_pairs={{0,26},{1,14},{2,28},{3,8},{4,30},{5,10},{6,24},{7,12},{8,2},{9,22... | collective-permute-start | bytes 786440 | tf_op jit(solution)/shard_map/ppermute | solution.py:351
  76.7 1.3 %collective-permute-done.25 = bf16[256,512]{1,0:T(8,128)(2,1)S(1)} collective-permute-done((bf16[256,512]{1,0:T(8,128)(2,1)S(1)}, bf16[256,512]{1,0:T(8,128)(2,1)S(1)}, u32[]{:S(2)}, u32[]{:S(2)}) %collective-permute-start.25) | collective-permute-done | bytes 262176 | tf_op jit(solution)/shard_map/ppermute | solution.py:341
  78.0 1.8 %collective-permute-start.26 = (bf16[256,512]{1,0:T(8,128)(2,1)S(1)}, bf16[256,512]{1,0:T(8,128)(2,1)S(1)}, u32[]{:S(2)}, u32[]{:S(2)}) collective-permute-start(bf16[256,512]{1,0:T(8,128)(2,1)S(1)} %add_convert_fusion), channel_id=1, source_target_pairs={{0,2},{1,22},{2,4},{3,16},{4,6},{5,18},{6,0},{7,20},{8,10},{9,30},... | collective-permute-start | bytes 786440 | tf_op jit(solution)/shard_map/ppermute | solution.py:351
  79.8 4.7 %collective-permute-done.23.mixed_stay = bf16[256,512]{1,0:T(8,128)(2,1)S(1)} collective-permute-done((bf16[256,512]{1,0:T(8,128)(2,1)S(1)}, bf16[256,512]{1,0:T(8,128)(2,1)S(1)}, u32[]{:S(2)}, u32[]{:S(2)}) %collective-permute-start.23) | collective-permute-done | bytes 262176 | tf_op jit(solution)/shard_map/ppermute | solution.py:351
  84.5 4.6 %collective-permute-done.19.near_passed = bf16[256,512]{1,0:T(8,128)(2,1)S(1)} collective-permute-done((bf16[256,512]{1,0:T(8,128)(2,1)S(1)}, bf16[256,512]{1,0:T(8,128)(2,1)S(1)}, u32[]{:S(2)}, u32[]{:S(2)}) %collective-permute-start.19) | collective-permute-done | bytes 262176 | tf_op jit(solution)/shard_map/ppermute | solution.py:351
  89.0 0.9 %finish.1 = bf16[256,1024]{1,0:T(8,128)(2,1)} custom-call(bf16[256,512]{1,0:T(8,128)(2,1)S(1)} %collective-permute-done.16.near_stay, bf16[256,512]{1,0:T(8,128)(2,1)S(1)} %collective-permute-done.19.near_passed, bf16[256,512]{1,0:T(8,128)(2,1)S(1)} %collective-permute-done.23.mixed_stay, bf16[256,512]{1,0:T(8,128)(2,1)S(1)} %collective-permute-done.26.mixed_passed), custom_call_target="tpu_custom_call" | custom-call | bytes 2097152 | tf_op jit(solution)/shard_map/finish/pallas_call | solution.py:328
  (52 shorter events, 4.2 us)
Async XLA Ops:
  0.0 0.9 copy-start.4
  0.9 11.1 %copy-start = (bf16[512,128]{1,0:T(8,128)(2,1)}, bf16[512,128]{1,0:T(8,128)(2,1)S(1)}, u32[]{:S(2)}) copy-start(bf16[512,128]{1,0:T(8,128)(2,1)S(1)} %constant_dynamic-update-slice_fusion.refs_0_) | copy-start | bytes 393220
  0.9 8.0 %collective-permute-start.2 = (bf16[512,128]{1,0:T(8,128)(2,1)S(1)}, bf16[512,128]{1,0:T(8,128)(2,1)S(1)}, u32[]{:S(2)}, u32[]{:S(2)}) collective-permute-start(bf16[512,128]{1,0:T(8,128)(2,1)S(1)} %constant_dynamic-update-slice_fusion.refs_0_), channel_id=1, source_target_pairs={{0,64},{32,96},{64,0},{96,32},{1,65},{33,97},{65,1},{97,33},{2,66}... | collective-permute-start | bytes 393224 | tf_op jit(solution)/shard_map/ppermute | solution.py:25
  4.9 7.1 %collective-permute-start.1 = (bf16[512,128]{1,0:T(8,128)(2,1)S(1)}, bf16[512,128]{1,0:T(8,128)(2,1)S(1)}, u32[]{:S(2)}, u32[]{:S(2)}) collective-permute-start(bf16[512,128]{1,0:T(8,128)(2,1)S(1)} %constant_dynamic-update-slice_fusion.refs_0_), channel_id=1, source_target_pairs={{0,96},{32,0},{64,32},{96,64},{1,97},{33,1},{65,33},{97,65},{2,98}... | collective-permute-start | bytes 393224 | tf_op jit(solution)/shard_map/ppermute | solution.py:25
  5.6 6.4 %collective-permute-start = (bf16[512,128]{1,0:T(8,128)(2,1)S(1)}, bf16[512,128]{1,0:T(8,128)(2,1)S(1)}, u32[]{:S(2)}, u32[]{:S(2)}) collective-permute-start(bf16[512,128]{1,0:T(8,128)(2,1)S(1)} %constant_dynamic-update-slice_fusion.refs_0_), channel_id=1, source_target_pairs={{0,32},{32,64},{64,96},{96,0},{1,33},{33,65},{65,97},{97,1},{2,34}... | collective-permute-start | bytes 393224 | tf_op jit(solution)/shard_map/ppermute | solution.py:25
  6.9 5.1 %collective-permute-start.3 = (bf16[512,128]{1,0:T(8,128)(2,1)S(1)}, bf16[512,128]{1,0:T(8,128)(2,1)S(1)}, u32[]{:S(2)}, u32[]{:S(2)}) collective-permute-start(bf16[512,128]{1,0:T(8,128)(2,1)S(1)} %constant_dynamic-update-slice_fusion.refs_0_), channel_id=1, source_target_pairs={{0,8},{8,16},{16,24},{24,0},{1,9},{9,17},{17,25},{25,1},{2,10},{10... | collective-permute-start | bytes 393224 | tf_op jit(solution)/shard_map/ppermute | solution.py:25
  7.4 6.2 %collective-permute-start.4 = (bf16[512,128]{1,0:T(8,128)(2,1)S(1)}, bf16[512,128]{1,0:T(8,128)(2,1)S(1)}, u32[]{:S(2)}, u32[]{:S(2)}) collective-permute-start(bf16[512,128]{1,0:T(8,128)(2,1)S(1)} %constant_dynamic-update-slice_fusion.refs_0_), channel_id=1, source_target_pairs={{0,24},{8,0},{16,8},{24,16},{1,25},{9,1},{17,9},{25,17},{2,26},{10... | collective-permute-start | bytes 393224 | tf_op jit(solution)/shard_map/ppermute | solution.py:25
  13.5 8.9 %collective-permute-start.5 = (bf16[1536,128]{1,0:T(8,128)(2,1)S(1)}, bf16[1536,128]{1,0:T(8,128)(2,1)S(1)}, u32[]{:S(2)}, u32[]{:S(2)}) collective-permute-start(bf16[1536,128]{1,0:T(8,128)(2,1)S(1)} %pad_maximum_fusion.refs_1_), channel_id=1, source_target_pairs={{0,8},{8,16},{16,24},{24,0},{1,9},{9,17},{17,25},{25,1},{2,10},{10... | collective-permute-start | bytes 1179656 | tf_op jit(solution)/shard_map/ppermute | solution.py:25
  13.8 9.8 %collective-permute-start.6 = (bf16[1536,128]{1,0:T(8,128)(2,1)S(1)}, bf16[1536,128]{1,0:T(8,128)(2,1)S(1)}, u32[]{:S(2)}, u32[]{:S(2)}) collective-permute-start(bf16[1536,128]{1,0:T(8,128)(2,1)S(1)} %pad_maximum_fusion.refs_1_), channel_id=1, source_target_pairs={{0,24},{8,0},{16,8},{24,16},{1,25},{9,1},{17,9},{25,17},{2,26},{10... | collective-permute-start | bytes 1179656 | tf_op jit(solution)/shard_map/ppermute | solution.py:25
  15.6 24.1 %collective-permute-start.10 = (bf16[1024,512]{1,0:T(8,128)(2,1)}, bf16[1024,512]{1,0:T(8,128)(2,1)S(1)}, u32[]{:S(2)}, u32[]{:S(2)}) collective-permute-start(bf16[1024,512]{1,0:T(8,128)(2,1)} %refs_0_.2), channel_id=1, source_target_pairs={{0,32},{32,64},{64,96},{96,0},{1,33},{33,65},{65,97},{97,1},{2,34}... | collective-permute-start | bytes 3145736 | tf_op jit(solution)/shard_map/ppermute | solution.py:25
  16.6 24.4 %collective-permute-start.11 = (bf16[1024,512]{1,0:T(8,128)(2,1)}, bf16[1024,512]{1,0:T(8,128)(2,1)S(1)}, u32[]{:S(2)}, u32[]{:S(2)}) collective-permute-start(bf16[1024,512]{1,0:T(8,128)(2,1)} %refs_0_.2), channel_id=1, source_target_pairs={{0,96},{32,0},{64,32},{96,64},{1,97},{33,1},{65,33},{97,65},{2,98}... | collective-permute-start | bytes 3145736 | tf_op jit(solution)/shard_map/ppermute | solution.py:25
  23.6 3.4 %copy-start.5 = (s32[4096]{0:T(1024)S(1)}, s32[4096]{0:T(1024)}, u32[]{:S(2)}) copy-start(s32[4096]{0:T(1024)} %param.10) | copy-start | bytes 49156
  24.5 2.0 %copy-start.8 = (s32[2,4]{1,0:T(2,128)S(1)}, s32[2,4]{1,0:T(2,128)}, u32[]{:S(2)}) copy-start(s32[2,4]{1,0:T(2,128)} %param.12) | copy-start | bytes 100
  24.5 7.2 %collective-permute-start.7 = (bf16[1024,128]{1,0:T(8,128)(2,1)}, bf16[1024,128]{1,0:T(8,128)(2,1)}, u32[]{:S(2)}, u32[]{:S(2)}) collective-permute-start(bf16[1024,128]{1,0:T(8,128)(2,1)} %get-tuple-element.35), channel_id=1, source_target_pairs={{0,8},{8,16},{16,24},{24,0},{1,9},{9,17},{17,25},{25,1},{2,10},{10... | collective-permute-start | bytes 786440 | tf_op jit(solution)/shard_map/ppermute | solution.py:25
  24.8 7.9 %collective-permute-start.8 = (bf16[1024,128]{1,0:T(8,128)(2,1)}, bf16[1024,128]{1,0:T(8,128)(2,1)}, u32[]{:S(2)}, u32[]{:S(2)}) collective-permute-start(bf16[1024,128]{1,0:T(8,128)(2,1)} %get-tuple-element.36), channel_id=1, source_target_pairs={{0,24},{8,0},{16,8},{24,16},{1,25},{9,1},{17,9},{25,17},{2,26},{10... | collective-permute-start | bytes 786440 | tf_op jit(solution)/shard_map/ppermute | solution.py:25
  28.6 0.6 copy-start.6
  28.6 0.7 copy-start.7
  28.6 0.7 copy-start.9
  29.4 0.9 %copy-start.1 = (bf16[512,128]{1,0:T(8,128)(2,1)S(1)}, bf16[512,128]{1,0:T(8,128)(2,1)}, u32[]{:S(2)}) copy-start(bf16[512,128]{1,0:T(8,128)(2,1)} %copy-done) | copy-start | bytes 393220
  32.7 1.2 %copy-start.3 = (bf16[256,1024]{1,0:T(8,128)(2,1)S(1)}, bf16[256,1024]{1,0:T(8,128)(2,1)}, u32[]{:S(2)}) copy-start(bf16[256,1024]{1,0:T(8,128)(2,1)} %q.1) | copy-start | bytes 1572868
  37.4 12.1 %collective-permute-start.9 = (bf16[256,1024]{1,0:T(8,128)(2,1)S(1)}, bf16[256,1024]{1,0:T(8,128)(2,1)S(1)}, u32[]{:S(2)}, u32[]{:S(2)}) collective-permute-start(bf16[256,1024]{1,0:T(8,128)(2,1)S(1)} %attend.1.rows), channel_id=1, source_target_pairs={{0,8},{8,16},{16,24},{24,0},{1,9},{9,17},{17,25},{25,1},{2,10},{10... | collective-permute-start | bytes 1572872 | tf_op jit(solution)/shard_map/ppermute | solution.py:25
  37.8 12.1 %collective-permute-start.14 = (bf16[256,1024]{1,0:T(8,128)(2,1)S(1)}, bf16[256,1024]{1,0:T(8,128)(2,1)S(1)}, u32[]{:S(2)}, u32[]{:S(2)}) collective-permute-start(bf16[256,1024]{1,0:T(8,128)(2,1)S(1)} %attend.1.rows), channel_id=1, source_target_pairs={{0,24},{8,0},{16,8},{24,16},{1,25},{9,1},{17,9},{25,17},{2,26},{10... | collective-permute-start | bytes 1572872 | tf_op jit(solution)/shard_map/ppermute | solution.py:25
  39.7 12.5 %collective-permute-start.12 = (bf16[512,512]{1,0:T(8,128)(2,1)S(1)}, bf16[512,512]{1,0:T(8,128)(2,1)S(1)}, u32[]{:S(2)}, u32[]{:S(2)}) collective-permute-start(bf16[512,512]{1,0:T(8,128)(2,1)S(1)} %join.4), channel_id=1, source_target_pairs={{0,32},{32,64},{64,96},{96,0},{1,33},{33,65},{65,97},{97,1},{2,34}... | collective-permute-start | bytes 1572872 | tf_op jit(solution)/shard_map/ppermute | solution.py:25
  41.0 11.2 %copy-start.2 = (bf16[1024,512]{1,0:T(8,128)(2,1)S(1)}, bf16[1024,512]{1,0:T(8,128)(2,1)}, u32[]{:S(2)}) copy-start(bf16[1024,512]{1,0:T(8,128)(2,1)} %refs_0_.2) | copy-start | bytes 3145732
  41.0 11.2 %collective-permute-start.13 = (bf16[512,512]{1,0:T(8,128)(2,1)S(1)}, bf16[512,512]{1,0:T(8,128)(2,1)S(1)}, u32[]{:S(2)}, u32[]{:S(2)}) collective-permute-start(bf16[512,512]{1,0:T(8,128)(2,1)S(1)} %join.5), channel_id=1, source_target_pairs={{0,96},{32,0},{64,32},{96,64},{1,97},{33,1},{65,33},{97,65},{2,98}... | collective-permute-start | bytes 1572872 | tf_op jit(solution)/shard_map/ppermute | solution.py:25
  49.5 6.5 %collective-permute-start.20 = (bf16[128,1024]{1,0:T(8,128)(2,1)S(1)}, bf16[128,1024]{1,0:T(8,128)(2,1)S(1)}, u32[]{:S(2)}, u32[]{:S(2)}) collective-permute-start(bf16[128,1024]{1,0:T(8,128)(2,1)S(1)} %join.6), channel_id=1, source_target_pairs={{0,8},{8,16},{16,24},{24,0},{1,9},{9,17},{17,25},{25,1},{2,10},{10... | collective-permute-start | bytes 786440 | tf_op jit(solution)/shard_map/ppermute | solution.py:25
  49.9 7.9 %collective-permute-start.21 = (bf16[128,1024]{1,0:T(8,128)(2,1)S(1)}, bf16[128,1024]{1,0:T(8,128)(2,1)S(1)}, u32[]{:S(2)}, u32[]{:S(2)}) collective-permute-start(bf16[128,1024]{1,0:T(8,128)(2,1)S(1)} %join.7), channel_id=1, source_target_pairs={{0,24},{8,0},{16,8},{24,16},{1,25},{9,1},{17,9},{25,17},{2,26},{10... | collective-permute-start | bytes 786440 | tf_op jit(solution)/shard_map/ppermute | solution.py:25
  55.9 3.3 %collective-permute-start.15 = (bf16[4,256,512]{2,1,0:T(8,128)(2,1)S(1)}, bf16[4,256,512]{2,1,0:T(8,128)(2,1)S(1)}, u32[]{:S(2)}, u32[]{:S(2)}) collective-permute-start(bf16[4,256,512]{2,1,0:T(8,128)(2,1)S(1)} %get-tuple-element.48), channel_id=1, source_target_pairs={{0,1},{1,0},{2,3},{3,2},{4,5},{5,4},{6,7},{7,6},{8,9},{9,8},{10,11... | collective-permute-start | bytes 3145736 | tf_op jit(solution)/shard_map/ppermute | solution.py:29
  59.1 2.7 %collective-permute-start.22 = (bf16[4,256,512]{2,1,0:T(8,128)(2,1)S(1)}, bf16[4,256,512]{2,1,0:T(8,128)(2,1)S(1)}, u32[]{:S(2)}, u32[]{:S(2)}) collective-permute-start(bf16[4,256,512]{2,1,0:T(8,128)(2,1)S(1)} %get-tuple-element.54), channel_id=1, source_target_pairs={{0,1},{1,0},{2,3},{3,2},{4,5},{5,4},{6,7},{7,6},{8,9},{9,8},{10,11... | collective-permute-start | bytes 3145736 | tf_op jit(solution)/shard_map/ppermute | solution.py:29
  59.8 7.7 %collective-permute-start.17 = (bf16[256,512]{1,0:T(8,128)(2,1)S(1)}, bf16[256,512]{1,0:T(8,128)(2,1)S(1)}, u32[]{:S(2)}, u32[]{:S(2)}) collective-permute-start(bf16[256,512]{1,0:T(8,128)(2,1)S(1)} %get-tuple-element.52), channel_id=1, source_target_pairs={{0,2},{1,7},{2,4},{3,1},{4,6},{5,3},{6,0},{7,5},{8,10},{9,15},{10,... | collective-permute-start | bytes 786440 | tf_op jit(solution)/shard_map/ppermute | solution.py:341
  62.4 7.8 %collective-permute-start.24 = (bf16[256,512]{1,0:T(8,128)(2,1)S(1)}, bf16[256,512]{1,0:T(8,128)(2,1)S(1)}, u32[]{:S(2)}, u32[]{:S(2)}) collective-permute-start(bf16[256,512]{1,0:T(8,128)(2,1)S(1)} %get-tuple-element.58), channel_id=1, source_target_pairs={{0,2},{1,7},{2,4},{3,1},{4,6},{5,3},{6,0},{7,5},{8,10},{9,15},{10,... | collective-permute-start | bytes 786440 | tf_op jit(solution)/shard_map/ppermute | solution.py:341
  67.5 7.7 %collective-permute-start.18 = (bf16[256,512]{1,0:T(8,128)(2,1)S(1)}, bf16[256,512]{1,0:T(8,128)(2,1)S(1)}, u32[]{:S(2)}, u32[]{:S(2)}) collective-permute-start(bf16[256,512]{1,0:T(8,128)(2,1)S(1)} %add_convert_fusion.3), channel_id=1, source_target_pairs={{0,2},{1,7},{2,4},{3,1},{4,6},{5,3},{6,0},{7,5},{8,10},{9,15},{10,... | collective-permute-start | bytes 786440 | tf_op jit(solution)/shard_map/ppermute | solution.py:341
  70.3 7.7 %collective-permute-start.25 = (bf16[256,512]{1,0:T(8,128)(2,1)S(1)}, bf16[256,512]{1,0:T(8,128)(2,1)S(1)}, u32[]{:S(2)}, u32[]{:S(2)}) collective-permute-start(bf16[256,512]{1,0:T(8,128)(2,1)S(1)} %add_convert_fusion.1), channel_id=1, source_target_pairs={{0,2},{1,7},{2,4},{3,1},{4,6},{5,3},{6,0},{7,5},{8,10},{9,15},{10,... | collective-permute-start | bytes 786440 | tf_op jit(solution)/shard_map/ppermute | solution.py:341
  70.7 9.1 %collective-permute-start.16 = (bf16[256,512]{1,0:T(8,128)(2,1)S(1)}, bf16[256,512]{1,0:T(8,128)(2,1)S(1)}, u32[]{:S(2)}, u32[]{:S(2)}) collective-permute-start(bf16[256,512]{1,0:T(8,128)(2,1)S(1)} %get-tuple-element.49), channel_id=1, source_target_pairs={{0,24},{1,8},{2,26},{3,10},{4,28},{5,12},{6,30},{7,14},{8,0},{9,16... | collective-permute-start | bytes 786440 | tf_op jit(solution)/shard_map/ppermute | solution.py:351
  72.5 11.9 %collective-permute-start.23 = (bf16[256,512]{1,0:T(8,128)(2,1)S(1)}, bf16[256,512]{1,0:T(8,128)(2,1)S(1)}, u32[]{:S(2)}, u32[]{:S(2)}) collective-permute-start(bf16[256,512]{1,0:T(8,128)(2,1)S(1)} %get-tuple-element.55), channel_id=1, source_target_pairs={{0,0},{1,16},{2,2},{3,18},{4,4},{5,20},{6,6},{7,22},{8,8},{9,24},{... | collective-permute-start | bytes 786440 | tf_op jit(solution)/shard_map/ppermute | solution.py:351
  75.2 13.8 %collective-permute-start.19 = (bf16[256,512]{1,0:T(8,128)(2,1)S(1)}, bf16[256,512]{1,0:T(8,128)(2,1)S(1)}, u32[]{:S(2)}, u32[]{:S(2)}) collective-permute-start(bf16[256,512]{1,0:T(8,128)(2,1)S(1)} %add_convert_fusion.2), channel_id=1, source_target_pairs={{0,26},{1,14},{2,28},{3,8},{4,30},{5,10},{6,24},{7,12},{8,2},{9,22... | collective-permute-start | bytes 786440 | tf_op jit(solution)/shard_map/ppermute | solution.py:351
  78.0 11.0 %collective-permute-start.26 = (bf16[256,512]{1,0:T(8,128)(2,1)S(1)}, bf16[256,512]{1,0:T(8,128)(2,1)S(1)}, u32[]{:S(2)}, u32[]{:S(2)}) collective-permute-start(bf16[256,512]{1,0:T(8,128)(2,1)S(1)} %add_convert_fusion), channel_id=1, source_target_pairs={{0,2},{1,22},{2,4},{3,16},{4,6},{5,18},{6,0},{7,20},{8,10},{9,30},... | collective-permute-start | bytes 786440 | tf_op jit(solution)/shard_map/ppermute | solution.py:351
